TPU v7x, 128 devices: a whole 4x4x4 slice. The times are simulated.
128 devices in a mesh: off: 16 (over x, y), col: 8 (over z, core).
Axes of the slice: x: 4, y: 4, z: 4, core: 2. Of those that a mesh axis runs over, the one named last changes fastest.
Arguments:
- noise_cov: float32 [512, 256, 256], P('off', 'col'), as said below
- couplings: float32 [3, 256, 256], replicated, may hold values from -0.3125 to 0.3125
- shifts: int32 [3], replicated, may hold values from -1 to 1
Outputs:
- covariance: float32 [512, 256, 256], P('off', 'col')
Inputs may be any that keep to these rules, and one draw needn't show every extreme that they name: noise_cov[d] is the transpose of noise_cov[(512 - d) mod 512].
All inputs are finite; a program needn't handle non-finite values.
Results may differ from a plain program's by a relative error of at most 0.0003.
Values sent between devices are 32-bit elements; how exact they have to be, the bound alone decides.
No kernel may reach another device: no remote copies, remote signals or barrier semaphores. Data moves between devices by JAX's collectives and lax.ppermute only.
A program may use at most 64 MiB of HBM per device.

v0:
```python
import jax
import jax.numpy as jnp
from jax import lax
from jax.experimental import pallas as pl
from jax.experimental.pallas import tpu as pltpu
from jax.sharding import PartitionSpec as P

f32 = jnp.float32
bf16 = jnp.bfloat16

N = 256
R = 32
HALO = 6
GRID = 6
BASE = 3

def place(d):
    slot = d + BASE
    return slot % GRID, slot // GRID


def grid_tile(j, g, offsets):
    return [(j, GRID * q + g - BASE) if GRID * q + g - BASE in offsets else None for q in range(4)]


def local_tiles():
    tiles = [grid_tile(3, g, range(3, 20)) for g in range(GRID)]
    tiles += [grid_tile(2, g, range(2, 19)) for g in range(GRID)]
    tiles += [grid_tile(1, 5, range(1, 18))]
    free = [(tile, q) for tile in tiles[:-1] for q in range(4) if tile[q] is None]
    left = [d for d in range(1, 18) if place(d)[0] != 5]
    for tile, q in [f for f in free if f[1] == 3]:
        d = next(d for d in left if place(d)[1] == 3)
        left.remove(d)
        tile[q] = (1, d)
        free.remove((tile, q))
    for (tile, q), d in zip(free, left):
        tile[q] = (1, d)
    return tiles


LOCAL = local_tiles()
HALOS = [
    [(3, -3), (3, -2), (3, -1), (3, 0)],
    [(3, 1), (3, 2), (2, -2), (2, -1)],
    [(2, 0), (2, 1), (1, -1), (1, 0)],
]
WHERE = {entry: (m, p) for m, tile in enumerate(LOCAL + HALOS) for p, entry in enumerate(tile) if entry}
RESULT = [[5, 3, 9, 15], [11, 4, 10, 16], [0, 6, 12, None], [1, 7, 13, None], [2, 8, 14, None]]
LOCAL_LANES = 128 * len(LOCAL)
HALO_LANES = 128 * len(HALOS)
OUT_LANES = 128 * len(RESULT)
SLOTS = [(1, 0), (3, 0), (2, 0), (1, 1), (3, 1), (2, 1), (0, 1), (0, 0)]


def coordinates():
    col = lax.axis_index("col")
    return col // 2, col % 2


def target(k, e):
    z, core = coordinates()
    return 2 * ((z + k) % 4) + (core + e) % 2


def source(k, e):
    z, core = coordinates()
    return 2 * ((z + 4 - k) % 4) + (core + e) % 2


def split(x):
    high = x.astype(bf16)
    return high, (x - high.astype(f32)).astype(bf16)


def split_taps(c_ref, shift_ref, b_ref):
    for s in (-1, 0, 1):
        block = None
        for t in range(3):
            chosen = jnp.where(shift_ref[t] == s, f32(1), f32(0)) * c_ref[t]
            block = chosen if block is None else block + chosen
        high, low = split(block)
        b_ref[s + 1, :, :N] = high
        b_ref[s + 1, :, N : 2 * N] = high
        b_ref[s + 1, :, 2 * N :] = low


def block_of_lane(rows):
    return lax.broadcasted_iota(jnp.int32, (rows, 128), 1) // 32


def exchange_blocks(tiles):
    block = block_of_lane(tiles[0].shape[0])
    low = block < 2
    even = block % 2 == 0
    a = list(tiles)
    for q in (0, 1):
        x, y = a[q], a[q + 2]
        a[q] = jnp.where(low, x, pltpu.roll(y, 64, 1))
        a[q + 2] = jnp.where(low, pltpu.roll(x, 64, 1), y)
    for q in (0, 2):
        x, y = a[q], a[q + 1]
        a[q] = jnp.where(even, x, pltpu.roll(y, 32, 1))
        a[q + 1] = jnp.where(even, pltpu.roll(x, 96, 1), y)
    return a


def nt(x, y):
    return lax.dot_general(x, y, (((1,), (1,)), ((), ())), preferred_element_type=f32)


def nn(x, y):
    return lax.dot_general(x, y, (((1,), (0,)), ((), ())), preferred_element_type=f32)


def right_products(x, first, tiles, b_scr, x_scr, v_scr, m_ref):
    count = x.shape[0] // R
    start = {}
    for j in (1, 2, 3):
        high, low = split(x)
        x_scr[: count * R, :N] = high
        x_scr[: count * R, N : 2 * N] = low
        x_scr[: count * R, 2 * N :] = high
        count -= 2
        first += 1
        total = None
        for s in range(3):
            part = nt(x_scr[s * R : (s + count) * R], b_scr[s])
            total = part if total is None else total + part
        x = total
        v_scr[j - 1, : count * R] = x
        start[j] = first
    for m, entries in enumerate(tiles):
        filler = next(entry for entry in entries if entry is not None)
        for h in range(2):
            parts = []
            for entry in entries:
                j, d = entry or filler
                row = (d - start[j]) * R
                parts.append(v_scr[j - 1, row : row + R, 128 * h : 128 * (h + 1)])
            for b, part in enumerate(exchange_blocks(parts)):
                m_ref[4 * h + b, :, 128 * m : 128 * (m + 1)] = part


def local_kernel(shift_ref, n_ref, c_ref, *rest):
    outs = rest[:8]
    edge_ref, first_ref, b_ref, x_scr, v_scr, m_scr = rest[8:]
    edge_ref[...] = n_ref[R - HALO :]
    first_ref[...] = n_ref[:HALO]
    split_taps(c_ref, shift_ref, b_ref)
    right_products(n_ref[0:23].reshape(23 * R, N), 0, LOCAL, b_ref, x_scr, v_scr, m_scr)
    for out, slot in zip(outs, SLOTS):
        out[...] = m_scr[target(*slot)]


def halo_kernel(halo_ref, first_ref, b_ref, *rest):
    outs = rest[:4]
    x_scr, v_scr, m_scr = rest[4:]
    x = jnp.concatenate([halo_ref[...].reshape(HALO * R, N), first_ref[...].reshape(HALO * R, N)], axis=0)
    right_products(x, -HALO, HALOS, b_ref, x_scr, v_scr, m_scr)
    for k, out in enumerate(outs):
        for e in range(2):
            out[e] = m_scr[target(k, e)]


def gather_kernel(*refs):
    for ref, slot in zip(refs, SLOTS):
        row = pl.multiple_of(source(*slot) * R, R)
        refs[8][pl.ds(row, R), :] = ref[...]


def left_kernel(b_ref, r_ref, *rest):
    received = rest[:4]
    other_ref, result_ref, mirror_ref, x_scr, h_scr = rest[4:]
    for k, ref in enumerate(received):
        h_scr[pl.ds(pl.multiple_of(source(k, 0) * R, R), R), :] = ref[0]
        h_scr[pl.ds(pl.multiple_of(source(k, 1) * R, R), R), :] = other_ref[k]
    block = block_of_lane(N)
    total = None
    for j in (3, 2, 1):
        tiles = []
        for g in range(GRID):
            value = None
            for q in range(4):
                entry = (j, GRID * q + g - BASE)
                if entry not in WHERE:
                    continue
                m, p = WHERE[entry]
                if m < len(LOCAL):
                    part = r_ref[:, 128 * m : 128 * (m + 1)]
                else:
                    part = h_scr[:, 128 * (m - len(LOCAL)) : 128 * (m - len(LOCAL) + 1)]
                if p != q:
                    part = pltpu.roll(part, (32 * (q - p)) % 128, 1)
                value = part if value is None else jnp.where(block == q, part, value)
            tiles.append(value if total is None else value + total[:, 128 * g : 128 * (g + 1)])
        edges = [pltpu.roll(tiles[-1], 32, 1)] + tiles + [pltpu.roll(tiles[0], 96, 1)]
        for g, part in enumerate(edges):
            high, low = split(part)
            x_scr[:N, 128 * g : 128 * (g + 1)] = high
            x_scr[N : 2 * N, 128 * g : 128 * (g + 1)] = low
            x_scr[2 * N :, 128 * g : 128 * (g + 1)] = high
        total = None
        for s in range(3):
            part = nn(b_ref[s], x_scr[:, 128 * (2 - s) : 128 * (2 - s + GRID)])
            total = part if total is None else total + part
    tiles = [total[:, 128 * g : 128 * (g + 1)] for g in range(GRID)]
    for m, entries in enumerate(RESULT):
        value = None
        for q, d in enumerate(entries):
            if d is None:
                continue
            g, p = place(d)
            part = tiles[g] if p == q else pltpu.roll(tiles[g], (32 * (q - p)) % 128, 1)
            value = part if value is None else jnp.where(block == q, part, value)
        result_ref[:, 128 * m : 128 * (m + 1)] = value
    for g in range(GRID):
        turned = tiles[g].T
        for q in range(4):
            d = GRID * q + g - BASE
            if 1 <= d <= 15:
                mirror_ref[15 - d] = turned[32 * q : 32 * (q + 1)]


def pack_kernel(result_ref, *outs):
    for k, out in enumerate(outs):
        for e in range(2):
            row = pl.multiple_of(target(k, e) * R, R)
            out[e] = result_ref[pl.ds(row, R), :]


def mirror_kernel(n_ref, mirror_ref, out_ref):
    out_ref[...] = n_ref[17:] + mirror_ref[...]


def join_kernel(n_ref, mirror_ref, *rest):
    received = rest[:4]
    other_ref, out_ref, r_scr = rest[4:]
    for k, ref in enumerate(received):
        r_scr[source(k, 0)] = ref[0]
        r_scr[source(k, 1)] = other_ref[k]
    for m, entries in enumerate(RESULT):
        for h in range(2):
            lanes = slice(128 * h, 128 * (h + 1))
            parts = [r_scr[4 * h + b, :, 128 * m : 128 * (m + 1)] for b in range(4)]
            for d, part in zip(entries, exchange_blocks(parts)):
                if d is not None:
                    out_ref[d, :, lanes] = n_ref[d, :, lanes] + part
    out_ref[17:] = mirror_ref[...]


PARAMS = pltpu.CompilerParams(vmem_limit_bytes=24 * 1024 * 1024)
SMEM = pl.BlockSpec(memory_space=pltpu.SMEM)
VMEM = pl.BlockSpec(memory_space=pltpu.VMEM)


def send(array, k, e):
    pairs = [(c, 2 * ((c // 2 + k) % 4) + (c + e) % 2) for c in range(8)]
    return lax.ppermute(array, "col", pairs)


def cost(units, elements):
    return pl.CostEstimate(flops=units * 18 * R * N * N, bytes_accessed=4 * elements, transcendentals=0)


def right_scratch(offsets):
    return [
        pltpu.VMEM((offsets * R, 3 * N), bf16),
        pltpu.VMEM((3, (offsets - 2) * R, N), f32),
    ]


def two_level(parts):
    parts = [parts[0]] + [send(parts[k], k, 0) for k in (1, 3, 2)]
    parts = [parts[0], parts[1], parts[3], parts[2]]
    return parts, send(jnp.stack([part[1] for part in parts]), 0, 1)


def body(noise_cov, couplings, shifts):
    *local, edge, first, taps_split = pl.pallas_call(
        local_kernel,
        out_shape=[jax.ShapeDtypeStruct((R, LOCAL_LANES), f32)] * 8
        + [jax.ShapeDtypeStruct((HALO, R, N), f32)] * 2
        + [jax.ShapeDtypeStruct((3, N, 3 * N), bf16)],
        in_specs=[SMEM, VMEM, VMEM],
        out_specs=[VMEM] * 11,
        scratch_shapes=right_scratch(23) + [pltpu.VMEM((8, R, LOCAL_LANES), f32)],
        compiler_params=PARAMS,
        cost_estimate=cost(57, 1 << 20),
        name="local_right_products",
    )(shifts, noise_cov, couplings)
    halo = lax.ppermute(noise_cov[R - HALO :], "off", [(o, (o + 1) % 16) for o in range(16)])
    local = [array if slot == (0, 0) else send(array, *slot) for array, slot in zip(local, SLOTS)]
    halos = pl.pallas_call(
        halo_kernel,
        out_shape=[jax.ShapeDtypeStruct((2, R, HALO_LANES), f32)] * 4,
        in_specs=[VMEM] * 3,
        out_specs=[VMEM] * 4,
        scratch_shapes=right_scratch(12) + [pltpu.VMEM((8, R, HALO_LANES), f32)],
        compiler_params=PARAMS,
        cost_estimate=cost(10, 1 << 19),
        name="halo_right_products",
    )(halo, first, taps_split)
    halos, other = two_level(halos)
    rows = pl.pallas_call(
        gather_kernel,
        out_shape=jax.ShapeDtypeStruct((N, LOCAL_LANES), f32),
        in_specs=[VMEM] * 8,
        out_specs=VMEM,
        compiler_params=PARAMS,
        cost_estimate=cost(300, 1 << 20),
        name="gather_rows",
    )(*local)
    result, mirror = pl.pallas_call(
        left_kernel,
        out_shape=[jax.ShapeDtypeStruct((N, OUT_LANES), f32), jax.ShapeDtypeStruct((15, R, N), f32)],
        in_specs=[VMEM] * 7,
        out_specs=[VMEM] * 2,
        scratch_shapes=[
            pltpu.VMEM((3 * N, 128 * (GRID + 2)), bf16),
            pltpu.VMEM((N, HALO_LANES), f32),
        ],
        compiler_params=PARAMS,
        cost_estimate=cost(72, 1 << 21),
        name="left_products",
    )(taps_split, rows, *halos, other)
    rows = pl.pallas_call(
        pack_kernel,
        out_shape=[jax.ShapeDtypeStruct((2, R, OUT_LANES), f32)] * 4,
        in_specs=[VMEM],
        out_specs=[VMEM] * 4,
        compiler_params=PARAMS,
        cost_estimate=cost(30, 1 << 19),
        name="pack",
    )(result)
    mirror = lax.ppermute(mirror, "off", [(o, 15 - o) for o in range(16)])
    mirror = pl.pallas_call(
        mirror_kernel,
        out_shape=jax.ShapeDtypeStruct((15, R, N), f32),
        in_specs=[VMEM] * 2,
        out_specs=VMEM,
        compiler_params=PARAMS,
        cost_estimate=cost(300, 1 << 19),
        name="join_mirror",
    )(noise_cov, mirror)
    rows, other = two_level(rows)
    return pl.pallas_call(
        join_kernel,
        out_shape=jax.ShapeDtypeStruct((R, R, N), f32),
        in_specs=[VMEM] * 7,
        out_specs=VMEM,
        scratch_shapes=[pltpu.VMEM((8, R, OUT_LANES), f32)],
        compiler_params=PARAMS,
        name="join",
    )(noise_cov, mirror, *rows, other)


def solution(mesh):
    return jax.shard_map(
        body,
        mesh=mesh,
        in_specs=(P("off", "col", None), P(), P()),
        out_specs=P("off", "col", None),
        check_vma=False,
    )
```

profile of v0, /device:TPU:1, one launch (start us, length us, event | category | flops | bytes accessed | tf_op | source)
XLA Modules:
  0.0 66.0 jit_solution(6305493627089514673)
XLA Ops:
  0.0 0.9 %slice.27 = f32[6,32,256]{2,1,0:T(8,128)S(1)} slice(f32[32,32,256]{2,1,0:T(8,128)} %n_ref.5), slice={[26:32], [0:32], [0:256]} | slice | bytes 393216 | tf_op jit(solution)/shard_map/slice | solution.py:292
  0.9 2.2 %collective-permute-start.7 = (f32[6,32,256]{2,1,0:T(8,128)S(1)}, f32[6,32,256]{2,1,0:T(8,128)S(1)}, u32[]{:S(2)}, u32[]{:S(2)}) collective-permute-start(f32[6,32,256]{2,1,0:T(8,128)S(1)} %slice.27), channel_id=1, source_target_pairs={{0,8},{8,16},{16,24},{24,32},{32,40},{40,48},{48,56},{56,64},{64,7... | collective-permute-start | bytes 589832 | tf_op jit(solution)/shard_map/ppermute | solution.py:292
  3.1 1.2 %copy-done = f32[32,32,256]{2,1,0:T(8,128)S(1)} copy-done((f32[32,32,256]{2,1,0:T(8,128)S(1)}, f32[32,32,256]{2,1,0:T(8,128)}, u32[]{:S(2)}) %copy-start) | copy-done | bytes 1048600
  4.4 1.1 %copy-done.2 = f32[3,256,256]{2,1,0:T(8,128)S(1)} copy-done((f32[3,256,256]{2,1,0:T(8,128)S(1)}, f32[3,256,256]{2,1,0:T(8,128)}, u32[]{:S(2)}) %copy-start.2) | copy-done | bytes 786456
  5.5 0.7 copy-done.3
  6.2 5.6 %local_right_products.1 = (f32[32,1664]{1,0:T(8,128)S(1)}, f32[32,1664]{1,0:T(8,128)S(1)}, f32[32,1664]{1,0:T(8,128)S(1)}, f32[32,1664]{1,0:T(8,128)S(1)}, f32[3...) custom-call(s32[3]{0:T(128)S(1)} %copy-done.3, ...), custom_call_target="tpu_custom_call" | custom-call | flops 2151677952 | bytes 4194304 | tf_op jit(solution)/shard_map/local_right_products/pallas_call | solution.py:280
  11.8 1.6 %collective-permute-start = (f32[32,1664]{1,0:T(8,128)S(1)}, f32[32,1664]{1,0:T(8,128)S(1)}, u32[]{:S(2)}, u32[]{:S(2)}) collective-permute-start(f32[32,1664]{1,0:T(8,128)S(1)} %get-tuple-element.26), channel_id=1, source_target_pairs={{0,2},{1,3},{2,4},{3,5},{4,6},{5,7},{6,0},{7,1},{8,10},{9,11},{10,... | collective-permute-start | bytes 638984 | tf_op jit(solution)/shard_map/ppermute | solution.py:259
  13.4 2.1 %collective-permute-start.1 = (f32[32,1664]{1,0:T(8,128)S(1)}, f32[32,1664]{1,0:T(8,128)S(1)}, u32[]{:S(2)}, u32[]{:S(2)}) collective-permute-start(f32[32,1664]{1,0:T(8,128)S(1)} %get-tuple-element.27), channel_id=1, source_target_pairs={{0,6},{1,7},{2,0},{3,1},{4,2},{5,3},{6,4},{7,5},{8,14},{9,15},{10,... | collective-permute-start | bytes 638984 | tf_op jit(solution)/shard_map/ppermute | solution.py:259
  15.5 2.3 %halo_right_products.1 = (f32[2,32,384]{2,1,0:T(8,128)S(1)}, f32[2,32,384]{2,1,0:T(8,128)S(1)}, f32[2,32,384]{2,1,0:T(8,128)S(1)}, f32[2,32,384]{2,1,0:T(8,128)S(1)}) custom-call(f32[6,32,256]{2,1,0:T(8,128)S(1)} %collective-permute-done.7.halo_ref, f32[6,32,256]{2,1,0:T(8,128)S(1)} %get-tuple-element.34.first_ref, ...), custom_call_target="tpu_custom_call" | custom-call | flops 377487360 | bytes 2097152 | tf_op jit(solution)/shard_map/halo_right_products/pallas_call | solution.py:294
  17.9 2.6 %collective-permute-start.9 = (f32[2,32,384]{2,1,0:T(8,128)S(1)}, f32[2,32,384]{2,1,0:T(8,128)S(1)}, u32[]{:S(2)}, u32[]{:S(2)}) collective-permute-start(f32[2,32,384]{2,1,0:T(8,128)S(1)} %get-tuple-element.37), channel_id=1, source_target_pairs={{0,4},{1,5},{2,6},{3,7},{4,0},{5,1},{6,2},{7,3},{8,12},{9,13},{10,... | collective-permute-start | bytes 294920 | tf_op jit(solution)/shard_map/ppermute | solution.py:259
  20.5 0.7 %collective-permute-start.10 = (f32[2,32,384]{2,1,0:T(8,128)S(1)}, f32[2,32,384]{2,1,0:T(8,128)S(1)}, u32[]{:S(2)}, u32[]{:S(2)}) collective-permute-start(f32[2,32,384]{2,1,0:T(8,128)S(1)} %get-tuple-element.38), channel_id=1, source_target_pairs={{0,6},{1,7},{2,0},{3,1},{4,2},{5,3},{6,4},{7,5},{8,14},{9,15},{10,... | collective-permute-start | bytes 294920 | tf_op jit(solution)/shard_map/ppermute | solution.py:259
  21.3 1.7 %collective-permute-start.2 = (f32[32,1664]{1,0:T(8,128)S(1)}, f32[32,1664]{1,0:T(8,128)S(1)}, u32[]{:S(2)}, u32[]{:S(2)}) collective-permute-start(f32[32,1664]{1,0:T(8,128)S(1)} %get-tuple-element.28), channel_id=1, source_target_pairs={{0,4},{1,5},{2,6},{3,7},{4,0},{5,1},{6,2},{7,3},{8,12},{9,13},{10,... | collective-permute-start | bytes 638984 | tf_op jit(solution)/shard_map/ppermute | solution.py:259
  22.9 1.7 %collective-permute-start.3 = (f32[32,1664]{1,0:T(8,128)S(1)}, f32[32,1664]{1,0:T(8,128)S(1)}, u32[]{:S(2)}, u32[]{:S(2)}) collective-permute-start(f32[32,1664]{1,0:T(8,128)S(1)} %get-tuple-element.29), channel_id=1, source_target_pairs={{0,3},{1,2},{2,5},{3,4},{4,7},{5,6},{6,1},{7,0},{8,11},{9,10},{10,... | collective-permute-start | bytes 638984 | tf_op jit(solution)/shard_map/ppermute | solution.py:259
  24.6 2.4 %collective-permute-start.4 = (f32[32,1664]{1,0:T(8,128)S(1)}, f32[32,1664]{1,0:T(8,128)S(1)}, u32[]{:S(2)}, u32[]{:S(2)}) collective-permute-start(f32[32,1664]{1,0:T(8,128)S(1)} %get-tuple-element.30), channel_id=1, source_target_pairs={{0,7},{1,6},{2,1},{3,0},{4,3},{5,2},{6,5},{7,4},{8,15},{9,14},{10,... | collective-permute-start | bytes 638984 | tf_op jit(solution)/shard_map/ppermute | solution.py:259
  27.0 2.3 %collective-permute-start.5 = (f32[32,1664]{1,0:T(8,128)S(1)}, f32[32,1664]{1,0:T(8,128)S(1)}, u32[]{:S(2)}, u32[]{:S(2)}) collective-permute-start(f32[32,1664]{1,0:T(8,128)S(1)} %get-tuple-element.31), channel_id=1, source_target_pairs={{0,5},{1,4},{2,7},{3,6},{4,1},{5,0},{6,3},{7,2},{8,13},{9,12},{10,... | collective-permute-start | bytes 638984 | tf_op jit(solution)/shard_map/ppermute | solution.py:259
  29.4 0.3 collective-permute-done.2.refs_2_
  29.7 3.6 %collective-permute-start.11 = (f32[4,32,384]{2,1,0:T(8,128)S(1)}, f32[4,32,384]{2,1,0:T(8,128)S(1)}, u32[]{:S(2)}, u32[]{:S(2)}) collective-permute-start(f32[4,32,384]{2,1,0:T(8,128)S(1)} %pad_maximum_fusion.1), channel_id=1, source_target_pairs={{0,1},{1,0},{2,3},{3,2},{4,5},{5,4},{6,7},{7,6},{8,9},{9,8},{10,11... | collective-permute-start | bytes 589832 | tf_op jit(solution)/shard_map/ppermute | solution.py:259
  33.3 4.1 %collective-permute-done.3.refs_3_ = f32[32,1664]{1,0:T(8,128)S(1)} collective-permute-done((f32[32,1664]{1,0:T(8,128)S(1)}, f32[32,1664]{1,0:T(8,128)S(1)}, u32[]{:S(2)}, u32[]{:S(2)}) %collective-permute-start.3) | collective-permute-done | bytes 213024 | tf_op jit(solution)/shard_map/ppermute | solution.py:259
  37.4 0.4 collective-permute-done.4.refs_4_
  37.8 2.4 %collective-permute-done.5.refs_5_ = f32[32,1664]{1,0:T(8,128)S(1)} collective-permute-done((f32[32,1664]{1,0:T(8,128)S(1)}, f32[32,1664]{1,0:T(8,128)S(1)}, u32[]{:S(2)}, u32[]{:S(2)}) %collective-permute-start.5) | collective-permute-done | bytes 213024 | tf_op jit(solution)/shard_map/ppermute | solution.py:259
  40.1 0.1 gather_rows.1.r_ref
  40.3 5.0 %left_products.1 = (f32[256,640]{1,0:T(8,128)S(1)}, f32[15,32,256]{2,1,0:T(8,128)S(1)}) custom-call(bf16[3,256,768]{2,1,0:T(8,128)(2,1)S(1)} %get-tuple-element.25.b_ref, f32[256,1664]{1,0:T(8,128)S(1)} %gather_rows.1.r_ref, f32[2,32,384]{2,1,0:T(8,128)S(1)} %get-tuple-element.35.rest_0_, f32[2,32,384]{2,1,0:T(8,128)S(1)} %collective-permute-done.8.rest_1_, ...), custom_call_target="tpu_custom_call" | custom-call | flops 2717908992 | bytes 8388608 | tf_op jit(solution)/shard_map/left_products/pallas_call | solution.py:314
  45.3 3.7 %collective-permute-start.12 = (f32[15,32,256]{2,1,0:T(8,128)S(1)}, f32[15,32,256]{2,1,0:T(8,128)S(1)}, u32[]{:S(2)}, u32[]{:S(2)}) collective-permute-start(f32[15,32,256]{2,1,0:T(8,128)S(1)} %get-tuple-element.39), channel_id=1, source_target_pairs={{0,120},{8,112},{16,104},{24,96},{32,88},{40,80},{48,72},{56,64},{... | collective-permute-start | bytes 1474568 | tf_op jit(solution)/shard_map/ppermute | solution.py:336
  49.1 2.3 %collective-permute-start.15 = (f32[2,32,640]{2,1,0:T(8,128)S(1)}, f32[2,32,640]{2,1,0:T(8,128)S(1)}, u32[]{:S(2)}, u32[]{:S(2)}) collective-permute-start(f32[2,32,640]{2,1,0:T(8,128)S(1)} %get-tuple-element.44), channel_id=1, source_target_pairs={{0,6},{1,7},{2,0},{3,1},{4,2},{5,3},{6,4},{7,5},{8,14},{9,15},{10,... | collective-permute-start | bytes 491528 | tf_op jit(solution)/shard_map/ppermute | solution.py:259
  51.4 0.4 collective-permute-start.14
  51.8 0.3 collective-permute-start.13
  52.1 6.4 %collective-permute-done.15.rest_3_ = f32[2,32,640]{2,1,0:T(8,128)S(1)} collective-permute-done((f32[2,32,640]{2,1,0:T(8,128)S(1)}, f32[2,32,640]{2,1,0:T(8,128)S(1)}, u32[]{:S(2)}, u32[]{:S(2)}) %collective-permute-start.15) | collective-permute-done | bytes 163872 | tf_op jit(solution)/shard_map/ppermute | solution.py:259
  58.5 0.7 %collective-permute-done.14.rest_2_ = f32[2,32,640]{2,1,0:T(8,128)S(1)} collective-permute-done((f32[2,32,640]{2,1,0:T(8,128)S(1)}, f32[2,32,640]{2,1,0:T(8,128)S(1)}, u32[]{:S(2)}, u32[]{:S(2)}) %collective-permute-start.14) | collective-permute-done | bytes 163872 | tf_op jit(solution)/shard_map/ppermute | solution.py:259
  59.2 3.2 %collective-permute-done.13.rest_1_ = f32[2,32,640]{2,1,0:T(8,128)S(1)} collective-permute-done((f32[2,32,640]{2,1,0:T(8,128)S(1)}, f32[2,32,640]{2,1,0:T(8,128)S(1)}, u32[]{:S(2)}, u32[]{:S(2)}) %collective-permute-start.13) | collective-permute-done | bytes 163872 | tf_op jit(solution)/shard_map/ppermute | solution.py:259
  62.4 0.5 collective-permute-start.16
  63.0 1.2 %collective-permute-done.16.rest_4_ = f32[4,32,640]{2,1,0:T(8,128)S(1)} collective-permute-done((f32[4,32,640]{2,1,0:T(8,128)S(1)}, f32[4,32,640]{2,1,0:T(8,128)S(1)}, u32[]{:S(2)}, u32[]{:S(2)}) %collective-permute-start.16) | collective-permute-done | bytes 327712 | tf_op jit(solution)/shard_map/ppermute | solution.py:259
  64.2 1.8 %join.1 = f32[32,32,256]{2,1,0:T(8,128)} custom-call(f32[32,32,256]{2,1,0:T(8,128)S(1)} %copy-done.1, f32[15,32,256]{2,1,0:T(8,128)S(1)} %join_mirror.1.mirror_ref, f32[2,32,640]{2,1,0:T(8,128)S(1)} %get-tuple-element.41.rest_0_, f32[2,32,640]{2,1,0:T(8,128)S(1)} %collective-permute-done.13.rest_1_, f32[2,32,640]{2,1,0:T(8,128)S(1)} %collective-permute-done.14.rest_2_, ...), custom_call_target="tpu_custom_call" | custom-call | tf_op jit(solution)/shard_map/join/pallas_call | solution.py:347
  (28 shorter events, 0.3 us)
Async XLA Ops:
  0.9 14.6 %collective-permute-start.7 = (f32[6,32,256]{2,1,0:T(8,128)S(1)}, f32[6,32,256]{2,1,0:T(8,128)S(1)}, u32[]{:S(2)}, u32[]{:S(2)}) collective-permute-start(f32[6,32,256]{2,1,0:T(8,128)S(1)} %slice.27), channel_id=1, source_target_pairs={{0,8},{8,16},{16,24},{24,32},{32,40},{40,48},{48,56},{56,64},{64,7... | collective-permute-start | bytes 589832 | tf_op jit(solution)/shard_map/ppermute | solution.py:292
  3.1 1.2 %copy-start = (f32[32,32,256]{2,1,0:T(8,128)S(1)}, f32[32,32,256]{2,1,0:T(8,128)}, u32[]{:S(2)}) copy-start(f32[32,32,256]{2,1,0:T(8,128)} %n_ref.5) | copy-start | bytes 3145732
  4.4 1.1 %copy-start.2 = (f32[3,256,256]{2,1,0:T(8,128)S(1)}, f32[3,256,256]{2,1,0:T(8,128)}, u32[]{:S(2)}) copy-start(f32[3,256,256]{2,1,0:T(8,128)} %c_ref.1) | copy-start | bytes 2359300
  5.5 0.7 copy-start.3
  11.8 9.5 %collective-permute-start = (f32[32,1664]{1,0:T(8,128)S(1)}, f32[32,1664]{1,0:T(8,128)S(1)}, u32[]{:S(2)}, u32[]{:S(2)}) collective-permute-start(f32[32,1664]{1,0:T(8,128)S(1)} %get-tuple-element.26), channel_id=1, source_target_pairs={{0,2},{1,3},{2,4},{3,5},{4,6},{5,7},{6,0},{7,1},{8,10},{9,11},{10,... | collective-permute-start | bytes 638984 | tf_op jit(solution)/shard_map/ppermute | solution.py:259
  13.4 9.5 %collective-permute-start.1 = (f32[32,1664]{1,0:T(8,128)S(1)}, f32[32,1664]{1,0:T(8,128)S(1)}, u32[]{:S(2)}, u32[]{:S(2)}) collective-permute-start(f32[32,1664]{1,0:T(8,128)S(1)} %get-tuple-element.27), channel_id=1, source_target_pairs={{0,6},{1,7},{2,0},{3,1},{4,2},{5,3},{6,4},{7,5},{8,14},{9,15},{10,... | collective-permute-start | bytes 638984 | tf_op jit(solution)/shard_map/ppermute | solution.py:259
  17.8 6.8 %collective-permute-start.8 = (f32[2,32,384]{2,1,0:T(8,128)S(1)}, f32[2,32,384]{2,1,0:T(8,128)S(1)}, u32[]{:S(2)}, u32[]{:S(2)}) collective-permute-start(f32[2,32,384]{2,1,0:T(8,128)S(1)} %get-tuple-element.36), channel_id=1, source_target_pairs={{0,2},{1,3},{2,4},{3,5},{4,6},{5,7},{6,0},{7,1},{8,10},{9,11},{10,... | collective-permute-start | bytes 294920 | tf_op jit(solution)/shard_map/ppermute | solution.py:259
  17.9 9.1 %collective-permute-start.9 = (f32[2,32,384]{2,1,0:T(8,128)S(1)}, f32[2,32,384]{2,1,0:T(8,128)S(1)}, u32[]{:S(2)}, u32[]{:S(2)}) collective-permute-start(f32[2,32,384]{2,1,0:T(8,128)S(1)} %get-tuple-element.37), channel_id=1, source_target_pairs={{0,4},{1,5},{2,6},{3,7},{4,0},{5,1},{6,2},{7,3},{8,12},{9,13},{10,... | collective-permute-start | bytes 294920 | tf_op jit(solution)/shard_map/ppermute | solution.py:259
  20.5 8.8 %collective-permute-start.10 = (f32[2,32,384]{2,1,0:T(8,128)S(1)}, f32[2,32,384]{2,1,0:T(8,128)S(1)}, u32[]{:S(2)}, u32[]{:S(2)}) collective-permute-start(f32[2,32,384]{2,1,0:T(8,128)S(1)} %get-tuple-element.38), channel_id=1, source_target_pairs={{0,6},{1,7},{2,0},{3,1},{4,2},{5,3},{6,4},{7,5},{8,14},{9,15},{10,... | collective-permute-start | bytes 294920 | tf_op jit(solution)/shard_map/ppermute | solution.py:259
  21.3 8.4 %collective-permute-start.2 = (f32[32,1664]{1,0:T(8,128)S(1)}, f32[32,1664]{1,0:T(8,128)S(1)}, u32[]{:S(2)}, u32[]{:S(2)}) collective-permute-start(f32[32,1664]{1,0:T(8,128)S(1)} %get-tuple-element.28), channel_id=1, source_target_pairs={{0,4},{1,5},{2,6},{3,7},{4,0},{5,1},{6,2},{7,3},{8,12},{9,13},{10,... | collective-permute-start | bytes 638984 | tf_op jit(solution)/shard_map/ppermute | solution.py:259
  22.9 14.4 %collective-permute-start.3 = (f32[32,1664]{1,0:T(8,128)S(1)}, f32[32,1664]{1,0:T(8,128)S(1)}, u32[]{:S(2)}, u32[]{:S(2)}) collective-permute-start(f32[32,1664]{1,0:T(8,128)S(1)} %get-tuple-element.29), channel_id=1, source_target_pairs={{0,3},{1,2},{2,5},{3,4},{4,7},{5,6},{6,1},{7,0},{8,11},{9,10},{10,... | collective-permute-start | bytes 638984 | tf_op jit(solution)/shard_map/ppermute | solution.py:259
  24.6 13.1 %collective-permute-start.4 = (f32[32,1664]{1,0:T(8,128)S(1)}, f32[32,1664]{1,0:T(8,128)S(1)}, u32[]{:S(2)}, u32[]{:S(2)}) collective-permute-start(f32[32,1664]{1,0:T(8,128)S(1)} %get-tuple-element.30), channel_id=1, source_target_pairs={{0,7},{1,6},{2,1},{3,0},{4,3},{5,2},{6,5},{7,4},{8,15},{9,14},{10,... | collective-permute-start | bytes 638984 | tf_op jit(solution)/shard_map/ppermute | solution.py:259
  27.0 13.1 %collective-permute-start.5 = (f32[32,1664]{1,0:T(8,128)S(1)}, f32[32,1664]{1,0:T(8,128)S(1)}, u32[]{:S(2)}, u32[]{:S(2)}) collective-permute-start(f32[32,1664]{1,0:T(8,128)S(1)} %get-tuple-element.31), channel_id=1, source_target_pairs={{0,5},{1,4},{2,7},{3,6},{4,1},{5,0},{6,3},{7,2},{8,13},{9,12},{10,... | collective-permute-start | bytes 638984 | tf_op jit(solution)/shard_map/ppermute | solution.py:259
  29.4 10.8 %collective-permute-start.6 = (f32[32,1664]{1,0:T(8,128)S(1)}, f32[32,1664]{1,0:T(8,128)S(1)}, u32[]{:S(2)}, u32[]{:S(2)}) collective-permute-start(f32[32,1664]{1,0:T(8,128)S(1)} %get-tuple-element.32), channel_id=1, source_target_pairs={{0,1},{1,0},{2,3},{3,2},{4,5},{5,4},{6,7},{7,6},{8,9},{9,8},{10,11... | collective-permute-start | bytes 638984 | tf_op jit(solution)/shard_map/ppermute | solution.py:259
  29.7 10.6 %collective-permute-start.11 = (f32[4,32,384]{2,1,0:T(8,128)S(1)}, f32[4,32,384]{2,1,0:T(8,128)S(1)}, u32[]{:S(2)}, u32[]{:S(2)}) collective-permute-start(f32[4,32,384]{2,1,0:T(8,128)S(1)} %pad_maximum_fusion.1), channel_id=1, source_target_pairs={{0,1},{1,0},{2,3},{3,2},{4,5},{5,4},{6,7},{7,6},{8,9},{9,8},{10,11... | collective-permute-start | bytes 589832 | tf_op jit(solution)/shard_map/ppermute | solution.py:259
  45.3 17.7 %collective-permute-start.12 = (f32[15,32,256]{2,1,0:T(8,128)S(1)}, f32[15,32,256]{2,1,0:T(8,128)S(1)}, u32[]{:S(2)}, u32[]{:S(2)}) collective-permute-start(f32[15,32,256]{2,1,0:T(8,128)S(1)} %get-tuple-element.39), channel_id=1, source_target_pairs={{0,120},{8,112},{16,104},{24,96},{32,88},{40,80},{48,72},{56,64},{... | collective-permute-start | bytes 1474568 | tf_op jit(solution)/shard_map/ppermute | solution.py:336
  49.0 13.9 %copy-start.1 = (f32[32,32,256]{2,1,0:T(8,128)S(1)}, f32[32,32,256]{2,1,0:T(8,128)}, u32[]{:S(2)}) copy-start(f32[32,32,256]{2,1,0:T(8,128)} %n_ref.5) | copy-start | bytes 3145732
  49.1 9.4 %collective-permute-start.15 = (f32[2,32,640]{2,1,0:T(8,128)S(1)}, f32[2,32,640]{2,1,0:T(8,128)S(1)}, u32[]{:S(2)}, u32[]{:S(2)}) collective-permute-start(f32[2,32,640]{2,1,0:T(8,128)S(1)} %get-tuple-element.44), channel_id=1, source_target_pairs={{0,6},{1,7},{2,0},{3,1},{4,2},{5,3},{6,4},{7,5},{8,14},{9,15},{10,... | collective-permute-start | bytes 491528 | tf_op jit(solution)/shard_map/ppermute | solution.py:259
  51.4 7.8 %collective-permute-start.14 = (f32[2,32,640]{2,1,0:T(8,128)S(1)}, f32[2,32,640]{2,1,0:T(8,128)S(1)}, u32[]{:S(2)}, u32[]{:S(2)}) collective-permute-start(f32[2,32,640]{2,1,0:T(8,128)S(1)} %get-tuple-element.43), channel_id=1, source_target_pairs={{0,4},{1,5},{2,6},{3,7},{4,0},{5,1},{6,2},{7,3},{8,12},{9,13},{10,... | collective-permute-start | bytes 491528 | tf_op jit(solution)/shard_map/ppermute | solution.py:259
  51.8 10.6 %collective-permute-start.13 = (f32[2,32,640]{2,1,0:T(8,128)S(1)}, f32[2,32,640]{2,1,0:T(8,128)S(1)}, u32[]{:S(2)}, u32[]{:S(2)}) collective-permute-start(f32[2,32,640]{2,1,0:T(8,128)S(1)} %get-tuple-element.42), channel_id=1, source_target_pairs={{0,2},{1,3},{2,4},{3,5},{4,6},{5,7},{6,0},{7,1},{8,10},{9,11},{10,... | collective-permute-start | bytes 491528 | tf_op jit(solution)/shard_map/ppermute | solution.py:259
  62.4 1.8 %collective-permute-start.16 = (f32[4,32,640]{2,1,0:T(8,128)S(1)}, f32[4,32,640]{2,1,0:T(8,128)S(1)}, u32[]{:S(2)}, u32[]{:S(2)}) collective-permute-start(f32[4,32,640]{2,1,0:T(8,128)S(1)} %pad_maximum_fusion), channel_id=1, source_target_pairs={{0,1},{1,0},{2,3},{3,2},{4,5},{5,4},{6,7},{7,6},{8,9},{9,8},{10,11... | collective-permute-start | bytes 983048 | tf_op jit(solution)/shard_map/ppermute | solution.py:259
where the time goes:
time: 66.2 us; the launch traced here: 66 us
  starting transfers between devices  28.4 us (43%)
  waiting for transfers between devices  18.6 us (28%)
  Pallas kernels  14.9 us (23%)
  local copies, waits for them, and re-layouts  4 us (6%)
    ppermute x15, starting transfers between devices, send(): return lax.ppermute(array, 'col', pairs)  22.4 us
    ppermute x15, waiting for transfers between devices, send(): return lax.ppermute(array, 'col', pairs)  18.6 us
    pallas_call x1, Pallas kernels, body(): pl.pallas_call(local_kernel, out_shape=[jax.ShapeDtypeStruct((R, LOCAL_LA...  5.63 us
    pallas_call x1, Pallas kernels, body(): pl.pallas_call(left_kernel, out_shape=[jax.ShapeDtypeStruct((N, OUT_LANES...  5 us
    ppermute x1, starting transfers between devices, body(): mirror = lax.ppermute(mirror, 'off', [(o, 15 - o) for o in range(16)])  3.73 us
    unnamed x8, local copies, waits for them, and re-layouts  3.02 us
    pallas_call x1, Pallas kernels, body(): pl.pallas_call(halo_kernel, out_shape=[jax.ShapeDtypeStruct((2, R, HALO_L...  2.27 us
    ppermute x1, starting transfers between devices, body(): lax.ppermute(noise_cov[R - HALO:], 'off', [(o, (o + 1) % 16) for o in ran...  2.19 us
  transfers between devices with their start and end apart: 17, of which 8 were waited for; matrix products, arithmetic and copies ran while one was open for 0% of the time, Pallas kernels for 12%

commit v1 on v0

--- a/solution.py
+++ b/solution.py
@@ -46,11 +46,14 @@
     [(2, 0), (2, 1), (1, -1), (1, 0)],
 ]
 WHERE = {entry: (m, p) for m, tile in enumerate(LOCAL + HALOS) for p, entry in enumerate(tile) if entry}
-RESULT = [[5, 3, 9, 15], [11, 4, 10, 16], [0, 6, 12, None], [1, 7, 13, None], [2, 8, 14, None]]
+RESULT = [[5, 3, 9, 15], [11, 4, 10, 16], [0, 6, 12, 2], [1, 7, 13, 8]]
+LAST = 14
+OUT_ROWS = R * len(RESULT) + 8
 LOCAL_LANES = 128 * len(LOCAL)
 HALO_LANES = 128 * len(HALOS)
-OUT_LANES = 128 * len(RESULT)
-SLOTS = [(1, 0), (3, 0), (2, 0), (1, 1), (3, 1), (2, 1), (0, 1), (0, 0)]
+EARLY = [(2, 0), (2, 1)]
+LATE = [(1, 0), (3, 0), (1, 1), (3, 1), (0, 1)]
+SLOTS = EARLY + LATE + [(0, 0)]
 
 
 def coordinates():
@@ -73,16 +76,13 @@
     return high, (x - high.astype(f32)).astype(bf16)
 
 
-def split_taps(c_ref, shift_ref, b_ref):
-    for s in (-1, 0, 1):
-        block = None
-        for t in range(3):
-            chosen = jnp.where(shift_ref[t] == s, f32(1), f32(0)) * c_ref[t]
-            block = chosen if block is None else block + chosen
-        high, low = split(block)
-        b_ref[s + 1, :, :N] = high
-        b_ref[s + 1, :, N : 2 * N] = high
-        b_ref[s + 1, :, 2 * N :] = low
+def split_taps(c_ref, b_ref):
+    for s in range(3):
+        high, low = split(c_ref[s])
+        k = 3 * N * s
+        b_ref[:, k : k + N] = high
+        b_ref[:, k + N : k + 2 * N] = high
+        b_ref[:, k + 2 * N : k + 3 * N] = low
 
 
 def block_of_lane(rows):
@@ -125,7 +125,7 @@
         first += 1
         total = None
         for s in range(3):
-            part = nt(x_scr[s * R : (s + count) * R], b_scr[s])
+            part = nt(x_scr[s * R : (s + count) * R], b_scr[:, 3 * N * s : 3 * N * (s + 1)])
             total = part if total is None else total + part
         x = total
         v_scr[j - 1, : count * R] = x
@@ -142,39 +142,56 @@
                 m_ref[4 * h + b, :, 128 * m : 128 * (m + 1)] = part
 
 
-def local_kernel(shift_ref, n_ref, c_ref, *rest):
+def taps_kernel(shift_ref, n_ref, c_ref, edge_ref, own_ref, taps_ref):
+    edge_ref[...] = n_ref[R - HALO :]
+    own_ref[...] = n_ref[:23]
+    for s in (-1, 0, 1):
+        block = None
+        for t in range(3):
+            chosen = jnp.where(shift_ref[t] == s, f32(1), f32(0)) * c_ref[t]
+            block = chosen if block is None else block + chosen
+        taps_ref[s + 1] = block
+
+
+def local_kernel(n_ref, c_ref, *rest):
     outs = rest[:8]
-    edge_ref, first_ref, b_ref, x_scr, v_scr, m_scr = rest[8:]
-    edge_ref[...] = n_ref[R - HALO :]
+    first_ref, b_scr, x_scr, v_scr, m_scr = rest[8:]
     first_ref[...] = n_ref[:HALO]
-    split_taps(c_ref, shift_ref, b_ref)
-    right_products(n_ref[0:23].reshape(23 * R, N), 0, LOCAL, b_ref, x_scr, v_scr, m_scr)
+    split_taps(c_ref, b_scr)
+    right_products(n_ref[...].reshape(23 * R, N), 0, LOCAL, b_scr, x_scr, v_scr, m_scr)
     for out, slot in zip(outs, SLOTS):
         out[...] = m_scr[target(*slot)]
 
 
-def halo_kernel(halo_ref, first_ref, b_ref, *rest):
-    outs = rest[:4]
-    x_scr, v_scr, m_scr = rest[4:]
+def halo_kernel(halo_ref, first_ref, c_ref, *rest):
+    local = rest[:5]
+    outs = rest[5:13]
+    b_scr, x_scr, v_scr, m_scr = rest[13:]
+    split_taps(c_ref, b_scr)
     x = jnp.concatenate([halo_ref[...].reshape(HALO * R, N), first_ref[...].reshape(HALO * R, N)], axis=0)
-    right_products(x, -HALO, HALOS, b_ref, x_scr, v_scr, m_scr)
-    for k, out in enumerate(outs):
-        for e in range(2):
-            out[e] = m_scr[target(k, e)]
+    right_products(x, -HALO, HALOS, b_scr, x_scr, v_scr, m_scr)
+    for out, slot in zip(outs, SLOTS):
+        lane = 0
+        if slot in LATE:
+            lane = LOCAL_LANES
+            out[:, :lane] = local[LATE.index(slot)][...]
+        out[:, lane:] = m_scr[target(*slot)]
 
 
 def gather_kernel(*refs):
-    for ref, slot in zip(refs, SLOTS):
-        row = pl.multiple_of(source(*slot) * R, R)
-        refs[8][pl.ds(row, R), :] = ref[...]
-
-
-def left_kernel(b_ref, r_ref, *rest):
-    received = rest[:4]
-    other_ref, result_ref, mirror_ref, x_scr, h_scr = rest[4:]
-    for k, ref in enumerate(received):
-        h_scr[pl.ds(pl.multiple_of(source(k, 0) * R, R), R), :] = ref[0]
-        h_scr[pl.ds(pl.multiple_of(source(k, 1) * R, R), R), :] = other_ref[k]
+    r_ref = refs[11]
+    local = dict(zip(EARLY + [(0, 0)], refs[:3]))
+    for ref, slot in zip(refs[3:11], SLOTS):
+        rows = pl.ds(pl.multiple_of(source(*slot) * R, R), R)
+        if slot in local:
+            r_ref[rows, :LOCAL_LANES] = local[slot][...]
+            r_ref[rows, LOCAL_LANES:] = ref[...]
+        else:
+            r_ref[rows, :] = ref[...]
+
+
+def left_kernel(c_ref, r_ref, result_ref, mirror_ref, b_scr, x_scr):
+    split_taps(c_ref, b_scr)
     block = block_of_lane(N)
     total = None
     for j in (3, 2, 1):
@@ -186,10 +203,7 @@
                 if entry not in WHERE:
                     continue
                 m, p = WHERE[entry]
-                if m < len(LOCAL):
-                    part = r_ref[:, 128 * m : 128 * (m + 1)]
-                else:
-                    part = h_scr[:, 128 * (m - len(LOCAL)) : 128 * (m - len(LOCAL) + 1)]
+                part = r_ref[:, 128 * m : 128 * (m + 1)]
                 if p != q:
                     part = pltpu.roll(part, (32 * (q - p)) % 128, 1)
                 value = part if value is None else jnp.where(block == q, part, value)
@@ -197,13 +211,15 @@
         edges = [pltpu.roll(tiles[-1], 32, 1)] + tiles + [pltpu.roll(tiles[0], 96, 1)]
         for g, part in enumerate(edges):
             high, low = split(part)
-            x_scr[:N, 128 * g : 128 * (g + 1)] = high
-            x_scr[N : 2 * N, 128 * g : 128 * (g + 1)] = low
-            x_scr[2 * N :, 128 * g : 128 * (g + 1)] = high
-        total = None
-        for s in range(3):
-            part = nn(b_ref[s], x_scr[:, 128 * (2 - s) : 128 * (2 - s + GRID)])
-            total = part if total is None else total + part
+            for s in range(3):
+                t = g - 2 + s
+                if 0 <= t < GRID:
+                    k = 3 * N * s
+                    lanes = slice(128 * t, 128 * (t + 1))
+                    x_scr[k : k + N, lanes] = high
+                    x_scr[k + N : k + 2 * N, lanes] = low
+                    x_scr[k + 2 * N : k + 3 * N, lanes] = high
+        total = nn(b_scr[...], x_scr[...])
     tiles = [total[:, 128 * g : 128 * (g + 1)] for g in range(GRID)]
     for m, entries in enumerate(RESULT):
         value = None
@@ -213,7 +229,16 @@
             g, p = place(d)
             part = tiles[g] if p == q else pltpu.roll(tiles[g], (32 * (q - p)) % 128, 1)
             value = part if value is None else jnp.where(block == q, part, value)
-        result_ref[:, 128 * m : 128 * (m + 1)] = value
+        result_ref[:, R * m : R * (m + 1), :] = value.reshape(8, R, 128)
+    g, p = place(LAST)
+    quarters = tiles[g].reshape(8, 4, 8, 128)
+    block = block_of_lane(64)
+    value = None
+    for a in range(4):
+        part = quarters[:, a].reshape(64, 128)
+        part = part if a == p else pltpu.roll(part, (32 * (a - p)) % 128, 1)
+        value = part if value is None else jnp.where(block == a, part, value)
+    result_ref[:, OUT_ROWS - 8 :, :] = value.reshape(8, 8, 128)
     for g in range(GRID):
         turned = tiles[g].T
         for q in range(4):
@@ -225,8 +250,7 @@
 def pack_kernel(result_ref, *outs):
     for k, out in enumerate(outs):
         for e in range(2):
-            row = pl.multiple_of(target(k, e) * R, R)
-            out[e] = result_ref[pl.ds(row, R), :]
+            out[e] = result_ref[target(k, e)]
 
 
 def mirror_kernel(n_ref, mirror_ref, out_ref):
@@ -235,21 +259,37 @@
 
 def join_kernel(n_ref, mirror_ref, *rest):
     received = rest[:4]
-    other_ref, out_ref, r_scr = rest[4:]
+    other_ref, out_ref, r_scr, o_scr, sems = rest[4:]
+    copies = [pltpu.make_async_copy(mirror_ref, out_ref.at[pl.ds(17, 15)], sems.at[17])]
+    copies[0].start()
     for k, ref in enumerate(received):
         r_scr[source(k, 0)] = ref[0]
         r_scr[source(k, 1)] = other_ref[k]
+    halves = (slice(0, 128), slice(128, 256))
+
+    def send_out(d):
+        copies.append(pltpu.make_async_copy(o_scr.at[d], out_ref.at[d], sems.at[d]))
+        copies[-1].start()
+
     for m, entries in enumerate(RESULT):
-        for h in range(2):
-            lanes = slice(128 * h, 128 * (h + 1))
-            parts = [r_scr[4 * h + b, :, 128 * m : 128 * (m + 1)] for b in range(4)]
+        for h, lanes in enumerate(halves):
+            parts = [r_scr[4 * h + b, R * m : R * (m + 1)] for b in range(4)]
             for d, part in zip(entries, exchange_blocks(parts)):
-                if d is not None:
-                    out_ref[d, :, lanes] = n_ref[d, :, lanes] + part
-    out_ref[17:] = mirror_ref[...]
+                o_scr[d, :, lanes] = n_ref[d, :, lanes] + part
+        for d in entries:
+            send_out(d)
+    for h, lanes in enumerate(halves):
+        parts = [r_scr[4 * h + b, OUT_ROWS - 8 :] for b in range(4)]
+        for a, part in enumerate(exchange_blocks(parts)):
+            rows = slice(8 * a, 8 * (a + 1))
+            o_scr[LAST, rows, lanes] = n_ref[LAST, rows, lanes] + part
+    send_out(LAST)
+    for copy in copies:
+        copy.wait()
 
 
 PARAMS = pltpu.CompilerParams(vmem_limit_bytes=24 * 1024 * 1024)
+HBM = pl.BlockSpec(memory_space=pl.ANY)
 SMEM = pl.BlockSpec(memory_space=pltpu.SMEM)
 VMEM = pl.BlockSpec(memory_space=pltpu.VMEM)
 
@@ -265,6 +305,7 @@
 
 def right_scratch(offsets):
     return [
+        pltpu.VMEM((N, 9 * N), bf16),
         pltpu.VMEM((offsets * R, 3 * N), bf16),
         pltpu.VMEM((3, (offsets - 2) * R, N), f32),
     ]
@@ -277,56 +318,69 @@
 
 
 def body(noise_cov, couplings, shifts):
-    *local, edge, first, taps_split = pl.pallas_call(
+    edge, own, taps = pl.pallas_call(
+        taps_kernel,
+        out_shape=[
+            jax.ShapeDtypeStruct((HALO, R, N), f32),
+            jax.ShapeDtypeStruct((23, R, N), f32),
+            jax.ShapeDtypeStruct((3, N, N), f32),
+        ],
+        in_specs=[SMEM, VMEM, VMEM],
+        out_specs=[VMEM] * 3,
+        compiler_params=PARAMS,
+        name="taps",
+    )(shifts, noise_cov, couplings)
+    halo = lax.ppermute(edge, "off", [(o, (o + 1) % 16) for o in range(16)])
+    *local, first = pl.pallas_call(
         local_kernel,
-        out_shape=[jax.ShapeDtypeStruct((R, LOCAL_LANES), f32)] * 8
-        + [jax.ShapeDtypeStruct((HALO, R, N), f32)] * 2
-        + [jax.ShapeDtypeStruct((3, N, 3 * N), bf16)],
-        in_specs=[SMEM, VMEM, VMEM],
-        out_specs=[VMEM] * 11,
+        out_shape=[jax.ShapeDtypeStruct((R, LOCAL_LANES), f32)] * 8 + [jax.ShapeDtypeStruct((HALO, R, N), f32)],
+        in_specs=[VMEM, VMEM],
+        out_specs=[VMEM] * 9,
         scratch_shapes=right_scratch(23) + [pltpu.VMEM((8, R, LOCAL_LANES), f32)],
         compiler_params=PARAMS,
         cost_estimate=cost(57, 1 << 20),
         name="local_right_products",
-    )(shifts, noise_cov, couplings)
-    halo = lax.ppermute(noise_cov[R - HALO :], "off", [(o, (o + 1) % 16) for o in range(16)])
-    local = [array if slot == (0, 0) else send(array, *slot) for array, slot in zip(local, SLOTS)]
+    )(own, taps)
+    local = dict(zip(SLOTS, local))
+    early = [send(local[slot], *slot) for slot in EARLY]
     halos = pl.pallas_call(
         halo_kernel,
-        out_shape=[jax.ShapeDtypeStruct((2, R, HALO_LANES), f32)] * 4,
-        in_specs=[VMEM] * 3,
-        out_specs=[VMEM] * 4,
+        out_shape=[
+            jax.ShapeDtypeStruct((R, HALO_LANES + LOCAL_LANES * (slot in LATE)), f32) for slot in SLOTS
+        ],
+        in_specs=[VMEM] * 8,
+        out_specs=[VMEM] * 8,
         scratch_shapes=right_scratch(12) + [pltpu.VMEM((8, R, HALO_LANES), f32)],
         compiler_params=PARAMS,
         cost_estimate=cost(10, 1 << 19),
         name="halo_right_products",
-    )(halo, first, taps_split)
-    halos, other = two_level(halos)
+    )(halo, first, taps, *[local[slot] for slot in LATE])
+    halos = [array if slot == (0, 0) else send(array, *slot) for array, slot in zip(halos, SLOTS)]
     rows = pl.pallas_call(
         gather_kernel,
-        out_shape=jax.ShapeDtypeStruct((N, LOCAL_LANES), f32),
-        in_specs=[VMEM] * 8,
+        out_shape=jax.ShapeDtypeStruct((N, LOCAL_LANES + HALO_LANES), f32),
+        in_specs=[VMEM] * 11,
         out_specs=VMEM,
         compiler_params=PARAMS,
-        cost_estimate=cost(300, 1 << 20),
+        cost_estimate=cost(10, 1 << 20),
         name="gather_rows",
-    )(*local)
+    )(*early, local[0, 0], *halos)
     result, mirror = pl.pallas_call(
         left_kernel,
-        out_shape=[jax.ShapeDtypeStruct((N, OUT_LANES), f32), jax.ShapeDtypeStruct((15, R, N), f32)],
-        in_specs=[VMEM] * 7,
+        out_shape=[jax.ShapeDtypeStruct((8, OUT_ROWS, 128), f32), jax.ShapeDtypeStruct((15, R, N), f32)],
+        in_specs=[VMEM] * 2,
         out_specs=[VMEM] * 2,
         scratch_shapes=[
-            pltpu.VMEM((3 * N, 128 * (GRID + 2)), bf16),
-            pltpu.VMEM((N, HALO_LANES), f32),
+            pltpu.VMEM((N, 9 * N), bf16),
+            pltpu.VMEM((9 * N, 128 * GRID), bf16),
         ],
         compiler_params=PARAMS,
         cost_estimate=cost(72, 1 << 21),
         name="left_products",
-    )(taps_split, rows, *halos, other)
+    )(taps, rows)
     rows = pl.pallas_call(
         pack_kernel,
-        out_shape=[jax.ShapeDtypeStruct((2, R, OUT_LANES), f32)] * 4,
+        out_shape=[jax.ShapeDtypeStruct((2, OUT_ROWS, 128), f32)] * 4,
         in_specs=[VMEM],
         out_specs=[VMEM] * 4,
         compiler_params=PARAMS,
@@ -348,8 +402,12 @@
         join_kernel,
         out_shape=jax.ShapeDtypeStruct((R, R, N), f32),
         in_specs=[VMEM] * 7,
-        out_specs=VMEM,
-        scratch_shapes=[pltpu.VMEM((8, R, OUT_LANES), f32)],
+        out_specs=HBM,
+        scratch_shapes=[
+            pltpu.VMEM((8, OUT_ROWS, 128), f32),
+            pltpu.VMEM((17, R, N), f32),
+            pltpu.SemaphoreType.DMA((18,)),
+        ],
         compiler_params=PARAMS,
         name="join",
     )(noise_cov, mirror, *rows, other)

time: 66.2 us -> 61.1 us (0.923)
  waiting for transfers between devices: 18.6 us -> 14.2 us
  starting transfers between devices: 28.4 us -> 29.7 us
  Pallas kernels: 14.9 us -> 13.8 us
  local copies, waits for them, and re-layouts: 4 us -> 3.04 us
    ppermute x15 -> x13, waiting for transfers between devices: 18.6 us -> 13 us  [send(): return lax.ppermute(array, 'col', pairs)]
    ppermute x15 -> x13, starting transfers between devices: 22.4 us -> 23.8 us  [send(): return lax.ppermute(array, 'col', pairs)]
    pallas_call x1, Pallas kernels: 5.63 us -> 4.35 us  [body(): pl.pallas_call(local_kernel, out_shape=[jax.ShapeDtypeStruct((R, LOCAL_LA...]
    ppermute x1, waiting for transfers between devices: 0.01 us -> 1.16 us  [body(): mirror = lax.ppermute(mirror, 'off', [(o, 15 - o) for o in range(16)])]
    slice x1 -> x0, local copies, waits for them, and re-layouts: 0.94 us -> none  [body(): noise_cov[R - HALO:]]
    pallas_call x3 -> x4, Pallas kernels: 7.31 us -> 7.76 us  [the longest x1 4.72 us: body(): pl.pallas_call(left_kernel, out_shape=[jax.ShapeDtypeStruct((8, OUT_ROWS,...]
  transfers between devices with their start and end apart: 17 -> 15, of which waited for: 8 -> 6; matrix products, arithmetic and copies ran while one was open for 0% -> 0% of each run, Pallas kernels for 12% -> 11%
where the time goes in v1:
time: 61.1 us; the launch traced here: 60.9 us
  starting transfers between devices  29.7 us (49%)
  waiting for transfers between devices  14.2 us (23%)
  Pallas kernels  13.8 us (23%)
  local copies, waits for them, and re-layouts  3.04 us (5%)
    ppermute x13, starting transfers between devices, send(): return lax.ppermute(array, 'col', pairs)  23.8 us
    ppermute x13, waiting for transfers between devices, send(): return lax.ppermute(array, 'col', pairs)  13 us
    pallas_call x1, Pallas kernels, body(): pl.pallas_call(left_kernel, out_shape=[jax.ShapeDtypeStruct((8, OUT_ROWS,...  4.72 us
    pallas_call x1, Pallas kernels, body(): pl.pallas_call(local_kernel, out_shape=[jax.ShapeDtypeStruct((R, LOCAL_LA...  4.35 us
    ppermute x1, starting transfers between devices, body(): mirror = lax.ppermute(mirror, 'off', [(o, 15 - o) for o in range(16)])  3.73 us
    unnamed x8, local copies, waits for them, and re-layouts  3.02 us
    pallas_call x1, Pallas kernels, body(): pl.pallas_call(halo_kernel, out_shape=[jax.ShapeDtypeStruct((R, HALO_LANE...  2.27 us
    ppermute x1, starting transfers between devices, body(): halo = lax.ppermute(edge, 'off', [(o, (o + 1) % 16) for o in range(16)])  2.19 us
  transfers between devices with their start and end apart: 15, of which 6 were waited for; matrix products, arithmetic and copies ran while one was open for 0% of the time, Pallas kernels for 11%

profile of v1, /device:TPU:1, one launch (start us, length us, event | category | flops | bytes accessed | tf_op | source)
XLA Modules:
  0.0 60.9 jit_solution(11188771198049845025)
XLA Ops:
  0.0 1.2 %copy-done = f32[32,32,256]{2,1,0:T(8,128)S(1)} copy-done((f32[32,32,256]{2,1,0:T(8,128)S(1)}, f32[32,32,256]{2,1,0:T(8,128)}, u32[]{:S(2)}) %copy-start) | copy-done | bytes 1048600
  1.2 1.1 %copy-done.2 = f32[3,256,256]{2,1,0:T(8,128)S(1)} copy-done((f32[3,256,256]{2,1,0:T(8,128)S(1)}, f32[3,256,256]{2,1,0:T(8,128)}, u32[]{:S(2)}) %copy-start.2) | copy-done | bytes 786456
  2.4 0.7 %copy-done.3 = s32[3]{0:T(128)S(1)} copy-done((s32[3]{0:T(128)S(1)}, s32[3]{0:T(128)}, u32[]{:S(2)}) %copy-start.3) | copy-done | bytes 36
  3.0 0.7 %taps.1 = (f32[6,32,256]{2,1,0:T(8,128)S(1)}, f32[23,32,256]{2,1,0:T(8,128)S(1)}, f32[3,256,256]{2,1,0:T(8,128)S(1)}) custom-call(s32[3]{0:T(128)S(1)} %copy-done.3, f32[32,32,256]{2,1,0:T(8,128)S(1)} %copy-done, f32[3,256,256]{2,1,0:T(8,128)S(1)} %copy-done.2), custom_call_target="tpu_custom_call" | custom-call | tf_op jit(solution)/shard_map/taps/pallas_call | solution.py:321
  3.8 2.2 %collective-permute-start.2 = (f32[6,32,256]{2,1,0:T(8,128)S(1)}, f32[6,32,256]{2,1,0:T(8,128)S(1)}, u32[]{:S(2)}, u32[]{:S(2)}) collective-permute-start(f32[6,32,256]{2,1,0:T(8,128)S(1)} %get-tuple-element.36), channel_id=1, source_target_pairs={{0,8},{8,16},{16,24},{24,32},{32,40},{40,48},{48,56},{56,64},{64,7... | collective-permute-start | bytes 589832 | tf_op jit(solution)/shard_map/ppermute | solution.py:333
  5.9 4.4 %local_right_products.1 = (f32[32,1664]{1,0:T(8,128)S(1)}, f32[32,1664]{1,0:T(8,128)S(1)}, f32[32,1664]{1,0:T(8,128)S(1)}, f32[32,1664]{1,0:T(8,128)S(1)}, f32[3...) custom-call(f32[23,32,256]{2,1,0:T(8,128)S(1)} %get-tuple-element.32, ...), custom_call_target="tpu_custom_call" | custom-call | flops 2151677952 | bytes 4194304 | tf_op jit(solution)/shard_map/local_right_products/pallas_call | solution.py:334
  10.3 3.7 %collective-permute-start = (f32[32,1664]{1,0:T(8,128)S(1)}, f32[32,1664]{1,0:T(8,128)S(1)}, u32[]{:S(2)}, u32[]{:S(2)}) collective-permute-start(f32[32,1664]{1,0:T(8,128)S(1)} %get-tuple-element.33), channel_id=1, source_target_pairs={{0,4},{1,5},{2,6},{3,7},{4,0},{5,1},{6,2},{7,3},{8,12},{9,13},{10,... | collective-permute-start | bytes 638984 | tf_op jit(solution)/shard_map/ppermute | solution.py:299
  14.0 0.9 %collective-permute-start.1 = (f32[32,1664]{1,0:T(8,128)S(1)}, f32[32,1664]{1,0:T(8,128)S(1)}, u32[]{:S(2)}, u32[]{:S(2)}) collective-permute-start(f32[32,1664]{1,0:T(8,128)S(1)} %get-tuple-element.34), channel_id=1, source_target_pairs={{0,5},{1,4},{2,7},{3,6},{4,1},{5,0},{6,3},{7,2},{8,13},{9,12},{10,... | collective-permute-start | bytes 638984 | tf_op jit(solution)/shard_map/ppermute | solution.py:299
  14.9 0.0 collective-permute-done.2.halo_ref
  14.9 2.3 %halo_right_products.1 = (f32[32,384]{1,0:T(8,128)S(1)}, f32[32,384]{1,0:T(8,128)S(1)}, f32[32,2048]{1,0:T(8,128)S(1)}, f32[32,2048]{1,0:T(8,128)S(1)}, f32[32,2...) custom-call(f32[6,32,256]{2,1,0:T(8,128)S(1)} %collective-permute-done.2.halo_ref, ...), custom_call_target="tpu_custom_call" | custom-call | flops 377487360 | bytes 2097152 | tf_op jit(solution)/shard_map/halo_right_products/pallas_call | solution.py:346
  17.2 3.2 %collective-permute-start.3 = (f32[32,384]{1,0:T(8,128)S(1)}, f32[32,384]{1,0:T(8,128)S(1)}, u32[]{:S(2)}, u32[]{:S(2)}) collective-permute-start(f32[32,384]{1,0:T(8,128)S(1)} %get-tuple-element.43), channel_id=1, source_target_pairs={{0,4},{1,5},{2,6},{3,7},{4,0},{5,1},{6,2},{7,3},{8,12},{9,13},{10,... | collective-permute-start | bytes 147464 | tf_op jit(solution)/shard_map/ppermute | solution.py:299
  20.4 0.9 %collective-permute-start.4 = (f32[32,384]{1,0:T(8,128)S(1)}, f32[32,384]{1,0:T(8,128)S(1)}, u32[]{:S(2)}, u32[]{:S(2)}) collective-permute-start(f32[32,384]{1,0:T(8,128)S(1)} %get-tuple-element.44), channel_id=1, source_target_pairs={{0,5},{1,4},{2,7},{3,6},{4,1},{5,0},{6,3},{7,2},{8,13},{9,12},{10,... | collective-permute-start | bytes 147464 | tf_op jit(solution)/shard_map/ppermute | solution.py:299
  21.4 1.2 %collective-permute-start.5 = (f32[32,2048]{1,0:T(8,128)S(1)}, f32[32,2048]{1,0:T(8,128)S(1)}, u32[]{:S(2)}, u32[]{:S(2)}) collective-permute-start(f32[32,2048]{1,0:T(8,128)S(1)} %get-tuple-element.45), channel_id=1, source_target_pairs={{0,2},{1,3},{2,4},{3,5},{4,6},{5,7},{6,0},{7,1},{8,10},{9,11},{10,... | collective-permute-start | bytes 786440 | tf_op jit(solution)/shard_map/ppermute | solution.py:299
  22.6 0.0 collective-permute-done.refs_0_
  22.6 2.1 %collective-permute-start.6 = (f32[32,2048]{1,0:T(8,128)S(1)}, f32[32,2048]{1,0:T(8,128)S(1)}, u32[]{:S(2)}, u32[]{:S(2)}) collective-permute-start(f32[32,2048]{1,0:T(8,128)S(1)} %get-tuple-element.46), channel_id=1, source_target_pairs={{0,6},{1,7},{2,0},{3,1},{4,2},{5,3},{6,4},{7,5},{8,14},{9,15},{10,... | collective-permute-start | bytes 786440 | tf_op jit(solution)/shard_map/ppermute | solution.py:299
  24.7 1.4 %collective-permute-start.7 = (f32[32,2048]{1,0:T(8,128)S(1)}, f32[32,2048]{1,0:T(8,128)S(1)}, u32[]{:S(2)}, u32[]{:S(2)}) collective-permute-start(f32[32,2048]{1,0:T(8,128)S(1)} %get-tuple-element.47), channel_id=1, source_target_pairs={{0,3},{1,2},{2,5},{3,4},{4,7},{5,6},{6,1},{7,0},{8,11},{9,10},{10,... | collective-permute-start | bytes 786440 | tf_op jit(solution)/shard_map/ppermute | solution.py:299
  26.1 4.2 %collective-permute-start.8 = (f32[32,2048]{1,0:T(8,128)S(1)}, f32[32,2048]{1,0:T(8,128)S(1)}, u32[]{:S(2)}, u32[]{:S(2)}) collective-permute-start(f32[32,2048]{1,0:T(8,128)S(1)} %get-tuple-element.48), channel_id=1, source_target_pairs={{0,7},{1,6},{2,1},{3,0},{4,3},{5,2},{6,5},{7,4},{8,15},{9,14},{10,... | collective-permute-start | bytes 786440 | tf_op jit(solution)/shard_map/ppermute | solution.py:299
  30.3 1.8 %collective-permute-done.5.refs_5_ = f32[32,2048]{1,0:T(8,128)S(1)} collective-permute-done((f32[32,2048]{1,0:T(8,128)S(1)}, f32[32,2048]{1,0:T(8,128)S(1)}, u32[]{:S(2)}, u32[]{:S(2)}) %collective-permute-start.5) | collective-permute-done | bytes 262176 | tf_op jit(solution)/shard_map/ppermute | solution.py:299
  32.1 5.6 %collective-permute-done.7.refs_7_ = f32[32,2048]{1,0:T(8,128)S(1)} collective-permute-done((f32[32,2048]{1,0:T(8,128)S(1)}, f32[32,2048]{1,0:T(8,128)S(1)}, u32[]{:S(2)}, u32[]{:S(2)}) %collective-permute-start.7) | collective-permute-done | bytes 262176 | tf_op jit(solution)/shard_map/ppermute | solution.py:299
  37.7 0.4 collective-permute-done.8.refs_8_
  38.1 0.2 gather_rows.1.r_ref
  38.3 4.7 %left_products.1 = (f32[8,136,128]{2,1,0:T(8,128)S(1)}, f32[15,32,256]{2,1,0:T(8,128)S(1)}) custom-call(f32[3,256,256]{2,1,0:T(8,128)S(1)} %get-tuple-element.31.c_ref, f32[256,2048]{1,0:T(8,128)S(1)} %gather_rows.1.r_ref), custom_call_target="tpu_custom_call" | custom-call | flops 2717908992 | bytes 8388608 | tf_op jit(solution)/shard_map/left_products/pallas_call | solution.py:368
  43.0 3.7 %collective-permute-start.10 = (f32[15,32,256]{2,1,0:T(8,128)S(1)}, f32[15,32,256]{2,1,0:T(8,128)S(1)}, u32[]{:S(2)}, u32[]{:S(2)}) collective-permute-start(f32[15,32,256]{2,1,0:T(8,128)S(1)} %get-tuple-element.51), channel_id=1, source_target_pairs={{0,120},{8,112},{16,104},{24,96},{32,88},{40,80},{48,72},{56,64},{... | collective-permute-start | bytes 1474568 | tf_op jit(solution)/shard_map/ppermute | solution.py:390
  46.8 0.9 %collective-permute-start.11 = (f32[2,136,128]{2,1,0:T(8,128)S(1)}, f32[2,136,128]{2,1,0:T(8,128)S(1)}, u32[]{:S(2)}, u32[]{:S(2)}) collective-permute-start(f32[2,136,128]{2,1,0:T(8,128)S(1)} %get-tuple-element.54), channel_id=1, source_target_pairs={{0,2},{1,3},{2,4},{3,5},{4,6},{5,7},{6,0},{7,1},{8,10},{9,11},{10,... | collective-permute-start | bytes 417800 | tf_op jit(solution)/shard_map/ppermute | solution.py:299
  47.7 2.8 %collective-permute-start.12 = (f32[2,136,128]{2,1,0:T(8,128)S(1)}, f32[2,136,128]{2,1,0:T(8,128)S(1)}, u32[]{:S(2)}, u32[]{:S(2)}) collective-permute-start(f32[2,136,128]{2,1,0:T(8,128)S(1)} %get-tuple-element.55), channel_id=1, source_target_pairs={{0,4},{1,5},{2,6},{3,7},{4,0},{5,1},{6,2},{7,3},{8,12},{9,13},{10,... | collective-permute-start | bytes 417800 | tf_op jit(solution)/shard_map/ppermute | solution.py:299
  50.4 0.9 %collective-permute-start.13 = (f32[2,136,128]{2,1,0:T(8,128)S(1)}, f32[2,136,128]{2,1,0:T(8,128)S(1)}, u32[]{:S(2)}, u32[]{:S(2)}) collective-permute-start(f32[2,136,128]{2,1,0:T(8,128)S(1)} %get-tuple-element.56), channel_id=1, source_target_pairs={{0,6},{1,7},{2,0},{3,1},{4,2},{5,3},{6,4},{7,5},{8,14},{9,15},{10,... | collective-permute-start | bytes 417800 | tf_op jit(solution)/shard_map/ppermute | solution.py:299
  51.4 1.8 %collective-permute-done.11.rest_1_ = f32[2,136,128]{2,1,0:T(8,128)S(1)} collective-permute-done((f32[2,136,128]{2,1,0:T(8,128)S(1)}, f32[2,136,128]{2,1,0:T(8,128)S(1)}, u32[]{:S(2)}, u32[]{:S(2)}) %collective-permute-start.11) | collective-permute-done | bytes 139296 | tf_op jit(solution)/shard_map/ppermute | solution.py:299
  53.2 3.4 %collective-permute-done.12.rest_2_ = f32[2,136,128]{2,1,0:T(8,128)S(1)} collective-permute-done((f32[2,136,128]{2,1,0:T(8,128)S(1)}, f32[2,136,128]{2,1,0:T(8,128)S(1)}, u32[]{:S(2)}, u32[]{:S(2)}) %collective-permute-start.12) | collective-permute-done | bytes 139296 | tf_op jit(solution)/shard_map/ppermute | solution.py:299
  56.6 1.6 %collective-permute-start.14 = (f32[4,136,128]{2,1,0:T(8,128)S(1)}, f32[4,136,128]{2,1,0:T(8,128)S(1)}, u32[]{:S(2)}, u32[]{:S(2)}) collective-permute-start(f32[4,136,128]{2,1,0:T(8,128)S(1)} %pad_maximum_fusion), channel_id=1, source_target_pairs={{0,1},{1,0},{2,3},{3,2},{4,5},{5,4},{6,7},{7,6},{8,9},{9,8},{10,11... | collective-permute-start | bytes 835592 | tf_op jit(solution)/shard_map/ppermute | solution.py:299
  58.2 1.2 %collective-permute-done.10.mirror_ref = f32[15,32,256]{2,1,0:T(8,128)S(1)} collective-permute-done((f32[15,32,256]{2,1,0:T(8,128)S(1)}, f32[15,32,256]{2,1,0:T(8,128)S(1)}, u32[]{:S(2)}, u32[]{:S(2)}) %collective-permute-start.10) | collective-permute-done | bytes 491552 | tf_op jit(solution)/shard_map/ppermute | solution.py:390
  59.4 0.1 join_mirror.1.mirror_ref
  59.4 1.5 %join.1 = f32[32,32,256]{2,1,0:T(8,128)} custom-call(f32[32,32,256]{2,1,0:T(8,128)S(1)} %copy-done.1, f32[15,32,256]{2,1,0:T(8,128)S(1)} %join_mirror.1.mirror_ref, f32[2,136,128]{2,1,0:T(8,128)S(1)} %get-tuple-element.53.rest_0_, f32[2,136,128]{2,1,0:T(8,128)S(1)} %collective-permute-done.11.rest_1_, f32[2,136,128]{2,1,0:T(8,128)S(1)} %collective-permute-done.12.rest_2_, ...), custom_call_target="tpu_custom_call" | custom-call | tf_op jit(solution)/shard_map/join/pallas_call | solution.py:401
  (19 shorter events, 0.1 us)
Async XLA Ops:
  0.0 1.2 %copy-start = (f32[32,32,256]{2,1,0:T(8,128)S(1)}, f32[32,32,256]{2,1,0:T(8,128)}, u32[]{:S(2)}) copy-start(f32[32,32,256]{2,1,0:T(8,128)} %n_ref.5) | copy-start | bytes 3145732
  1.2 1.1 %copy-start.2 = (f32[3,256,256]{2,1,0:T(8,128)S(1)}, f32[3,256,256]{2,1,0:T(8,128)}, u32[]{:S(2)}) copy-start(f32[3,256,256]{2,1,0:T(8,128)} %c_ref.1) | copy-start | bytes 2359300
  2.4 0.7 %copy-start.3 = (s32[3]{0:T(128)S(1)}, s32[3]{0:T(128)}, u32[]{:S(2)}) copy-start(s32[3]{0:T(128)} %shift_ref.1) | copy-start | bytes 40
  3.8 11.2 %collective-permute-start.2 = (f32[6,32,256]{2,1,0:T(8,128)S(1)}, f32[6,32,256]{2,1,0:T(8,128)S(1)}, u32[]{:S(2)}, u32[]{:S(2)}) collective-permute-start(f32[6,32,256]{2,1,0:T(8,128)S(1)} %get-tuple-element.36), channel_id=1, source_target_pairs={{0,8},{8,16},{16,24},{24,32},{32,40},{40,48},{48,56},{56,64},{64,7... | collective-permute-start | bytes 589832 | tf_op jit(solution)/shard_map/ppermute | solution.py:333
  10.3 12.3 %collective-permute-start = (f32[32,1664]{1,0:T(8,128)S(1)}, f32[32,1664]{1,0:T(8,128)S(1)}, u32[]{:S(2)}, u32[]{:S(2)}) collective-permute-start(f32[32,1664]{1,0:T(8,128)S(1)} %get-tuple-element.33), channel_id=1, source_target_pairs={{0,4},{1,5},{2,6},{3,7},{4,0},{5,1},{6,2},{7,3},{8,12},{9,13},{10,... | collective-permute-start | bytes 638984 | tf_op jit(solution)/shard_map/ppermute | solution.py:299
  14.0 10.7 %collective-permute-start.1 = (f32[32,1664]{1,0:T(8,128)S(1)}, f32[32,1664]{1,0:T(8,128)S(1)}, u32[]{:S(2)}, u32[]{:S(2)}) collective-permute-start(f32[32,1664]{1,0:T(8,128)S(1)} %get-tuple-element.34), channel_id=1, source_target_pairs={{0,5},{1,4},{2,7},{3,6},{4,1},{5,0},{6,3},{7,2},{8,13},{9,12},{10,... | collective-permute-start | bytes 638984 | tf_op jit(solution)/shard_map/ppermute | solution.py:299
  17.2 8.9 %collective-permute-start.3 = (f32[32,384]{1,0:T(8,128)S(1)}, f32[32,384]{1,0:T(8,128)S(1)}, u32[]{:S(2)}, u32[]{:S(2)}) collective-permute-start(f32[32,384]{1,0:T(8,128)S(1)} %get-tuple-element.43), channel_id=1, source_target_pairs={{0,4},{1,5},{2,6},{3,7},{4,0},{5,1},{6,2},{7,3},{8,12},{9,13},{10,... | collective-permute-start | bytes 147464 | tf_op jit(solution)/shard_map/ppermute | solution.py:299
  20.4 9.9 %collective-permute-start.4 = (f32[32,384]{1,0:T(8,128)S(1)}, f32[32,384]{1,0:T(8,128)S(1)}, u32[]{:S(2)}, u32[]{:S(2)}) collective-permute-start(f32[32,384]{1,0:T(8,128)S(1)} %get-tuple-element.44), channel_id=1, source_target_pairs={{0,5},{1,4},{2,7},{3,6},{4,1},{5,0},{6,3},{7,2},{8,13},{9,12},{10,... | collective-permute-start | bytes 147464 | tf_op jit(solution)/shard_map/ppermute | solution.py:299
  21.4 10.7 %collective-permute-start.5 = (f32[32,2048]{1,0:T(8,128)S(1)}, f32[32,2048]{1,0:T(8,128)S(1)}, u32[]{:S(2)}, u32[]{:S(2)}) collective-permute-start(f32[32,2048]{1,0:T(8,128)S(1)} %get-tuple-element.45), channel_id=1, source_target_pairs={{0,2},{1,3},{2,4},{3,5},{4,6},{5,7},{6,0},{7,1},{8,10},{9,11},{10,... | collective-permute-start | bytes 786440 | tf_op jit(solution)/shard_map/ppermute | solution.py:299
  22.6 9.5 %collective-permute-start.6 = (f32[32,2048]{1,0:T(8,128)S(1)}, f32[32,2048]{1,0:T(8,128)S(1)}, u32[]{:S(2)}, u32[]{:S(2)}) collective-permute-start(f32[32,2048]{1,0:T(8,128)S(1)} %get-tuple-element.46), channel_id=1, source_target_pairs={{0,6},{1,7},{2,0},{3,1},{4,2},{5,3},{6,4},{7,5},{8,14},{9,15},{10,... | collective-permute-start | bytes 786440 | tf_op jit(solution)/shard_map/ppermute | solution.py:299
  24.7 13.0 %collective-permute-start.7 = (f32[32,2048]{1,0:T(8,128)S(1)}, f32[32,2048]{1,0:T(8,128)S(1)}, u32[]{:S(2)}, u32[]{:S(2)}) collective-permute-start(f32[32,2048]{1,0:T(8,128)S(1)} %get-tuple-element.47), channel_id=1, source_target_pairs={{0,3},{1,2},{2,5},{3,4},{4,7},{5,6},{6,1},{7,0},{8,11},{9,10},{10,... | collective-permute-start | bytes 786440 | tf_op jit(solution)/shard_map/ppermute | solution.py:299
  26.1 12.0 %collective-permute-start.8 = (f32[32,2048]{1,0:T(8,128)S(1)}, f32[32,2048]{1,0:T(8,128)S(1)}, u32[]{:S(2)}, u32[]{:S(2)}) collective-permute-start(f32[32,2048]{1,0:T(8,128)S(1)} %get-tuple-element.48), channel_id=1, source_target_pairs={{0,7},{1,6},{2,1},{3,0},{4,3},{5,2},{6,5},{7,4},{8,15},{9,14},{10,... | collective-permute-start | bytes 786440 | tf_op jit(solution)/shard_map/ppermute | solution.py:299
  30.3 7.9 %collective-permute-start.9 = (f32[32,2048]{1,0:T(8,128)S(1)}, f32[32,2048]{1,0:T(8,128)S(1)}, u32[]{:S(2)}, u32[]{:S(2)}) collective-permute-start(f32[32,2048]{1,0:T(8,128)S(1)} %get-tuple-element.49), channel_id=1, source_target_pairs={{0,1},{1,0},{2,3},{3,2},{4,5},{5,4},{6,7},{7,6},{8,9},{9,8},{10,11... | collective-permute-start | bytes 786440 | tf_op jit(solution)/shard_map/ppermute | solution.py:299
  43.0 16.3 %collective-permute-start.10 = (f32[15,32,256]{2,1,0:T(8,128)S(1)}, f32[15,32,256]{2,1,0:T(8,128)S(1)}, u32[]{:S(2)}, u32[]{:S(2)}) collective-permute-start(f32[15,32,256]{2,1,0:T(8,128)S(1)} %get-tuple-element.51), channel_id=1, source_target_pairs={{0,120},{8,112},{16,104},{24,96},{32,88},{40,80},{48,72},{56,64},{... | collective-permute-start | bytes 1474568 | tf_op jit(solution)/shard_map/ppermute | solution.py:390
  46.8 12.6 %copy-start.1 = (f32[32,32,256]{2,1,0:T(8,128)S(1)}, f32[32,32,256]{2,1,0:T(8,128)}, u32[]{:S(2)}) copy-start(f32[32,32,256]{2,1,0:T(8,128)} %n_ref.5) | copy-start | bytes 3145732
  46.8 6.4 %collective-permute-start.11 = (f32[2,136,128]{2,1,0:T(8,128)S(1)}, f32[2,136,128]{2,1,0:T(8,128)S(1)}, u32[]{:S(2)}, u32[]{:S(2)}) collective-permute-start(f32[2,136,128]{2,1,0:T(8,128)S(1)} %get-tuple-element.54), channel_id=1, source_target_pairs={{0,2},{1,3},{2,4},{3,5},{4,6},{5,7},{6,0},{7,1},{8,10},{9,11},{10,... | collective-permute-start | bytes 417800 | tf_op jit(solution)/shard_map/ppermute | solution.py:299
  47.7 8.9 %collective-permute-start.12 = (f32[2,136,128]{2,1,0:T(8,128)S(1)}, f32[2,136,128]{2,1,0:T(8,128)S(1)}, u32[]{:S(2)}, u32[]{:S(2)}) collective-permute-start(f32[2,136,128]{2,1,0:T(8,128)S(1)} %get-tuple-element.55), channel_id=1, source_target_pairs={{0,4},{1,5},{2,6},{3,7},{4,0},{5,1},{6,2},{7,3},{8,12},{9,13},{10,... | collective-permute-start | bytes 417800 | tf_op jit(solution)/shard_map/ppermute | solution.py:299
  50.4 6.1 %collective-permute-start.13 = (f32[2,136,128]{2,1,0:T(8,128)S(1)}, f32[2,136,128]{2,1,0:T(8,128)S(1)}, u32[]{:S(2)}, u32[]{:S(2)}) collective-permute-start(f32[2,136,128]{2,1,0:T(8,128)S(1)} %get-tuple-element.56), channel_id=1, source_target_pairs={{0,6},{1,7},{2,0},{3,1},{4,2},{5,3},{6,4},{7,5},{8,14},{9,15},{10,... | collective-permute-start | bytes 417800 | tf_op jit(solution)/shard_map/ppermute | solution.py:299
  56.6 2.8 %collective-permute-start.14 = (f32[4,136,128]{2,1,0:T(8,128)S(1)}, f32[4,136,128]{2,1,0:T(8,128)S(1)}, u32[]{:S(2)}, u32[]{:S(2)}) collective-permute-start(f32[4,136,128]{2,1,0:T(8,128)S(1)} %pad_maximum_fusion), channel_id=1, source_target_pairs={{0,1},{1,0},{2,3},{3,2},{4,5},{5,4},{6,7},{7,6},{8,9},{9,8},{10,11... | collective-permute-start | bytes 835592 | tf_op jit(solution)/shard_map/ppermute | solution.py:299

commit v2 on v1

--- a/solution.py
+++ b/solution.py
@@ -48,12 +48,14 @@
 WHERE = {entry: (m, p) for m, tile in enumerate(LOCAL + HALOS) for p, entry in enumerate(tile) if entry}
 RESULT = [[5, 3, 9, 15], [11, 4, 10, 16], [0, 6, 12, 2], [1, 7, 13, 8]]
 LAST = 14
+DISTANCES = (0, 2, 1, 3)
 OUT_ROWS = R * len(RESULT) + 8
 LOCAL_LANES = 128 * len(LOCAL)
 HALO_LANES = 128 * len(HALOS)
 EARLY = [(2, 0), (2, 1)]
 LATE = [(1, 0), (3, 0), (1, 1), (3, 1), (0, 1)]
 SLOTS = EARLY + LATE + [(0, 0)]
+SECOND = [(1, 0), (3, 0), (2, 0), (2, 1), (1, 1), (3, 1), (0, 1), (0, 0)]
 
 
 def coordinates():
@@ -142,22 +144,22 @@
                 m_ref[4 * h + b, :, 128 * m : 128 * (m + 1)] = part
 
 
-def taps_kernel(shift_ref, n_ref, c_ref, edge_ref, own_ref, taps_ref):
+def edge_kernel(n_ref, edge_ref, own_ref):
     edge_ref[...] = n_ref[R - HALO :]
     own_ref[...] = n_ref[:23]
+
+
+def local_kernel(shift_ref, n_ref, c_ref, *rest):
+    outs = rest[:8]
+    first_ref, taps_ref, b_scr, x_scr, v_scr, m_scr = rest[8:]
+    first_ref[...] = n_ref[:HALO]
     for s in (-1, 0, 1):
         block = None
         for t in range(3):
             chosen = jnp.where(shift_ref[t] == s, f32(1), f32(0)) * c_ref[t]
             block = chosen if block is None else block + chosen
         taps_ref[s + 1] = block
-
-
-def local_kernel(n_ref, c_ref, *rest):
-    outs = rest[:8]
-    first_ref, b_scr, x_scr, v_scr, m_scr = rest[8:]
-    first_ref[...] = n_ref[:HALO]
-    split_taps(c_ref, b_scr)
+    split_taps(taps_ref, b_scr)
     right_products(n_ref[...].reshape(23 * R, N), 0, LOCAL, b_scr, x_scr, v_scr, m_scr)
     for out, slot in zip(outs, SLOTS):
         out[...] = m_scr[target(*slot)]
@@ -170,7 +172,7 @@
     split_taps(c_ref, b_scr)
     x = jnp.concatenate([halo_ref[...].reshape(HALO * R, N), first_ref[...].reshape(HALO * R, N)], axis=0)
     right_products(x, -HALO, HALOS, b_scr, x_scr, v_scr, m_scr)
-    for out, slot in zip(outs, SLOTS):
+    for out, slot in zip(outs, SECOND):
         lane = 0
         if slot in LATE:
             lane = LOCAL_LANES
@@ -181,7 +183,7 @@
 def gather_kernel(*refs):
     r_ref = refs[11]
     local = dict(zip(EARLY + [(0, 0)], refs[:3]))
-    for ref, slot in zip(refs[3:11], SLOTS):
+    for ref, slot in zip(refs[3:11], SECOND):
         rows = pl.ds(pl.multiple_of(source(*slot) * R, R), R)
         if slot in local:
             r_ref[rows, :LOCAL_LANES] = local[slot][...]
@@ -248,7 +250,7 @@
 
 
 def pack_kernel(result_ref, *outs):
-    for k, out in enumerate(outs):
+    for k, out in zip(DISTANCES, outs):
         for e in range(2):
             out[e] = result_ref[target(k, e)]
 
@@ -262,9 +264,9 @@
     other_ref, out_ref, r_scr, o_scr, sems = rest[4:]
     copies = [pltpu.make_async_copy(mirror_ref, out_ref.at[pl.ds(17, 15)], sems.at[17])]
     copies[0].start()
-    for k, ref in enumerate(received):
+    for n, (k, ref) in enumerate(zip(DISTANCES, received)):
         r_scr[source(k, 0)] = ref[0]
-        r_scr[source(k, 1)] = other_ref[k]
+        r_scr[source(k, 1)] = other_ref[n]
     halves = (slice(0, 128), slice(128, 256))
 
     def send_out(d):
@@ -312,41 +314,37 @@
 
 
 def two_level(parts):
-    parts = [parts[0]] + [send(parts[k], k, 0) for k in (1, 3, 2)]
-    parts = [parts[0], parts[1], parts[3], parts[2]]
+    parts = [part if k == 0 else send(part, k, 0) for k, part in zip(DISTANCES, parts)]
     return parts, send(jnp.stack([part[1] for part in parts]), 0, 1)
 
 
 def body(noise_cov, couplings, shifts):
-    edge, own, taps = pl.pallas_call(
-        taps_kernel,
-        out_shape=[
-            jax.ShapeDtypeStruct((HALO, R, N), f32),
-            jax.ShapeDtypeStruct((23, R, N), f32),
-            jax.ShapeDtypeStruct((3, N, N), f32),
-        ],
+    edge, own = pl.pallas_call(
+        edge_kernel,
+        out_shape=[jax.ShapeDtypeStruct((HALO, R, N), f32), jax.ShapeDtypeStruct((23, R, N), f32)],
+        in_specs=[VMEM],
+        out_specs=[VMEM] * 2,
+        compiler_params=PARAMS,
+        cost_estimate=cost(200, 1 << 20),
+        name="edge",
+    )(noise_cov)
+    halo = lax.ppermute(edge, "off", [(o, (o + 1) % 16) for o in range(16)])
+    *local, first, taps = pl.pallas_call(
+        local_kernel,
+        out_shape=[jax.ShapeDtypeStruct((R, LOCAL_LANES), f32)] * 8 + [jax.ShapeDtypeStruct((HALO, R, N), f32), jax.ShapeDtypeStruct((3, N, N), f32)],
         in_specs=[SMEM, VMEM, VMEM],
-        out_specs=[VMEM] * 3,
-        compiler_params=PARAMS,
-        name="taps",
-    )(shifts, noise_cov, couplings)
-    halo = lax.ppermute(edge, "off", [(o, (o + 1) % 16) for o in range(16)])
-    *local, first = pl.pallas_call(
-        local_kernel,
-        out_shape=[jax.ShapeDtypeStruct((R, LOCAL_LANES), f32)] * 8 + [jax.ShapeDtypeStruct((HALO, R, N), f32)],
-        in_specs=[VMEM, VMEM],
-        out_specs=[VMEM] * 9,
+        out_specs=[VMEM] * 10,
         scratch_shapes=right_scratch(23) + [pltpu.VMEM((8, R, LOCAL_LANES), f32)],
         compiler_params=PARAMS,
         cost_estimate=cost(57, 1 << 20),
         name="local_right_products",
-    )(own, taps)
+    )(shifts, own, couplings)
     local = dict(zip(SLOTS, local))
     early = [send(local[slot], *slot) for slot in EARLY]
     halos = pl.pallas_call(
         halo_kernel,
         out_shape=[
-            jax.ShapeDtypeStruct((R, HALO_LANES + LOCAL_LANES * (slot in LATE)), f32) for slot in SLOTS
+            jax.ShapeDtypeStruct((R, HALO_LANES + LOCAL_LANES * (slot in LATE)), f32) for slot in SECOND
         ],
         in_specs=[VMEM] * 8,
         out_specs=[VMEM] * 8,
@@ -355,7 +353,7 @@
         cost_estimate=cost(10, 1 << 19),
         name="halo_right_products",
     )(halo, first, taps, *[local[slot] for slot in LATE])
-    halos = [array if slot == (0, 0) else send(array, *slot) for array, slot in zip(halos, SLOTS)]
+    halos = [array if slot == (0, 0) else send(array, *slot) for array, slot in zip(halos, SECOND)]
     rows = pl.pallas_call(
         gather_kernel,
         out_shape=jax.ShapeDtypeStruct((N, LOCAL_LANES + HALO_LANES), f32),

time: 61.1 us -> 59.5 us (0.974)
  local copies, waits for them, and re-layouts: 3.04 us -> 1.26 us
  starting transfers between devices: 29.7 us -> 30.6 us
    unnamed x8, local copies, waits for them, and re-layouts: 3.02 us -> 1.24 us
    ppermute x1, starting transfers between devices: 3.73 us -> 4.7 us  [body(): mirror = lax.ppermute(mirror, 'off', [(o, 15 - o) for o in range(16)])]
    pallas_call x1, Pallas kernels: 0.73 us -> 0.06 us  [body(): pl.pallas_call(edge_kernel, out_shape=[jax.ShapeDtypeStruct((HALO, R, N),...]
  transfers between devices with their start and end apart: 15 -> 15, of which waited for: 6 -> 8; matrix products, arithmetic and copies ran while one was open for 0% -> 0% of each run, Pallas kernels for 11% -> 12%
where the time goes in v2:
time: 59.5 us; the launch traced here: 59.4 us
  starting transfers between devices  30.6 us (51%)
  waiting for transfers between devices  13.8 us (23%)
  Pallas kernels  13.7 us (23%)
  local copies, waits for them, and re-layouts  1.26 us (2%)
    ppermute x13, starting transfers between devices, send(): return lax.ppermute(array, 'col', pairs)  23.7 us
    ppermute x13, waiting for transfers between devices, send(): return lax.ppermute(array, 'col', pairs)  13.1 us
    pallas_call x1, Pallas kernels, body(): pl.pallas_call(local_kernel, out_shape=[jax.ShapeDtypeStruct((R, LOCAL_LA...  4.92 us
    pallas_call x1, Pallas kernels, body(): pl.pallas_call(left_kernel, out_shape=[jax.ShapeDtypeStruct((8, OUT_ROWS,...  4.73 us
    ppermute x1, starting transfers between devices, body(): mirror = lax.ppermute(mirror, 'off', [(o, 15 - o) for o in range(16)])  4.7 us
    pallas_call x1, Pallas kernels, body(): pl.pallas_call(halo_kernel, out_shape=[jax.ShapeDtypeStruct((R, HALO_LANE...  2.27 us
    ppermute x1, starting transfers between devices, body(): halo = lax.ppermute(edge, 'off', [(o, (o + 1) % 16) for o in range(16)])  2.19 us
    pallas_call x1, Pallas kernels, body(): pl.pallas_call(join_kernel, out_shape=jax.ShapeDtypeStruct((R, R, N), f32...  1.46 us
  transfers between devices with their start and end apart: 15, of which 8 were waited for; matrix products, arithmetic and copies ran while one was open for 0% of the time, Pallas kernels for 12%

profile of v2, /device:TPU:1, one launch (start us, length us, event | category | flops | bytes accessed | tf_op | source)
XLA Modules:
  0.0 59.4 jit_solution(9797047364617640458)
XLA Ops:
  0.0 1.2 %copy-done = f32[32,32,256]{2,1,0:T(8,128)S(1)} copy-done((f32[32,32,256]{2,1,0:T(8,128)S(1)}, f32[32,32,256]{2,1,0:T(8,128)}, u32[]{:S(2)}) %copy-start) | copy-done | bytes 1048600
  1.2 0.1 edge.1
  1.3 2.2 %collective-permute-start.2 = (f32[6,32,256]{2,1,0:T(8,128)S(1)}, f32[6,32,256]{2,1,0:T(8,128)S(1)}, u32[]{:S(2)}, u32[]{:S(2)}) collective-permute-start(f32[6,32,256]{2,1,0:T(8,128)S(1)} %get-tuple-element.36), channel_id=1, source_target_pairs={{0,8},{8,16},{16,24},{24,32},{32,40},{40,48},{48,56},{56,64},{64,7... | collective-permute-start | bytes 589832 | tf_op jit(solution)/shard_map/ppermute | solution.py:331
  3.5 4.9 %local_right_products.1 = (f32[32,1664]{1,0:T(8,128)S(1)}, f32[32,1664]{1,0:T(8,128)S(1)}, f32[32,1664]{1,0:T(8,128)S(1)}, f32[32,1664]{1,0:T(8,128)S(1)}, f32[3...) custom-call(s32[3]{0:T(128)S(1)} %copy-done.3, ...), custom_call_target="tpu_custom_call" | custom-call | flops 2151677952 | bytes 4194304 | tf_op jit(solution)/shard_map/local_right_products/pallas_call | solution.py:332
  8.4 3.7 %collective-permute-start = (f32[32,1664]{1,0:T(8,128)S(1)}, f32[32,1664]{1,0:T(8,128)S(1)}, u32[]{:S(2)}, u32[]{:S(2)}) collective-permute-start(f32[32,1664]{1,0:T(8,128)S(1)} %get-tuple-element.33), channel_id=1, source_target_pairs={{0,4},{1,5},{2,6},{3,7},{4,0},{5,1},{6,2},{7,3},{8,12},{9,13},{10,... | collective-permute-start | bytes 638984 | tf_op jit(solution)/shard_map/ppermute | solution.py:301
  12.1 0.9 %collective-permute-start.1 = (f32[32,1664]{1,0:T(8,128)S(1)}, f32[32,1664]{1,0:T(8,128)S(1)}, u32[]{:S(2)}, u32[]{:S(2)}) collective-permute-start(f32[32,1664]{1,0:T(8,128)S(1)} %get-tuple-element.34), channel_id=1, source_target_pairs={{0,5},{1,4},{2,7},{3,6},{4,1},{5,0},{6,3},{7,2},{8,13},{9,12},{10,... | collective-permute-start | bytes 638984 | tf_op jit(solution)/shard_map/ppermute | solution.py:301
  13.0 0.0 collective-permute-done.2.halo_ref
  13.0 2.3 %halo_right_products.1 = (f32[32,2048]{1,0:T(8,128)S(1)}, f32[32,2048]{1,0:T(8,128)S(1)}, f32[32,384]{1,0:T(8,128)S(1)}, f32[32,384]{1,0:T(8,128)S(1)}, f32[32,2...) custom-call(f32[6,32,256]{2,1,0:T(8,128)S(1)} %collective-permute-done.2.halo_ref, ...), custom_call_target="tpu_custom_call" | custom-call | flops 377487360 | bytes 2097152 | tf_op jit(solution)/shard_map/halo_right_products/pallas_call | solution.py:344
  15.3 3.2 %collective-permute-start.5 = (f32[32,384]{1,0:T(8,128)S(1)}, f32[32,384]{1,0:T(8,128)S(1)}, u32[]{:S(2)}, u32[]{:S(2)}) collective-permute-start(f32[32,384]{1,0:T(8,128)S(1)} %get-tuple-element.45), channel_id=1, source_target_pairs={{0,4},{1,5},{2,6},{3,7},{4,0},{5,1},{6,2},{7,3},{8,12},{9,13},{10,... | collective-permute-start | bytes 147464 | tf_op jit(solution)/shard_map/ppermute | solution.py:301
  18.6 0.3 collective-permute-start.6
  18.9 1.2 %collective-permute-start.3 = (f32[32,2048]{1,0:T(8,128)S(1)}, f32[32,2048]{1,0:T(8,128)S(1)}, u32[]{:S(2)}, u32[]{:S(2)}) collective-permute-start(f32[32,2048]{1,0:T(8,128)S(1)} %get-tuple-element.43), channel_id=1, source_target_pairs={{0,2},{1,3},{2,4},{3,5},{4,6},{5,7},{6,0},{7,1},{8,10},{9,11},{10,... | collective-permute-start | bytes 786440 | tf_op jit(solution)/shard_map/ppermute | solution.py:301
  20.1 0.0 collective-permute-done.refs_0_
  20.1 2.1 %collective-permute-start.4 = (f32[32,2048]{1,0:T(8,128)S(1)}, f32[32,2048]{1,0:T(8,128)S(1)}, u32[]{:S(2)}, u32[]{:S(2)}) collective-permute-start(f32[32,2048]{1,0:T(8,128)S(1)} %get-tuple-element.44), channel_id=1, source_target_pairs={{0,6},{1,7},{2,0},{3,1},{4,2},{5,3},{6,4},{7,5},{8,14},{9,15},{10,... | collective-permute-start | bytes 786440 | tf_op jit(solution)/shard_map/ppermute | solution.py:301
  22.2 0.4 collective-permute-done.1.refs_1_
  22.6 1.6 %collective-permute-start.7 = (f32[32,2048]{1,0:T(8,128)S(1)}, f32[32,2048]{1,0:T(8,128)S(1)}, u32[]{:S(2)}, u32[]{:S(2)}) collective-permute-start(f32[32,2048]{1,0:T(8,128)S(1)} %get-tuple-element.47), channel_id=1, source_target_pairs={{0,3},{1,2},{2,5},{3,4},{4,7},{5,6},{6,1},{7,0},{8,11},{9,10},{10,... | collective-permute-start | bytes 786440 | tf_op jit(solution)/shard_map/ppermute | solution.py:301
  24.2 4.2 %collective-permute-start.8 = (f32[32,2048]{1,0:T(8,128)S(1)}, f32[32,2048]{1,0:T(8,128)S(1)}, u32[]{:S(2)}, u32[]{:S(2)}) collective-permute-start(f32[32,2048]{1,0:T(8,128)S(1)} %get-tuple-element.48), channel_id=1, source_target_pairs={{0,7},{1,6},{2,1},{3,0},{4,3},{5,2},{6,5},{7,4},{8,15},{9,14},{10,... | collective-permute-start | bytes 786440 | tf_op jit(solution)/shard_map/ppermute | solution.py:301
  28.4 1.8 %collective-permute-done.3.refs_3_ = f32[32,2048]{1,0:T(8,128)S(1)} collective-permute-done((f32[32,2048]{1,0:T(8,128)S(1)}, f32[32,2048]{1,0:T(8,128)S(1)}, u32[]{:S(2)}, u32[]{:S(2)}) %collective-permute-start.3) | collective-permute-done | bytes 262176 | tf_op jit(solution)/shard_map/ppermute | solution.py:301
  30.2 5.6 %collective-permute-done.7.refs_7_ = f32[32,2048]{1,0:T(8,128)S(1)} collective-permute-done((f32[32,2048]{1,0:T(8,128)S(1)}, f32[32,2048]{1,0:T(8,128)S(1)}, u32[]{:S(2)}, u32[]{:S(2)}) %collective-permute-start.7) | collective-permute-done | bytes 262176 | tf_op jit(solution)/shard_map/ppermute | solution.py:301
  35.8 0.4 collective-permute-done.8.refs_8_
  36.3 0.2 gather_rows.1.r_ref
  36.4 4.7 %left_products.1 = (f32[8,136,128]{2,1,0:T(8,128)S(1)}, f32[15,32,256]{2,1,0:T(8,128)S(1)}) custom-call(f32[3,256,256]{2,1,0:T(8,128)S(1)} %get-tuple-element.32.c_ref, f32[256,2048]{1,0:T(8,128)S(1)} %gather_rows.1.r_ref), custom_call_target="tpu_custom_call" | custom-call | flops 2717908992 | bytes 8388608 | tf_op jit(solution)/shard_map/left_products/pallas_call | solution.py:366
  41.2 4.7 %collective-permute-start.10 = (f32[15,32,256]{2,1,0:T(8,128)S(1)}, f32[15,32,256]{2,1,0:T(8,128)S(1)}, u32[]{:S(2)}, u32[]{:S(2)}) collective-permute-start(f32[15,32,256]{2,1,0:T(8,128)S(1)} %get-tuple-element.51), channel_id=1, source_target_pairs={{0,120},{8,112},{16,104},{24,96},{32,88},{40,80},{48,72},{56,64},{... | collective-permute-start | bytes 1474568 | tf_op jit(solution)/shard_map/ppermute | solution.py:388
  45.9 2.5 %collective-permute-start.11 = (f32[2,136,128]{2,1,0:T(8,128)S(1)}, f32[2,136,128]{2,1,0:T(8,128)S(1)}, u32[]{:S(2)}, u32[]{:S(2)}) collective-permute-start(f32[2,136,128]{2,1,0:T(8,128)S(1)} %get-tuple-element.54), channel_id=1, source_target_pairs={{0,4},{1,5},{2,6},{3,7},{4,0},{5,1},{6,2},{7,3},{8,12},{9,13},{10,... | collective-permute-start | bytes 417800 | tf_op jit(solution)/shard_map/ppermute | solution.py:301
  48.4 0.6 %collective-permute-start.12 = (f32[2,136,128]{2,1,0:T(8,128)S(1)}, f32[2,136,128]{2,1,0:T(8,128)S(1)}, u32[]{:S(2)}, u32[]{:S(2)}) collective-permute-start(f32[2,136,128]{2,1,0:T(8,128)S(1)} %get-tuple-element.55), channel_id=1, source_target_pairs={{0,2},{1,3},{2,4},{3,5},{4,6},{5,7},{6,0},{7,1},{8,10},{9,11},{10,... | collective-permute-start | bytes 417800 | tf_op jit(solution)/shard_map/ppermute | solution.py:301
  49.0 2.0 %collective-permute-start.13 = (f32[2,136,128]{2,1,0:T(8,128)S(1)}, f32[2,136,128]{2,1,0:T(8,128)S(1)}, u32[]{:S(2)}, u32[]{:S(2)}) collective-permute-start(f32[2,136,128]{2,1,0:T(8,128)S(1)} %get-tuple-element.56), channel_id=1, source_target_pairs={{0,6},{1,7},{2,0},{3,1},{4,2},{5,3},{6,4},{7,5},{8,14},{9,15},{10,... | collective-permute-start | bytes 417800 | tf_op jit(solution)/shard_map/ppermute | solution.py:301
  51.1 1.5 %collective-permute-done.11.rest_1_ = f32[2,136,128]{2,1,0:T(8,128)S(1)} collective-permute-done((f32[2,136,128]{2,1,0:T(8,128)S(1)}, f32[2,136,128]{2,1,0:T(8,128)S(1)}, u32[]{:S(2)}, u32[]{:S(2)}) %collective-permute-start.11) | collective-permute-done | bytes 139296 | tf_op jit(solution)/shard_map/ppermute | solution.py:301
  52.6 2.9 %collective-permute-done.12.rest_2_ = f32[2,136,128]{2,1,0:T(8,128)S(1)} collective-permute-done((f32[2,136,128]{2,1,0:T(8,128)S(1)}, f32[2,136,128]{2,1,0:T(8,128)S(1)}, u32[]{:S(2)}, u32[]{:S(2)}) %collective-permute-start.12) | collective-permute-done | bytes 139296 | tf_op jit(solution)/shard_map/ppermute | solution.py:301
  55.6 1.2 %collective-permute-start.14 = (f32[4,136,128]{2,1,0:T(8,128)S(1)}, f32[4,136,128]{2,1,0:T(8,128)S(1)}, u32[]{:S(2)}, u32[]{:S(2)}) collective-permute-start(f32[4,136,128]{2,1,0:T(8,128)S(1)} %pad_maximum_fusion), channel_id=1, source_target_pairs={{0,1},{1,0},{2,3},{3,2},{4,5},{5,4},{6,7},{7,6},{8,9},{9,8},{10,11... | collective-permute-start | bytes 835592 | tf_op jit(solution)/shard_map/ppermute | solution.py:301
  56.7 0.7 %collective-permute-done.10.mirror_ref = f32[15,32,256]{2,1,0:T(8,128)S(1)} collective-permute-done((f32[15,32,256]{2,1,0:T(8,128)S(1)}, f32[15,32,256]{2,1,0:T(8,128)S(1)}, u32[]{:S(2)}, u32[]{:S(2)}) %collective-permute-start.10) | collective-permute-done | bytes 491552 | tf_op jit(solution)/shard_map/ppermute | solution.py:388
  57.5 0.1 join_mirror.1.mirror_ref
  57.5 0.4 collective-permute-done.14.rest_4_
  57.9 1.5 %join.1 = f32[32,32,256]{2,1,0:T(8,128)} custom-call(f32[32,32,256]{2,1,0:T(8,128)S(1)} %copy-done.1, f32[15,32,256]{2,1,0:T(8,128)S(1)} %join_mirror.1.mirror_ref, f32[2,136,128]{2,1,0:T(8,128)S(1)} %get-tuple-element.53.rest_0_, f32[2,136,128]{2,1,0:T(8,128)S(1)} %collective-permute-done.11.rest_1_, f32[2,136,128]{2,1,0:T(8,128)S(1)} %collective-permute-done.12.rest_2_, ...), custom_call_target="tpu_custom_call" | custom-call | tf_op jit(solution)/shard_map/join/pallas_call | solution.py:399
  (19 shorter events, 0.1 us)
Async XLA Ops:
  0.0 1.2 %copy-start = (f32[32,32,256]{2,1,0:T(8,128)S(1)}, f32[32,32,256]{2,1,0:T(8,128)}, u32[]{:S(2)}) copy-start(f32[32,32,256]{2,1,0:T(8,128)} %n_ref.5) | copy-start | bytes 3145732
  1.2 2.3 %copy-start.2 = (f32[3,256,256]{2,1,0:T(8,128)S(1)}, f32[3,256,256]{2,1,0:T(8,128)}, u32[]{:S(2)}) copy-start(f32[3,256,256]{2,1,0:T(8,128)} %c_ref.1) | copy-start | bytes 2359300
  1.2 2.3 %copy-start.3 = (s32[3]{0:T(128)S(1)}, s32[3]{0:T(128)}, u32[]{:S(2)}) copy-start(s32[3]{0:T(128)} %shift_ref.1) | copy-start | bytes 40
  1.3 11.7 %collective-permute-start.2 = (f32[6,32,256]{2,1,0:T(8,128)S(1)}, f32[6,32,256]{2,1,0:T(8,128)S(1)}, u32[]{:S(2)}, u32[]{:S(2)}) collective-permute-start(f32[6,32,256]{2,1,0:T(8,128)S(1)} %get-tuple-element.36), channel_id=1, source_target_pairs={{0,8},{8,16},{16,24},{24,32},{32,40},{40,48},{48,56},{56,64},{64,7... | collective-permute-start | bytes 589832 | tf_op jit(solution)/shard_map/ppermute | solution.py:331
  8.4 11.7 %collective-permute-start = (f32[32,1664]{1,0:T(8,128)S(1)}, f32[32,1664]{1,0:T(8,128)S(1)}, u32[]{:S(2)}, u32[]{:S(2)}) collective-permute-start(f32[32,1664]{1,0:T(8,128)S(1)} %get-tuple-element.33), channel_id=1, source_target_pairs={{0,4},{1,5},{2,6},{3,7},{4,0},{5,1},{6,2},{7,3},{8,12},{9,13},{10,... | collective-permute-start | bytes 638984 | tf_op jit(solution)/shard_map/ppermute | solution.py:301
  12.1 10.5 %collective-permute-start.1 = (f32[32,1664]{1,0:T(8,128)S(1)}, f32[32,1664]{1,0:T(8,128)S(1)}, u32[]{:S(2)}, u32[]{:S(2)}) collective-permute-start(f32[32,1664]{1,0:T(8,128)S(1)} %get-tuple-element.34), channel_id=1, source_target_pairs={{0,5},{1,4},{2,7},{3,6},{4,1},{5,0},{6,3},{7,2},{8,13},{9,12},{10,... | collective-permute-start | bytes 638984 | tf_op jit(solution)/shard_map/ppermute | solution.py:301
  15.3 8.9 %collective-permute-start.5 = (f32[32,384]{1,0:T(8,128)S(1)}, f32[32,384]{1,0:T(8,128)S(1)}, u32[]{:S(2)}, u32[]{:S(2)}) collective-permute-start(f32[32,384]{1,0:T(8,128)S(1)} %get-tuple-element.45), channel_id=1, source_target_pairs={{0,4},{1,5},{2,6},{3,7},{4,0},{5,1},{6,2},{7,3},{8,12},{9,13},{10,... | collective-permute-start | bytes 147464 | tf_op jit(solution)/shard_map/ppermute | solution.py:301
  18.6 9.9 %collective-permute-start.6 = (f32[32,384]{1,0:T(8,128)S(1)}, f32[32,384]{1,0:T(8,128)S(1)}, u32[]{:S(2)}, u32[]{:S(2)}) collective-permute-start(f32[32,384]{1,0:T(8,128)S(1)} %get-tuple-element.46), channel_id=1, source_target_pairs={{0,5},{1,4},{2,7},{3,6},{4,1},{5,0},{6,3},{7,2},{8,13},{9,12},{10,... | collective-permute-start | bytes 147464 | tf_op jit(solution)/shard_map/ppermute | solution.py:301
  18.9 11.3 %collective-permute-start.3 = (f32[32,2048]{1,0:T(8,128)S(1)}, f32[32,2048]{1,0:T(8,128)S(1)}, u32[]{:S(2)}, u32[]{:S(2)}) collective-permute-start(f32[32,2048]{1,0:T(8,128)S(1)} %get-tuple-element.43), channel_id=1, source_target_pairs={{0,2},{1,3},{2,4},{3,5},{4,6},{5,7},{6,0},{7,1},{8,10},{9,11},{10,... | collective-permute-start | bytes 786440 | tf_op jit(solution)/shard_map/ppermute | solution.py:301
  20.1 10.1 %collective-permute-start.4 = (f32[32,2048]{1,0:T(8,128)S(1)}, f32[32,2048]{1,0:T(8,128)S(1)}, u32[]{:S(2)}, u32[]{:S(2)}) collective-permute-start(f32[32,2048]{1,0:T(8,128)S(1)} %get-tuple-element.44), channel_id=1, source_target_pairs={{0,6},{1,7},{2,0},{3,1},{4,2},{5,3},{6,4},{7,5},{8,14},{9,15},{10,... | collective-permute-start | bytes 786440 | tf_op jit(solution)/shard_map/ppermute | solution.py:301
  22.6 13.2 %collective-permute-start.7 = (f32[32,2048]{1,0:T(8,128)S(1)}, f32[32,2048]{1,0:T(8,128)S(1)}, u32[]{:S(2)}, u32[]{:S(2)}) collective-permute-start(f32[32,2048]{1,0:T(8,128)S(1)} %get-tuple-element.47), channel_id=1, source_target_pairs={{0,3},{1,2},{2,5},{3,4},{4,7},{5,6},{6,1},{7,0},{8,11},{9,10},{10,... | collective-permute-start | bytes 786440 | tf_op jit(solution)/shard_map/ppermute | solution.py:301
  24.2 12.0 %collective-permute-start.8 = (f32[32,2048]{1,0:T(8,128)S(1)}, f32[32,2048]{1,0:T(8,128)S(1)}, u32[]{:S(2)}, u32[]{:S(2)}) collective-permute-start(f32[32,2048]{1,0:T(8,128)S(1)} %get-tuple-element.48), channel_id=1, source_target_pairs={{0,7},{1,6},{2,1},{3,0},{4,3},{5,2},{6,5},{7,4},{8,15},{9,14},{10,... | collective-permute-start | bytes 786440 | tf_op jit(solution)/shard_map/ppermute | solution.py:301
  28.4 7.8 %collective-permute-start.9 = (f32[32,2048]{1,0:T(8,128)S(1)}, f32[32,2048]{1,0:T(8,128)S(1)}, u32[]{:S(2)}, u32[]{:S(2)}) collective-permute-start(f32[32,2048]{1,0:T(8,128)S(1)} %get-tuple-element.49), channel_id=1, source_target_pairs={{0,1},{1,0},{2,3},{3,2},{4,5},{5,4},{6,7},{7,6},{8,9},{9,8},{10,11... | collective-permute-start | bytes 786440 | tf_op jit(solution)/shard_map/ppermute | solution.py:301
  41.2 16.3 %collective-permute-start.10 = (f32[15,32,256]{2,1,0:T(8,128)S(1)}, f32[15,32,256]{2,1,0:T(8,128)S(1)}, u32[]{:S(2)}, u32[]{:S(2)}) collective-permute-start(f32[15,32,256]{2,1,0:T(8,128)S(1)} %get-tuple-element.51), channel_id=1, source_target_pairs={{0,120},{8,112},{16,104},{24,96},{32,88},{40,80},{48,72},{56,64},{... | collective-permute-start | bytes 1474568 | tf_op jit(solution)/shard_map/ppermute | solution.py:388
  45.9 11.6 %copy-start.1 = (f32[32,32,256]{2,1,0:T(8,128)S(1)}, f32[32,32,256]{2,1,0:T(8,128)}, u32[]{:S(2)}) copy-start(f32[32,32,256]{2,1,0:T(8,128)} %n_ref.5) | copy-start | bytes 3145732
  45.9 6.7 %collective-permute-start.11 = (f32[2,136,128]{2,1,0:T(8,128)S(1)}, f32[2,136,128]{2,1,0:T(8,128)S(1)}, u32[]{:S(2)}, u32[]{:S(2)}) collective-permute-start(f32[2,136,128]{2,1,0:T(8,128)S(1)} %get-tuple-element.54), channel_id=1, source_target_pairs={{0,4},{1,5},{2,6},{3,7},{4,0},{5,1},{6,2},{7,3},{8,12},{9,13},{10,... | collective-permute-start | bytes 417800 | tf_op jit(solution)/shard_map/ppermute | solution.py:301
  48.4 7.1 %collective-permute-start.12 = (f32[2,136,128]{2,1,0:T(8,128)S(1)}, f32[2,136,128]{2,1,0:T(8,128)S(1)}, u32[]{:S(2)}, u32[]{:S(2)}) collective-permute-start(f32[2,136,128]{2,1,0:T(8,128)S(1)} %get-tuple-element.55), channel_id=1, source_target_pairs={{0,2},{1,3},{2,4},{3,5},{4,6},{5,7},{6,0},{7,1},{8,10},{9,11},{10,... | collective-permute-start | bytes 417800 | tf_op jit(solution)/shard_map/ppermute | solution.py:301
  49.0 6.5 %collective-permute-start.13 = (f32[2,136,128]{2,1,0:T(8,128)S(1)}, f32[2,136,128]{2,1,0:T(8,128)S(1)}, u32[]{:S(2)}, u32[]{:S(2)}) collective-permute-start(f32[2,136,128]{2,1,0:T(8,128)S(1)} %get-tuple-element.56), channel_id=1, source_target_pairs={{0,6},{1,7},{2,0},{3,1},{4,2},{5,3},{6,4},{7,5},{8,14},{9,15},{10,... | collective-permute-start | bytes 417800 | tf_op jit(solution)/shard_map/ppermute | solution.py:301
  55.6 2.3 %collective-permute-start.14 = (f32[4,136,128]{2,1,0:T(8,128)S(1)}, f32[4,136,128]{2,1,0:T(8,128)S(1)}, u32[]{:S(2)}, u32[]{:S(2)}) collective-permute-start(f32[4,136,128]{2,1,0:T(8,128)S(1)} %pad_maximum_fusion), channel_id=1, source_target_pairs={{0,1},{1,0},{2,3},{3,2},{4,5},{5,4},{6,7},{7,6},{8,9},{9,8},{10,11... | collective-permute-start | bytes 835592 | tf_op jit(solution)/shard_map/ppermute | solution.py:301

commit v3 on v2

--- a/solution.py
+++ b/solution.py
@@ -192,7 +192,7 @@
             r_ref[rows, :] = ref[...]
 
 
-def left_kernel(c_ref, r_ref, result_ref, mirror_ref, b_scr, x_scr):
+def left_kernel(c_ref, r_ref, tiles_ref, mirror_ref, b_scr, x_scr):
     split_taps(c_ref, b_scr)
     block = block_of_lane(N)
     total = None
@@ -223,6 +223,20 @@
                     x_scr[k + 2 * N : k + 3 * N, lanes] = high
         total = nn(b_scr[...], x_scr[...])
     tiles = [total[:, 128 * g : 128 * (g + 1)] for g in range(GRID)]
+    for g in range(GRID):
+        turned = tiles[g].T
+        for q in range(4):
+            d = GRID * q + g - BASE
+            if 1 <= d <= 15:
+                mirror_ref[15 - d] = turned[32 * q : 32 * (q + 1)]
+    tiles_ref[...] = total
+
+
+def pack_kernel(tiles_ref, *rest):
+    outs = rest[:4]
+    result_ref = rest[4]
+    tiles = [tiles_ref[:, 128 * g : 128 * (g + 1)] for g in range(GRID)]
+    block = block_of_lane(N)
     for m, entries in enumerate(RESULT):
         value = None
         for q, d in enumerate(entries):
@@ -241,15 +255,6 @@
         part = part if a == p else pltpu.roll(part, (32 * (a - p)) % 128, 1)
         value = part if value is None else jnp.where(block == a, part, value)
     result_ref[:, OUT_ROWS - 8 :, :] = value.reshape(8, 8, 128)
-    for g in range(GRID):
-        turned = tiles[g].T
-        for q in range(4):
-            d = GRID * q + g - BASE
-            if 1 <= d <= 15:
-                mirror_ref[15 - d] = turned[32 * q : 32 * (q + 1)]
-
-
-def pack_kernel(result_ref, *outs):
     for k, out in zip(DISTANCES, outs):
         for e in range(2):
             out[e] = result_ref[target(k, e)]
@@ -365,7 +370,7 @@
     )(*early, local[0, 0], *halos)
     result, mirror = pl.pallas_call(
         left_kernel,
-        out_shape=[jax.ShapeDtypeStruct((8, OUT_ROWS, 128), f32), jax.ShapeDtypeStruct((15, R, N), f32)],
+        out_shape=[jax.ShapeDtypeStruct((N, 128 * GRID), f32), jax.ShapeDtypeStruct((15, R, N), f32)],
         in_specs=[VMEM] * 2,
         out_specs=[VMEM] * 2,
         scratch_shapes=[
@@ -381,6 +386,7 @@
         out_shape=[jax.ShapeDtypeStruct((2, OUT_ROWS, 128), f32)] * 4,
         in_specs=[VMEM],
         out_specs=[VMEM] * 4,
+        scratch_shapes=[pltpu.VMEM((8, OUT_ROWS, 128), f32)],
         compiler_params=PARAMS,
         cost_estimate=cost(30, 1 << 19),
         name="pack",

time: 59.5 us -> 59.5 us (level)
  transfers between devices with their start and end apart: 15 -> 15, of which waited for: 8 -> 8; matrix products, arithmetic and copies ran while one was open for 0% -> 0% of each run, Pallas kernels for 12% -> 13%
where the time goes in v3:
time: 59.5 us; the launch traced here: 59.4 us
  starting transfers between devices  30.6 us (51%)
  waiting for transfers between devices  13.8 us (23%)
  Pallas kernels  13.7 us (23%)
  local copies, waits for them, and re-layouts  1.26 us (2%)
    ppermute x13, starting transfers between devices, send(): return lax.ppermute(array, 'col', pairs)  23.7 us
    ppermute x13, waiting for transfers between devices, send(): return lax.ppermute(array, 'col', pairs)  13.3 us
    pallas_call x1, Pallas kernels, body(): pl.pallas_call(local_kernel, out_shape=[jax.ShapeDtypeStruct((R, LOCAL_LA...  4.92 us
    ppermute x1, starting transfers between devices, body(): mirror = lax.ppermute(mirror, 'off', [(o, 15 - o) for o in range(16)])  4.69 us
    pallas_call x1, Pallas kernels, body(): pl.pallas_call(left_kernel, out_shape=[jax.ShapeDtypeStruct((N, 128 * GRI...  4.51 us
    pallas_call x1, Pallas kernels, body(): pl.pallas_call(halo_kernel, out_shape=[jax.ShapeDtypeStruct((R, HALO_LANE...  2.27 us
    ppermute x1, starting transfers between devices, body(): halo = lax.ppermute(edge, 'off', [(o, (o + 1) % 16) for o in range(16)])  2.19 us
    pallas_call x1, Pallas kernels, body(): pl.pallas_call(join_kernel, out_shape=jax.ShapeDtypeStruct((R, R, N), f32...  1.46 us
  transfers between devices with their start and end apart: 15, of which 8 were waited for; matrix products, arithmetic and copies ran while one was open for 0% of the time, Pallas kernels for 13%

profile of v3, /device:TPU:1, one launch (start us, length us, event | category | flops | bytes accessed | tf_op | source)
XLA Modules:
  0.0 59.4 jit_solution(17017360759619341435)
XLA Ops:
  0.0 1.2 %copy-done = f32[32,32,256]{2,1,0:T(8,128)S(1)} copy-done((f32[32,32,256]{2,1,0:T(8,128)S(1)}, f32[32,32,256]{2,1,0:T(8,128)}, u32[]{:S(2)}) %copy-start) | copy-done | bytes 1048600
  1.2 0.1 edge.1
  1.3 2.2 %collective-permute-start.2 = (f32[6,32,256]{2,1,0:T(8,128)S(1)}, f32[6,32,256]{2,1,0:T(8,128)S(1)}, u32[]{:S(2)}, u32[]{:S(2)}) collective-permute-start(f32[6,32,256]{2,1,0:T(8,128)S(1)} %get-tuple-element.36), channel_id=1, source_target_pairs={{0,8},{8,16},{16,24},{24,32},{32,40},{40,48},{48,56},{56,64},{64,7... | collective-permute-start | bytes 589832 | tf_op jit(solution)/shard_map/ppermute | solution.py:336
  3.5 4.9 %local_right_products.1 = (f32[32,1664]{1,0:T(8,128)S(1)}, f32[32,1664]{1,0:T(8,128)S(1)}, f32[32,1664]{1,0:T(8,128)S(1)}, f32[32,1664]{1,0:T(8,128)S(1)}, f32[3...) custom-call(s32[3]{0:T(128)S(1)} %copy-done.3, ...), custom_call_target="tpu_custom_call" | custom-call | flops 2151677952 | bytes 4194304 | tf_op jit(solution)/shard_map/local_right_products/pallas_call | solution.py:337
  8.4 3.7 %collective-permute-start = (f32[32,1664]{1,0:T(8,128)S(1)}, f32[32,1664]{1,0:T(8,128)S(1)}, u32[]{:S(2)}, u32[]{:S(2)}) collective-permute-start(f32[32,1664]{1,0:T(8,128)S(1)} %get-tuple-element.33), channel_id=1, source_target_pairs={{0,4},{1,5},{2,6},{3,7},{4,0},{5,1},{6,2},{7,3},{8,12},{9,13},{10,... | collective-permute-start | bytes 638984 | tf_op jit(solution)/shard_map/ppermute | solution.py:306
  12.1 0.9 %collective-permute-start.1 = (f32[32,1664]{1,0:T(8,128)S(1)}, f32[32,1664]{1,0:T(8,128)S(1)}, u32[]{:S(2)}, u32[]{:S(2)}) collective-permute-start(f32[32,1664]{1,0:T(8,128)S(1)} %get-tuple-element.34), channel_id=1, source_target_pairs={{0,5},{1,4},{2,7},{3,6},{4,1},{5,0},{6,3},{7,2},{8,13},{9,12},{10,... | collective-permute-start | bytes 638984 | tf_op jit(solution)/shard_map/ppermute | solution.py:306
  13.0 0.0 collective-permute-done.2.halo_ref
  13.0 2.3 %halo_right_products.1 = (f32[32,2048]{1,0:T(8,128)S(1)}, f32[32,2048]{1,0:T(8,128)S(1)}, f32[32,384]{1,0:T(8,128)S(1)}, f32[32,384]{1,0:T(8,128)S(1)}, f32[32,2...) custom-call(f32[6,32,256]{2,1,0:T(8,128)S(1)} %collective-permute-done.2.halo_ref, ...), custom_call_target="tpu_custom_call" | custom-call | flops 377487360 | bytes 2097152 | tf_op jit(solution)/shard_map/halo_right_products/pallas_call | solution.py:349
  15.3 3.2 %collective-permute-start.5 = (f32[32,384]{1,0:T(8,128)S(1)}, f32[32,384]{1,0:T(8,128)S(1)}, u32[]{:S(2)}, u32[]{:S(2)}) collective-permute-start(f32[32,384]{1,0:T(8,128)S(1)} %get-tuple-element.45), channel_id=1, source_target_pairs={{0,4},{1,5},{2,6},{3,7},{4,0},{5,1},{6,2},{7,3},{8,12},{9,13},{10,... | collective-permute-start | bytes 147464 | tf_op jit(solution)/shard_map/ppermute | solution.py:306
  18.6 0.3 collective-permute-start.6
  18.9 1.2 %collective-permute-start.3 = (f32[32,2048]{1,0:T(8,128)S(1)}, f32[32,2048]{1,0:T(8,128)S(1)}, u32[]{:S(2)}, u32[]{:S(2)}) collective-permute-start(f32[32,2048]{1,0:T(8,128)S(1)} %get-tuple-element.43), channel_id=1, source_target_pairs={{0,2},{1,3},{2,4},{3,5},{4,6},{5,7},{6,0},{7,1},{8,10},{9,11},{10,... | collective-permute-start | bytes 786440 | tf_op jit(solution)/shard_map/ppermute | solution.py:306
  20.1 2.1 %collective-permute-start.4 = (f32[32,2048]{1,0:T(8,128)S(1)}, f32[32,2048]{1,0:T(8,128)S(1)}, u32[]{:S(2)}, u32[]{:S(2)}) collective-permute-start(f32[32,2048]{1,0:T(8,128)S(1)} %get-tuple-element.44), channel_id=1, source_target_pairs={{0,6},{1,7},{2,0},{3,1},{4,2},{5,3},{6,4},{7,5},{8,14},{9,15},{10,... | collective-permute-start | bytes 786440 | tf_op jit(solution)/shard_map/ppermute | solution.py:306
  22.2 0.4 collective-permute-done.1.refs_1_
  22.6 1.6 %collective-permute-start.7 = (f32[32,2048]{1,0:T(8,128)S(1)}, f32[32,2048]{1,0:T(8,128)S(1)}, u32[]{:S(2)}, u32[]{:S(2)}) collective-permute-start(f32[32,2048]{1,0:T(8,128)S(1)} %get-tuple-element.47), channel_id=1, source_target_pairs={{0,3},{1,2},{2,5},{3,4},{4,7},{5,6},{6,1},{7,0},{8,11},{9,10},{10,... | collective-permute-start | bytes 786440 | tf_op jit(solution)/shard_map/ppermute | solution.py:306
  24.2 4.2 %collective-permute-start.8 = (f32[32,2048]{1,0:T(8,128)S(1)}, f32[32,2048]{1,0:T(8,128)S(1)}, u32[]{:S(2)}, u32[]{:S(2)}) collective-permute-start(f32[32,2048]{1,0:T(8,128)S(1)} %get-tuple-element.48), channel_id=1, source_target_pairs={{0,7},{1,6},{2,1},{3,0},{4,3},{5,2},{6,5},{7,4},{8,15},{9,14},{10,... | collective-permute-start | bytes 786440 | tf_op jit(solution)/shard_map/ppermute | solution.py:306
  28.4 1.8 %collective-permute-done.3.refs_3_ = f32[32,2048]{1,0:T(8,128)S(1)} collective-permute-done((f32[32,2048]{1,0:T(8,128)S(1)}, f32[32,2048]{1,0:T(8,128)S(1)}, u32[]{:S(2)}, u32[]{:S(2)}) %collective-permute-start.3) | collective-permute-done | bytes 262176 | tf_op jit(solution)/shard_map/ppermute | solution.py:306
  30.2 5.6 %collective-permute-done.7.refs_7_ = f32[32,2048]{1,0:T(8,128)S(1)} collective-permute-done((f32[32,2048]{1,0:T(8,128)S(1)}, f32[32,2048]{1,0:T(8,128)S(1)}, u32[]{:S(2)}, u32[]{:S(2)}) %collective-permute-start.7) | collective-permute-done | bytes 262176 | tf_op jit(solution)/shard_map/ppermute | solution.py:306
  35.8 0.4 collective-permute-done.8.refs_8_
  36.3 0.2 gather_rows.1.r_ref
  36.4 4.5 %left_products.1 = (f32[256,768]{1,0:T(8,128)S(1)}, f32[15,32,256]{2,1,0:T(8,128)S(1)}) custom-call(f32[3,256,256]{2,1,0:T(8,128)S(1)} %get-tuple-element.32.c_ref, f32[256,2048]{1,0:T(8,128)S(1)} %gather_rows.1.r_ref), custom_call_target="tpu_custom_call" | custom-call | flops 2717908992 | bytes 8388608 | tf_op jit(solution)/shard_map/left_products/pallas_call | solution.py:371
  40.9 4.7 %collective-permute-start.10 = (f32[15,32,256]{2,1,0:T(8,128)S(1)}, f32[15,32,256]{2,1,0:T(8,128)S(1)}, u32[]{:S(2)}, u32[]{:S(2)}) collective-permute-start(f32[15,32,256]{2,1,0:T(8,128)S(1)} %get-tuple-element.51), channel_id=1, source_target_pairs={{0,120},{8,112},{16,104},{24,96},{32,88},{40,80},{48,72},{56,64},{... | collective-permute-start | bytes 1474568 | tf_op jit(solution)/shard_map/ppermute | solution.py:394
  45.6 0.2 pack.1
  45.9 2.5 %collective-permute-start.11 = (f32[2,136,128]{2,1,0:T(8,128)S(1)}, f32[2,136,128]{2,1,0:T(8,128)S(1)}, u32[]{:S(2)}, u32[]{:S(2)}) collective-permute-start(f32[2,136,128]{2,1,0:T(8,128)S(1)} %get-tuple-element.54), channel_id=1, source_target_pairs={{0,4},{1,5},{2,6},{3,7},{4,0},{5,1},{6,2},{7,3},{8,12},{9,13},{10,... | collective-permute-start | bytes 417800 | tf_op jit(solution)/shard_map/ppermute | solution.py:306
  48.4 0.6 %collective-permute-start.12 = (f32[2,136,128]{2,1,0:T(8,128)S(1)}, f32[2,136,128]{2,1,0:T(8,128)S(1)}, u32[]{:S(2)}, u32[]{:S(2)}) collective-permute-start(f32[2,136,128]{2,1,0:T(8,128)S(1)} %get-tuple-element.55), channel_id=1, source_target_pairs={{0,2},{1,3},{2,4},{3,5},{4,6},{5,7},{6,0},{7,1},{8,10},{9,11},{10,... | collective-permute-start | bytes 417800 | tf_op jit(solution)/shard_map/ppermute | solution.py:306
  49.0 2.0 %collective-permute-start.13 = (f32[2,136,128]{2,1,0:T(8,128)S(1)}, f32[2,136,128]{2,1,0:T(8,128)S(1)}, u32[]{:S(2)}, u32[]{:S(2)}) collective-permute-start(f32[2,136,128]{2,1,0:T(8,128)S(1)} %get-tuple-element.56), channel_id=1, source_target_pairs={{0,6},{1,7},{2,0},{3,1},{4,2},{5,3},{6,4},{7,5},{8,14},{9,15},{10,... | collective-permute-start | bytes 417800 | tf_op jit(solution)/shard_map/ppermute | solution.py:306
  51.1 1.5 %collective-permute-done.11.rest_1_ = f32[2,136,128]{2,1,0:T(8,128)S(1)} collective-permute-done((f32[2,136,128]{2,1,0:T(8,128)S(1)}, f32[2,136,128]{2,1,0:T(8,128)S(1)}, u32[]{:S(2)}, u32[]{:S(2)}) %collective-permute-start.11) | collective-permute-done | bytes 139296 | tf_op jit(solution)/shard_map/ppermute | solution.py:306
  52.6 2.9 %collective-permute-done.12.rest_2_ = f32[2,136,128]{2,1,0:T(8,128)S(1)} collective-permute-done((f32[2,136,128]{2,1,0:T(8,128)S(1)}, f32[2,136,128]{2,1,0:T(8,128)S(1)}, u32[]{:S(2)}, u32[]{:S(2)}) %collective-permute-start.12) | collective-permute-done | bytes 139296 | tf_op jit(solution)/shard_map/ppermute | solution.py:306
  55.6 1.2 %collective-permute-start.14 = (f32[4,136,128]{2,1,0:T(8,128)S(1)}, f32[4,136,128]{2,1,0:T(8,128)S(1)}, u32[]{:S(2)}, u32[]{:S(2)}) collective-permute-start(f32[4,136,128]{2,1,0:T(8,128)S(1)} %pad_maximum_fusion), channel_id=1, source_target_pairs={{0,1},{1,0},{2,3},{3,2},{4,5},{5,4},{6,7},{7,6},{8,9},{9,8},{10,11... | collective-permute-start | bytes 835592 | tf_op jit(solution)/shard_map/ppermute | solution.py:306
  56.8 0.5 collective-permute-done.10.mirror_ref
  57.3 0.1 join_mirror.1.mirror_ref
  57.3 0.6 %collective-permute-done.14.rest_4_ = f32[4,136,128]{2,1,0:T(8,128)S(1)} collective-permute-done((f32[4,136,128]{2,1,0:T(8,128)S(1)}, f32[4,136,128]{2,1,0:T(8,128)S(1)}, u32[]{:S(2)}, u32[]{:S(2)}) %collective-permute-start.14) | collective-permute-done | bytes 278560 | tf_op jit(solution)/shard_map/ppermute | solution.py:306
  57.9 1.5 %join.1 = f32[32,32,256]{2,1,0:T(8,128)} custom-call(f32[32,32,256]{2,1,0:T(8,128)S(1)} %copy-done.1, f32[15,32,256]{2,1,0:T(8,128)S(1)} %join_mirror.1.mirror_ref, f32[2,136,128]{2,1,0:T(8,128)S(1)} %get-tuple-element.53.rest_0_, f32[2,136,128]{2,1,0:T(8,128)S(1)} %collective-permute-done.11.rest_1_, f32[2,136,128]{2,1,0:T(8,128)S(1)} %collective-permute-done.12.rest_2_, ...), custom_call_target="tpu_custom_call" | custom-call | tf_op jit(solution)/shard_map/join/pallas_call | solution.py:405
  (19 shorter events, 0.1 us)
Async XLA Ops:
  0.0 1.2 %copy-start = (f32[32,32,256]{2,1,0:T(8,128)S(1)}, f32[32,32,256]{2,1,0:T(8,128)}, u32[]{:S(2)}) copy-start(f32[32,32,256]{2,1,0:T(8,128)} %n_ref.5) | copy-start | bytes 3145732
  1.2 2.3 %copy-start.2 = (f32[3,256,256]{2,1,0:T(8,128)S(1)}, f32[3,256,256]{2,1,0:T(8,128)}, u32[]{:S(2)}) copy-start(f32[3,256,256]{2,1,0:T(8,128)} %c_ref.1) | copy-start | bytes 2359300
  1.2 2.3 %copy-start.3 = (s32[3]{0:T(128)S(1)}, s32[3]{0:T(128)}, u32[]{:S(2)}) copy-start(s32[3]{0:T(128)} %shift_ref.1) | copy-start | bytes 40
  1.3 11.7 %collective-permute-start.2 = (f32[6,32,256]{2,1,0:T(8,128)S(1)}, f32[6,32,256]{2,1,0:T(8,128)S(1)}, u32[]{:S(2)}, u32[]{:S(2)}) collective-permute-start(f32[6,32,256]{2,1,0:T(8,128)S(1)} %get-tuple-element.36), channel_id=1, source_target_pairs={{0,8},{8,16},{16,24},{24,32},{32,40},{40,48},{48,56},{56,64},{64,7... | collective-permute-start | bytes 589832 | tf_op jit(solution)/shard_map/ppermute | solution.py:336
  8.4 11.7 %collective-permute-start = (f32[32,1664]{1,0:T(8,128)S(1)}, f32[32,1664]{1,0:T(8,128)S(1)}, u32[]{:S(2)}, u32[]{:S(2)}) collective-permute-start(f32[32,1664]{1,0:T(8,128)S(1)} %get-tuple-element.33), channel_id=1, source_target_pairs={{0,4},{1,5},{2,6},{3,7},{4,0},{5,1},{6,2},{7,3},{8,12},{9,13},{10,... | collective-permute-start | bytes 638984 | tf_op jit(solution)/shard_map/ppermute | solution.py:306
  12.1 10.5 %collective-permute-start.1 = (f32[32,1664]{1,0:T(8,128)S(1)}, f32[32,1664]{1,0:T(8,128)S(1)}, u32[]{:S(2)}, u32[]{:S(2)}) collective-permute-start(f32[32,1664]{1,0:T(8,128)S(1)} %get-tuple-element.34), channel_id=1, source_target_pairs={{0,5},{1,4},{2,7},{3,6},{4,1},{5,0},{6,3},{7,2},{8,13},{9,12},{10,... | collective-permute-start | bytes 638984 | tf_op jit(solution)/shard_map/ppermute | solution.py:306
  15.3 8.9 %collective-permute-start.5 = (f32[32,384]{1,0:T(8,128)S(1)}, f32[32,384]{1,0:T(8,128)S(1)}, u32[]{:S(2)}, u32[]{:S(2)}) collective-permute-start(f32[32,384]{1,0:T(8,128)S(1)} %get-tuple-element.45), channel_id=1, source_target_pairs={{0,4},{1,5},{2,6},{3,7},{4,0},{5,1},{6,2},{7,3},{8,12},{9,13},{10,... | collective-permute-start | bytes 147464 | tf_op jit(solution)/shard_map/ppermute | solution.py:306
  18.6 9.9 %collective-permute-start.6 = (f32[32,384]{1,0:T(8,128)S(1)}, f32[32,384]{1,0:T(8,128)S(1)}, u32[]{:S(2)}, u32[]{:S(2)}) collective-permute-start(f32[32,384]{1,0:T(8,128)S(1)} %get-tuple-element.46), channel_id=1, source_target_pairs={{0,5},{1,4},{2,7},{3,6},{4,1},{5,0},{6,3},{7,2},{8,13},{9,12},{10,... | collective-permute-start | bytes 147464 | tf_op jit(solution)/shard_map/ppermute | solution.py:306
  18.9 11.3 %collective-permute-start.3 = (f32[32,2048]{1,0:T(8,128)S(1)}, f32[32,2048]{1,0:T(8,128)S(1)}, u32[]{:S(2)}, u32[]{:S(2)}) collective-permute-start(f32[32,2048]{1,0:T(8,128)S(1)} %get-tuple-element.43), channel_id=1, source_target_pairs={{0,2},{1,3},{2,4},{3,5},{4,6},{5,7},{6,0},{7,1},{8,10},{9,11},{10,... | collective-permute-start | bytes 786440 | tf_op jit(solution)/shard_map/ppermute | solution.py:306
  20.1 10.1 %collective-permute-start.4 = (f32[32,2048]{1,0:T(8,128)S(1)}, f32[32,2048]{1,0:T(8,128)S(1)}, u32[]{:S(2)}, u32[]{:S(2)}) collective-permute-start(f32[32,2048]{1,0:T(8,128)S(1)} %get-tuple-element.44), channel_id=1, source_target_pairs={{0,6},{1,7},{2,0},{3,1},{4,2},{5,3},{6,4},{7,5},{8,14},{9,15},{10,... | collective-permute-start | bytes 786440 | tf_op jit(solution)/shard_map/ppermute | solution.py:306
  22.6 13.2 %collective-permute-start.7 = (f32[32,2048]{1,0:T(8,128)S(1)}, f32[32,2048]{1,0:T(8,128)S(1)}, u32[]{:S(2)}, u32[]{:S(2)}) collective-permute-start(f32[32,2048]{1,0:T(8,128)S(1)} %get-tuple-element.47), channel_id=1, source_target_pairs={{0,3},{1,2},{2,5},{3,4},{4,7},{5,6},{6,1},{7,0},{8,11},{9,10},{10,... | collective-permute-start | bytes 786440 | tf_op jit(solution)/shard_map/ppermute | solution.py:306
  24.2 12.0 %collective-permute-start.8 = (f32[32,2048]{1,0:T(8,128)S(1)}, f32[32,2048]{1,0:T(8,128)S(1)}, u32[]{:S(2)}, u32[]{:S(2)}) collective-permute-start(f32[32,2048]{1,0:T(8,128)S(1)} %get-tuple-element.48), channel_id=1, source_target_pairs={{0,7},{1,6},{2,1},{3,0},{4,3},{5,2},{6,5},{7,4},{8,15},{9,14},{10,... | collective-permute-start | bytes 786440 | tf_op jit(solution)/shard_map/ppermute | solution.py:306
  28.4 7.8 %collective-permute-start.9 = (f32[32,2048]{1,0:T(8,128)S(1)}, f32[32,2048]{1,0:T(8,128)S(1)}, u32[]{:S(2)}, u32[]{:S(2)}) collective-permute-start(f32[32,2048]{1,0:T(8,128)S(1)} %get-tuple-element.49), channel_id=1, source_target_pairs={{0,1},{1,0},{2,3},{3,2},{4,5},{5,4},{6,7},{7,6},{8,9},{9,8},{10,11... | collective-permute-start | bytes 786440 | tf_op jit(solution)/shard_map/ppermute | solution.py:306
  40.9 16.3 %collective-permute-start.10 = (f32[15,32,256]{2,1,0:T(8,128)S(1)}, f32[15,32,256]{2,1,0:T(8,128)S(1)}, u32[]{:S(2)}, u32[]{:S(2)}) collective-permute-start(f32[15,32,256]{2,1,0:T(8,128)S(1)} %get-tuple-element.51), channel_id=1, source_target_pairs={{0,120},{8,112},{16,104},{24,96},{32,88},{40,80},{48,72},{56,64},{... | collective-permute-start | bytes 1474568 | tf_op jit(solution)/shard_map/ppermute | solution.py:394
  45.6 11.6 %copy-start.1 = (f32[32,32,256]{2,1,0:T(8,128)S(1)}, f32[32,32,256]{2,1,0:T(8,128)}, u32[]{:S(2)}) copy-start(f32[32,32,256]{2,1,0:T(8,128)} %n_ref.5) | copy-start | bytes 3145732
  45.9 6.7 %collective-permute-start.11 = (f32[2,136,128]{2,1,0:T(8,128)S(1)}, f32[2,136,128]{2,1,0:T(8,128)S(1)}, u32[]{:S(2)}, u32[]{:S(2)}) collective-permute-start(f32[2,136,128]{2,1,0:T(8,128)S(1)} %get-tuple-element.54), channel_id=1, source_target_pairs={{0,4},{1,5},{2,6},{3,7},{4,0},{5,1},{6,2},{7,3},{8,12},{9,13},{10,... | collective-permute-start | bytes 417800 | tf_op jit(solution)/shard_map/ppermute | solution.py:306
  48.4 7.1 %collective-permute-start.12 = (f32[2,136,128]{2,1,0:T(8,128)S(1)}, f32[2,136,128]{2,1,0:T(8,128)S(1)}, u32[]{:S(2)}, u32[]{:S(2)}) collective-permute-start(f32[2,136,128]{2,1,0:T(8,128)S(1)} %get-tuple-element.55), channel_id=1, source_target_pairs={{0,2},{1,3},{2,4},{3,5},{4,6},{5,7},{6,0},{7,1},{8,10},{9,11},{10,... | collective-permute-start | bytes 417800 | tf_op jit(solution)/shard_map/ppermute | solution.py:306
  49.0 6.5 %collective-permute-start.13 = (f32[2,136,128]{2,1,0:T(8,128)S(1)}, f32[2,136,128]{2,1,0:T(8,128)S(1)}, u32[]{:S(2)}, u32[]{:S(2)}) collective-permute-start(f32[2,136,128]{2,1,0:T(8,128)S(1)} %get-tuple-element.56), channel_id=1, source_target_pairs={{0,6},{1,7},{2,0},{3,1},{4,2},{5,3},{6,4},{7,5},{8,14},{9,15},{10,... | collective-permute-start | bytes 417800 | tf_op jit(solution)/shard_map/ppermute | solution.py:306
  55.6 2.4 %collective-permute-start.14 = (f32[4,136,128]{2,1,0:T(8,128)S(1)}, f32[4,136,128]{2,1,0:T(8,128)S(1)}, u32[]{:S(2)}, u32[]{:S(2)}) collective-permute-start(f32[4,136,128]{2,1,0:T(8,128)S(1)} %pad_maximum_fusion), channel_id=1, source_target_pairs={{0,1},{1,0},{2,3},{3,2},{4,5},{5,4},{6,7},{7,6},{8,9},{9,8},{10,11... | collective-permute-start | bytes 835592 | tf_op jit(solution)/shard_map/ppermute | solution.py:306

commit v4 on v3

--- a/solution.py
+++ b/solution.py
@@ -180,8 +180,7 @@
         out[:, lane:] = m_scr[target(*slot)]
 
 
-def gather_kernel(*refs):
-    r_ref = refs[11]
+def gather_rows(refs, r_ref):
     local = dict(zip(EARLY + [(0, 0)], refs[:3]))
     for ref, slot in zip(refs[3:11], SECOND):
         rows = pl.ds(pl.multiple_of(source(*slot) * R, R), R)
@@ -192,7 +191,9 @@
             r_ref[rows, :] = ref[...]
 
 
-def left_kernel(c_ref, r_ref, tiles_ref, mirror_ref, b_scr, x_scr):
+def left_kernel(c_ref, *rest):
+    tiles_ref, mirror_ref, r_ref, b_scr, x_scr = rest[11:]
+    gather_rows(rest[:11], r_ref)
     split_taps(c_ref, b_scr)
     block = block_of_lane(N)
     total = None
@@ -359,28 +360,20 @@
         name="halo_right_products",
     )(halo, first, taps, *[local[slot] for slot in LATE])
     halos = [array if slot == (0, 0) else send(array, *slot) for array, slot in zip(halos, SECOND)]
-    rows = pl.pallas_call(
-        gather_kernel,
-        out_shape=jax.ShapeDtypeStruct((N, LOCAL_LANES + HALO_LANES), f32),
-        in_specs=[VMEM] * 11,
-        out_specs=VMEM,
-        compiler_params=PARAMS,
-        cost_estimate=cost(10, 1 << 20),
-        name="gather_rows",
-    )(*early, local[0, 0], *halos)
     result, mirror = pl.pallas_call(
         left_kernel,
         out_shape=[jax.ShapeDtypeStruct((N, 128 * GRID), f32), jax.ShapeDtypeStruct((15, R, N), f32)],
-        in_specs=[VMEM] * 2,
+        in_specs=[VMEM] * 12,
         out_specs=[VMEM] * 2,
         scratch_shapes=[
+            pltpu.VMEM((N, LOCAL_LANES + HALO_LANES), f32),
             pltpu.VMEM((N, 9 * N), bf16),
             pltpu.VMEM((9 * N, 128 * GRID), bf16),
         ],
         compiler_params=PARAMS,
         cost_estimate=cost(72, 1 << 21),
         name="left_products",
-    )(taps, rows)
+    )(taps, *early, local[0, 0], *halos)
     rows = pl.pallas_call(
         pack_kernel,
         out_shape=[jax.ShapeDtypeStruct((2, OUT_ROWS, 128), f32)] * 4,

time: 59.5 us -> 59.5 us (level)
  no operation moved by 1% of the time
where the time goes in v4:
time: 59.5 us; the launch traced here: 59.4 us
  starting transfers between devices  30.6 us (51%)
  waiting for transfers between devices  13.8 us (23%)
  Pallas kernels  13.7 us (23%)
  local copies, waits for them, and re-layouts  1.26 us (2%)
    ppermute x13, starting transfers between devices, send(): return lax.ppermute(array, 'col', pairs)  23.7 us
    ppermute x13, waiting for transfers between devices, send(): return lax.ppermute(array, 'col', pairs)  13.3 us
    pallas_call x1, Pallas kernels, body(): pl.pallas_call(local_kernel, out_shape=[jax.ShapeDtypeStruct((R, LOCAL_LA...  4.93 us
    ppermute x1, starting transfers between devices, body(): mirror = lax.ppermute(mirror, 'off', [(o, 15 - o) for o in range(16)])  4.69 us
    pallas_call x1, Pallas kernels, body(): pl.pallas_call(left_kernel, out_shape=[jax.ShapeDtypeStruct((N, 128 * GRI...  4.65 us
    pallas_call x1, Pallas kernels, body(): pl.pallas_call(halo_kernel, out_shape=[jax.ShapeDtypeStruct((R, HALO_LANE...  2.27 us
    ppermute x1, starting transfers between devices, body(): halo = lax.ppermute(edge, 'off', [(o, (o + 1) % 16) for o in range(16)])  2.19 us
    pallas_call x1, Pallas kernels, body(): pl.pallas_call(join_kernel, out_shape=jax.ShapeDtypeStruct((R, R, N), f32...  1.46 us
  transfers between devices with their start and end apart: 15, of which 8 were waited for; matrix products, arithmetic and copies ran while one was open for 0% of the time, Pallas kernels for 13%

profile of v4, /device:TPU:1, one launch (start us, length us, event | category | flops | bytes accessed | tf_op | source)
XLA Modules:
  0.0 59.4 jit_solution(13314767177873587613)
XLA Ops:
  0.0 1.2 %copy-done = f32[32,32,256]{2,1,0:T(8,128)S(1)} copy-done((f32[32,32,256]{2,1,0:T(8,128)S(1)}, f32[32,32,256]{2,1,0:T(8,128)}, u32[]{:S(2)}) %copy-start) | copy-done | bytes 1048600
  1.2 0.1 edge.1
  1.3 0.0 copy-start.3
  1.3 2.2 %collective-permute-start.2 = (f32[6,32,256]{2,1,0:T(8,128)S(1)}, f32[6,32,256]{2,1,0:T(8,128)S(1)}, u32[]{:S(2)}, u32[]{:S(2)}) collective-permute-start(f32[6,32,256]{2,1,0:T(8,128)S(1)} %get-tuple-element.36), channel_id=1, source_target_pairs={{0,8},{8,16},{16,24},{24,32},{32,40},{40,48},{48,56},{56,64},{64,7... | collective-permute-start | bytes 589832 | tf_op jit(solution)/shard_map/ppermute | solution.py:337
  3.5 4.9 %local_right_products.1 = (f32[32,1664]{1,0:T(8,128)S(1)}, f32[32,1664]{1,0:T(8,128)S(1)}, f32[32,1664]{1,0:T(8,128)S(1)}, f32[32,1664]{1,0:T(8,128)S(1)}, f32[3...) custom-call(s32[3]{0:T(128)S(1)} %copy-done.3, ...), custom_call_target="tpu_custom_call" | custom-call | flops 2151677952 | bytes 4194304 | tf_op jit(solution)/shard_map/local_right_products/pallas_call | solution.py:338
  8.4 3.7 %collective-permute-start = (f32[32,1664]{1,0:T(8,128)S(1)}, f32[32,1664]{1,0:T(8,128)S(1)}, u32[]{:S(2)}, u32[]{:S(2)}) collective-permute-start(f32[32,1664]{1,0:T(8,128)S(1)} %get-tuple-element.33), channel_id=1, source_target_pairs={{0,4},{1,5},{2,6},{3,7},{4,0},{5,1},{6,2},{7,3},{8,12},{9,13},{10,... | collective-permute-start | bytes 638984 | tf_op jit(solution)/shard_map/ppermute | solution.py:307
  12.1 0.9 %collective-permute-start.1 = (f32[32,1664]{1,0:T(8,128)S(1)}, f32[32,1664]{1,0:T(8,128)S(1)}, u32[]{:S(2)}, u32[]{:S(2)}) collective-permute-start(f32[32,1664]{1,0:T(8,128)S(1)} %get-tuple-element.34), channel_id=1, source_target_pairs={{0,5},{1,4},{2,7},{3,6},{4,1},{5,0},{6,3},{7,2},{8,13},{9,12},{10,... | collective-permute-start | bytes 638984 | tf_op jit(solution)/shard_map/ppermute | solution.py:307
  13.1 2.3 %halo_right_products.1 = (f32[32,2048]{1,0:T(8,128)S(1)}, f32[32,2048]{1,0:T(8,128)S(1)}, f32[32,384]{1,0:T(8,128)S(1)}, f32[32,384]{1,0:T(8,128)S(1)}, f32[32,2...) custom-call(f32[6,32,256]{2,1,0:T(8,128)S(1)} %collective-permute-done.2.halo_ref, ...), custom_call_target="tpu_custom_call" | custom-call | flops 377487360 | bytes 2097152 | tf_op jit(solution)/shard_map/halo_right_products/pallas_call | solution.py:350
  15.3 3.2 %collective-permute-start.5 = (f32[32,384]{1,0:T(8,128)S(1)}, f32[32,384]{1,0:T(8,128)S(1)}, u32[]{:S(2)}, u32[]{:S(2)}) collective-permute-start(f32[32,384]{1,0:T(8,128)S(1)} %get-tuple-element.45), channel_id=1, source_target_pairs={{0,4},{1,5},{2,6},{3,7},{4,0},{5,1},{6,2},{7,3},{8,12},{9,13},{10,... | collective-permute-start | bytes 147464 | tf_op jit(solution)/shard_map/ppermute | solution.py:307
  18.6 0.3 collective-permute-start.6
  18.9 1.2 %collective-permute-start.3 = (f32[32,2048]{1,0:T(8,128)S(1)}, f32[32,2048]{1,0:T(8,128)S(1)}, u32[]{:S(2)}, u32[]{:S(2)}) collective-permute-start(f32[32,2048]{1,0:T(8,128)S(1)} %get-tuple-element.43), channel_id=1, source_target_pairs={{0,2},{1,3},{2,4},{3,5},{4,6},{5,7},{6,0},{7,1},{8,10},{9,11},{10,... | collective-permute-start | bytes 786440 | tf_op jit(solution)/shard_map/ppermute | solution.py:307
  20.1 2.1 %collective-permute-start.4 = (f32[32,2048]{1,0:T(8,128)S(1)}, f32[32,2048]{1,0:T(8,128)S(1)}, u32[]{:S(2)}, u32[]{:S(2)}) collective-permute-start(f32[32,2048]{1,0:T(8,128)S(1)} %get-tuple-element.44), channel_id=1, source_target_pairs={{0,6},{1,7},{2,0},{3,1},{4,2},{5,3},{6,4},{7,5},{8,14},{9,15},{10,... | collective-permute-start | bytes 786440 | tf_op jit(solution)/shard_map/ppermute | solution.py:307
  22.2 0.4 collective-permute-done.1.rest_1_
  22.6 1.6 %collective-permute-start.7 = (f32[32,2048]{1,0:T(8,128)S(1)}, f32[32,2048]{1,0:T(8,128)S(1)}, u32[]{:S(2)}, u32[]{:S(2)}) collective-permute-start(f32[32,2048]{1,0:T(8,128)S(1)} %get-tuple-element.47), channel_id=1, source_target_pairs={{0,3},{1,2},{2,5},{3,4},{4,7},{5,6},{6,1},{7,0},{8,11},{9,10},{10,... | collective-permute-start | bytes 786440 | tf_op jit(solution)/shard_map/ppermute | solution.py:307
  24.2 4.2 %collective-permute-start.8 = (f32[32,2048]{1,0:T(8,128)S(1)}, f32[32,2048]{1,0:T(8,128)S(1)}, u32[]{:S(2)}, u32[]{:S(2)}) collective-permute-start(f32[32,2048]{1,0:T(8,128)S(1)} %get-tuple-element.48), channel_id=1, source_target_pairs={{0,7},{1,6},{2,1},{3,0},{4,3},{5,2},{6,5},{7,4},{8,15},{9,14},{10,... | collective-permute-start | bytes 786440 | tf_op jit(solution)/shard_map/ppermute | solution.py:307
  28.4 1.8 %collective-permute-done.3.rest_3_ = f32[32,2048]{1,0:T(8,128)S(1)} collective-permute-done((f32[32,2048]{1,0:T(8,128)S(1)}, f32[32,2048]{1,0:T(8,128)S(1)}, u32[]{:S(2)}, u32[]{:S(2)}) %collective-permute-start.3) | collective-permute-done | bytes 262176 | tf_op jit(solution)/shard_map/ppermute | solution.py:307
  30.2 5.6 %collective-permute-done.7.rest_7_ = f32[32,2048]{1,0:T(8,128)S(1)} collective-permute-done((f32[32,2048]{1,0:T(8,128)S(1)}, f32[32,2048]{1,0:T(8,128)S(1)}, u32[]{:S(2)}, u32[]{:S(2)}) %collective-permute-start.7) | collective-permute-done | bytes 262176 | tf_op jit(solution)/shard_map/ppermute | solution.py:307
  35.8 0.4 collective-permute-done.8.rest_8_
  36.3 4.7 %left_products.1 = (f32[256,768]{1,0:T(8,128)S(1)}, f32[15,32,256]{2,1,0:T(8,128)S(1)}) custom-call(f32[3,256,256]{2,1,0:T(8,128)S(1)} %get-tuple-element.32.c_ref, f32[32,1664]{1,0:T(8,128)S(1)} %collective-permute-done.rest_0_, f32[32,1664]{1,0:T(8,128)S(1)} %collective-permute-done.1.rest_1_, f32[32,1664]{1,0:T(8,128)S(1)} %get-tuple-element.35.rest_2_, ...), custom_call_target="tpu_custom_call" | custom-call | flops 2717908992 | bytes 8388608 | tf_op jit(solution)/shard_map/left_products/pallas_call | solution.py:363
  40.9 4.7 %collective-permute-start.10 = (f32[15,32,256]{2,1,0:T(8,128)S(1)}, f32[15,32,256]{2,1,0:T(8,128)S(1)}, u32[]{:S(2)}, u32[]{:S(2)}) collective-permute-start(f32[15,32,256]{2,1,0:T(8,128)S(1)} %get-tuple-element.51), channel_id=1, source_target_pairs={{0,120},{8,112},{16,104},{24,96},{32,88},{40,80},{48,72},{56,64},{... | collective-permute-start | bytes 1474568 | tf_op jit(solution)/shard_map/ppermute | solution.py:387
  45.6 0.2 pack.1
  45.9 0.0 copy-start.1
  45.9 2.5 %collective-permute-start.11 = (f32[2,136,128]{2,1,0:T(8,128)S(1)}, f32[2,136,128]{2,1,0:T(8,128)S(1)}, u32[]{:S(2)}, u32[]{:S(2)}) collective-permute-start(f32[2,136,128]{2,1,0:T(8,128)S(1)} %get-tuple-element.54), channel_id=1, source_target_pairs={{0,4},{1,5},{2,6},{3,7},{4,0},{5,1},{6,2},{7,3},{8,12},{9,13},{10,... | collective-permute-start | bytes 417800 | tf_op jit(solution)/shard_map/ppermute | solution.py:307
  48.4 0.6 %collective-permute-start.12 = (f32[2,136,128]{2,1,0:T(8,128)S(1)}, f32[2,136,128]{2,1,0:T(8,128)S(1)}, u32[]{:S(2)}, u32[]{:S(2)}) collective-permute-start(f32[2,136,128]{2,1,0:T(8,128)S(1)} %get-tuple-element.55), channel_id=1, source_target_pairs={{0,2},{1,3},{2,4},{3,5},{4,6},{5,7},{6,0},{7,1},{8,10},{9,11},{10,... | collective-permute-start | bytes 417800 | tf_op jit(solution)/shard_map/ppermute | solution.py:307
  49.0 2.0 %collective-permute-start.13 = (f32[2,136,128]{2,1,0:T(8,128)S(1)}, f32[2,136,128]{2,1,0:T(8,128)S(1)}, u32[]{:S(2)}, u32[]{:S(2)}) collective-permute-start(f32[2,136,128]{2,1,0:T(8,128)S(1)} %get-tuple-element.56), channel_id=1, source_target_pairs={{0,6},{1,7},{2,0},{3,1},{4,2},{5,3},{6,4},{7,5},{8,14},{9,15},{10,... | collective-permute-start | bytes 417800 | tf_op jit(solution)/shard_map/ppermute | solution.py:307
  51.1 1.5 %collective-permute-done.11.rest_1_ = f32[2,136,128]{2,1,0:T(8,128)S(1)} collective-permute-done((f32[2,136,128]{2,1,0:T(8,128)S(1)}, f32[2,136,128]{2,1,0:T(8,128)S(1)}, u32[]{:S(2)}, u32[]{:S(2)}) %collective-permute-start.11) | collective-permute-done | bytes 139296 | tf_op jit(solution)/shard_map/ppermute | solution.py:307
  52.6 2.9 %collective-permute-done.12.rest_2_ = f32[2,136,128]{2,1,0:T(8,128)S(1)} collective-permute-done((f32[2,136,128]{2,1,0:T(8,128)S(1)}, f32[2,136,128]{2,1,0:T(8,128)S(1)}, u32[]{:S(2)}, u32[]{:S(2)}) %collective-permute-start.12) | collective-permute-done | bytes 139296 | tf_op jit(solution)/shard_map/ppermute | solution.py:307
  55.6 1.2 %collective-permute-start.14 = (f32[4,136,128]{2,1,0:T(8,128)S(1)}, f32[4,136,128]{2,1,0:T(8,128)S(1)}, u32[]{:S(2)}, u32[]{:S(2)}) collective-permute-start(f32[4,136,128]{2,1,0:T(8,128)S(1)} %pad_maximum_fusion), channel_id=1, source_target_pairs={{0,1},{1,0},{2,3},{3,2},{4,5},{5,4},{6,7},{7,6},{8,9},{9,8},{10,11... | collective-permute-start | bytes 835592 | tf_op jit(solution)/shard_map/ppermute | solution.py:307
  56.8 0.5 collective-permute-done.10.mirror_ref
  57.2 0.1 join_mirror.1.mirror_ref
  57.3 0.6 %collective-permute-done.14.rest_4_ = f32[4,136,128]{2,1,0:T(8,128)S(1)} collective-permute-done((f32[4,136,128]{2,1,0:T(8,128)S(1)}, f32[4,136,128]{2,1,0:T(8,128)S(1)}, u32[]{:S(2)}, u32[]{:S(2)}) %collective-permute-start.14) | collective-permute-done | bytes 278560 | tf_op jit(solution)/shard_map/ppermute | solution.py:307
  57.9 1.5 %join.1 = f32[32,32,256]{2,1,0:T(8,128)} custom-call(f32[32,32,256]{2,1,0:T(8,128)S(1)} %copy-done.1, f32[15,32,256]{2,1,0:T(8,128)S(1)} %join_mirror.1.mirror_ref, f32[2,136,128]{2,1,0:T(8,128)S(1)} %get-tuple-element.53.rest_0_, f32[2,136,128]{2,1,0:T(8,128)S(1)} %collective-permute-done.11.rest_1_, f32[2,136,128]{2,1,0:T(8,128)S(1)} %collective-permute-done.12.rest_2_, ...), custom_call_target="tpu_custom_call" | custom-call | tf_op jit(solution)/shard_map/join/pallas_call | solution.py:398
  (18 shorter events, 0.1 us)
Async XLA Ops:
  0.0 1.2 %copy-start = (f32[32,32,256]{2,1,0:T(8,128)S(1)}, f32[32,32,256]{2,1,0:T(8,128)}, u32[]{:S(2)}) copy-start(f32[32,32,256]{2,1,0:T(8,128)} %n_ref.5) | copy-start | bytes 3145732
  1.2 2.3 %copy-start.2 = (f32[3,256,256]{2,1,0:T(8,128)S(1)}, f32[3,256,256]{2,1,0:T(8,128)}, u32[]{:S(2)}) copy-start(f32[3,256,256]{2,1,0:T(8,128)} %c_ref.1) | copy-start | bytes 2359300
  1.3 2.2 %copy-start.3 = (s32[3]{0:T(128)S(1)}, s32[3]{0:T(128)}, u32[]{:S(2)}) copy-start(s32[3]{0:T(128)} %shift_ref.1) | copy-start | bytes 40
  1.3 11.7 %collective-permute-start.2 = (f32[6,32,256]{2,1,0:T(8,128)S(1)}, f32[6,32,256]{2,1,0:T(8,128)S(1)}, u32[]{:S(2)}, u32[]{:S(2)}) collective-permute-start(f32[6,32,256]{2,1,0:T(8,128)S(1)} %get-tuple-element.36), channel_id=1, source_target_pairs={{0,8},{8,16},{16,24},{24,32},{32,40},{40,48},{48,56},{56,64},{64,7... | collective-permute-start | bytes 589832 | tf_op jit(solution)/shard_map/ppermute | solution.py:337
  8.4 11.7 %collective-permute-start = (f32[32,1664]{1,0:T(8,128)S(1)}, f32[32,1664]{1,0:T(8,128)S(1)}, u32[]{:S(2)}, u32[]{:S(2)}) collective-permute-start(f32[32,1664]{1,0:T(8,128)S(1)} %get-tuple-element.33), channel_id=1, source_target_pairs={{0,4},{1,5},{2,6},{3,7},{4,0},{5,1},{6,2},{7,3},{8,12},{9,13},{10,... | collective-permute-start | bytes 638984 | tf_op jit(solution)/shard_map/ppermute | solution.py:307
  12.1 10.5 %collective-permute-start.1 = (f32[32,1664]{1,0:T(8,128)S(1)}, f32[32,1664]{1,0:T(8,128)S(1)}, u32[]{:S(2)}, u32[]{:S(2)}) collective-permute-start(f32[32,1664]{1,0:T(8,128)S(1)} %get-tuple-element.34), channel_id=1, source_target_pairs={{0,5},{1,4},{2,7},{3,6},{4,1},{5,0},{6,3},{7,2},{8,13},{9,12},{10,... | collective-permute-start | bytes 638984 | tf_op jit(solution)/shard_map/ppermute | solution.py:307
  15.3 8.9 %collective-permute-start.5 = (f32[32,384]{1,0:T(8,128)S(1)}, f32[32,384]{1,0:T(8,128)S(1)}, u32[]{:S(2)}, u32[]{:S(2)}) collective-permute-start(f32[32,384]{1,0:T(8,128)S(1)} %get-tuple-element.45), channel_id=1, source_target_pairs={{0,4},{1,5},{2,6},{3,7},{4,0},{5,1},{6,2},{7,3},{8,12},{9,13},{10,... | collective-permute-start | bytes 147464 | tf_op jit(solution)/shard_map/ppermute | solution.py:307
  18.6 9.9 %collective-permute-start.6 = (f32[32,384]{1,0:T(8,128)S(1)}, f32[32,384]{1,0:T(8,128)S(1)}, u32[]{:S(2)}, u32[]{:S(2)}) collective-permute-start(f32[32,384]{1,0:T(8,128)S(1)} %get-tuple-element.46), channel_id=1, source_target_pairs={{0,5},{1,4},{2,7},{3,6},{4,1},{5,0},{6,3},{7,2},{8,13},{9,12},{10,... | collective-permute-start | bytes 147464 | tf_op jit(solution)/shard_map/ppermute | solution.py:307
  18.9 11.3 %collective-permute-start.3 = (f32[32,2048]{1,0:T(8,128)S(1)}, f32[32,2048]{1,0:T(8,128)S(1)}, u32[]{:S(2)}, u32[]{:S(2)}) collective-permute-start(f32[32,2048]{1,0:T(8,128)S(1)} %get-tuple-element.43), channel_id=1, source_target_pairs={{0,2},{1,3},{2,4},{3,5},{4,6},{5,7},{6,0},{7,1},{8,10},{9,11},{10,... | collective-permute-start | bytes 786440 | tf_op jit(solution)/shard_map/ppermute | solution.py:307
  20.1 10.1 %collective-permute-start.4 = (f32[32,2048]{1,0:T(8,128)S(1)}, f32[32,2048]{1,0:T(8,128)S(1)}, u32[]{:S(2)}, u32[]{:S(2)}) collective-permute-start(f32[32,2048]{1,0:T(8,128)S(1)} %get-tuple-element.44), channel_id=1, source_target_pairs={{0,6},{1,7},{2,0},{3,1},{4,2},{5,3},{6,4},{7,5},{8,14},{9,15},{10,... | collective-permute-start | bytes 786440 | tf_op jit(solution)/shard_map/ppermute | solution.py:307
  22.6 13.2 %collective-permute-start.7 = (f32[32,2048]{1,0:T(8,128)S(1)}, f32[32,2048]{1,0:T(8,128)S(1)}, u32[]{:S(2)}, u32[]{:S(2)}) collective-permute-start(f32[32,2048]{1,0:T(8,128)S(1)} %get-tuple-element.47), channel_id=1, source_target_pairs={{0,3},{1,2},{2,5},{3,4},{4,7},{5,6},{6,1},{7,0},{8,11},{9,10},{10,... | collective-permute-start | bytes 786440 | tf_op jit(solution)/shard_map/ppermute | solution.py:307
  24.2 12.0 %collective-permute-start.8 = (f32[32,2048]{1,0:T(8,128)S(1)}, f32[32,2048]{1,0:T(8,128)S(1)}, u32[]{:S(2)}, u32[]{:S(2)}) collective-permute-start(f32[32,2048]{1,0:T(8,128)S(1)} %get-tuple-element.48), channel_id=1, source_target_pairs={{0,7},{1,6},{2,1},{3,0},{4,3},{5,2},{6,5},{7,4},{8,15},{9,14},{10,... | collective-permute-start | bytes 786440 | tf_op jit(solution)/shard_map/ppermute | solution.py:307
  28.4 7.9 %collective-permute-start.9 = (f32[32,2048]{1,0:T(8,128)S(1)}, f32[32,2048]{1,0:T(8,128)S(1)}, u32[]{:S(2)}, u32[]{:S(2)}) collective-permute-start(f32[32,2048]{1,0:T(8,128)S(1)} %get-tuple-element.49), channel_id=1, source_target_pairs={{0,1},{1,0},{2,3},{3,2},{4,5},{5,4},{6,7},{7,6},{8,9},{9,8},{10,11... | collective-permute-start | bytes 786440 | tf_op jit(solution)/shard_map/ppermute | solution.py:307
  40.9 16.3 %collective-permute-start.10 = (f32[15,32,256]{2,1,0:T(8,128)S(1)}, f32[15,32,256]{2,1,0:T(8,128)S(1)}, u32[]{:S(2)}, u32[]{:S(2)}) collective-permute-start(f32[15,32,256]{2,1,0:T(8,128)S(1)} %get-tuple-element.51), channel_id=1, source_target_pairs={{0,120},{8,112},{16,104},{24,96},{32,88},{40,80},{48,72},{56,64},{... | collective-permute-start | bytes 1474568 | tf_op jit(solution)/shard_map/ppermute | solution.py:387
  45.9 11.4 %copy-start.1 = (f32[32,32,256]{2,1,0:T(8,128)S(1)}, f32[32,32,256]{2,1,0:T(8,128)}, u32[]{:S(2)}) copy-start(f32[32,32,256]{2,1,0:T(8,128)} %n_ref.5) | copy-start | bytes 3145732
  45.9 6.7 %collective-permute-start.11 = (f32[2,136,128]{2,1,0:T(8,128)S(1)}, f32[2,136,128]{2,1,0:T(8,128)S(1)}, u32[]{:S(2)}, u32[]{:S(2)}) collective-permute-start(f32[2,136,128]{2,1,0:T(8,128)S(1)} %get-tuple-element.54), channel_id=1, source_target_pairs={{0,4},{1,5},{2,6},{3,7},{4,0},{5,1},{6,2},{7,3},{8,12},{9,13},{10,... | collective-permute-start | bytes 417800 | tf_op jit(solution)/shard_map/ppermute | solution.py:307
  48.4 7.1 %collective-permute-start.12 = (f32[2,136,128]{2,1,0:T(8,128)S(1)}, f32[2,136,128]{2,1,0:T(8,128)S(1)}, u32[]{:S(2)}, u32[]{:S(2)}) collective-permute-start(f32[2,136,128]{2,1,0:T(8,128)S(1)} %get-tuple-element.55), channel_id=1, source_target_pairs={{0,2},{1,3},{2,4},{3,5},{4,6},{5,7},{6,0},{7,1},{8,10},{9,11},{10,... | collective-permute-start | bytes 417800 | tf_op jit(solution)/shard_map/ppermute | solution.py:307
  49.0 6.5 %collective-permute-start.13 = (f32[2,136,128]{2,1,0:T(8,128)S(1)}, f32[2,136,128]{2,1,0:T(8,128)S(1)}, u32[]{:S(2)}, u32[]{:S(2)}) collective-permute-start(f32[2,136,128]{2,1,0:T(8,128)S(1)} %get-tuple-element.56), channel_id=1, source_target_pairs={{0,6},{1,7},{2,0},{3,1},{4,2},{5,3},{6,4},{7,5},{8,14},{9,15},{10,... | collective-permute-start | bytes 417800 | tf_op jit(solution)/shard_map/ppermute | solution.py:307
  55.6 2.3 %collective-permute-start.14 = (f32[4,136,128]{2,1,0:T(8,128)S(1)}, f32[4,136,128]{2,1,0:T(8,128)S(1)}, u32[]{:S(2)}, u32[]{:S(2)}) collective-permute-start(f32[4,136,128]{2,1,0:T(8,128)S(1)} %pad_maximum_fusion), channel_id=1, source_target_pairs={{0,1},{1,0},{2,3},{3,2},{4,5},{5,4},{6,7},{7,6},{8,9},{9,8},{10,11... | collective-permute-start | bytes 835592 | tf_op jit(solution)/shard_map/ppermute | solution.py:307

commit v5 on v4

--- a/solution.py
+++ b/solution.py
@@ -48,7 +48,7 @@
 WHERE = {entry: (m, p) for m, tile in enumerate(LOCAL + HALOS) for p, entry in enumerate(tile) if entry}
 RESULT = [[5, 3, 9, 15], [11, 4, 10, 16], [0, 6, 12, 2], [1, 7, 13, 8]]
 LAST = 14
-DISTANCES = (0, 2, 1, 3)
+DISTANCES = (0, 1, 3, 2)
 OUT_ROWS = R * len(RESULT) + 8
 LOCAL_LANES = 128 * len(LOCAL)
 HALO_LANES = 128 * len(HALOS)

time: 59.5 us -> 60.1 us (1.010)
  waiting for transfers between devices: 13.8 us -> 15.3 us
  starting transfers between devices: 30.6 us -> 29.7 us
    ppermute x13, waiting for transfers between devices: 13.3 us -> 15.3 us  [send(): return lax.ppermute(array, 'col', pairs)]
    ppermute x13, starting transfers between devices: 23.7 us -> 22.8 us  [send(): return lax.ppermute(array, 'col', pairs)]
  transfers between devices with their start and end apart: 15 -> 15, of which waited for: 8 -> 7; matrix products, arithmetic and copies ran while one was open for 0% -> 0% of each run, Pallas kernels for 13% -> 12%
where the time goes in v5:
time: 60.1 us; the launch traced here: 60 us
  starting transfers between devices  29.7 us (49%)
  waiting for transfers between devices  15.3 us (25%)
  Pallas kernels  13.7 us (23%)
  local copies, waits for them, and re-layouts  1.26 us (2%)
    ppermute x13, starting transfers between devices, send(): return lax.ppermute(array, 'col', pairs)  22.8 us
    ppermute x13, waiting for transfers between devices, send(): return lax.ppermute(array, 'col', pairs)  15.3 us
    pallas_call x1, Pallas kernels, body(): pl.pallas_call(local_kernel, out_shape=[jax.ShapeDtypeStruct((R, LOCAL_LA...  4.93 us
    ppermute x1, starting transfers between devices, body(): mirror = lax.ppermute(mirror, 'off', [(o, 15 - o) for o in range(16)])  4.69 us
    pallas_call x1, Pallas kernels, body(): pl.pallas_call(left_kernel, out_shape=[jax.ShapeDtypeStruct((N, 128 * GRI...  4.65 us
    pallas_call x1, Pallas kernels, body(): pl.pallas_call(halo_kernel, out_shape=[jax.ShapeDtypeStruct((R, HALO_LANE...  2.27 us
    ppermute x1, starting transfers between devices, body(): halo = lax.ppermute(edge, 'off', [(o, (o + 1) % 16) for o in range(16)])  2.19 us
    pallas_call x1, Pallas kernels, body(): pl.pallas_call(join_kernel, out_shape=jax.ShapeDtypeStruct((R, R, N), f32...  1.46 us
  transfers between devices with their start and end apart: 15, of which 7 were waited for; matrix products, arithmetic and copies ran while one was open for 0% of the time, Pallas kernels for 12%

profile of v5, /device:TPU:1, one launch (start us, length us, event | category | flops | bytes accessed | tf_op | source)
XLA Modules:
  0.0 60.0 jit_solution(16688030986905236497)
XLA Ops:
  0.0 1.2 %copy-done = f32[32,32,256]{2,1,0:T(8,128)S(1)} copy-done((f32[32,32,256]{2,1,0:T(8,128)S(1)}, f32[32,32,256]{2,1,0:T(8,128)}, u32[]{:S(2)}) %copy-start) | copy-done | bytes 1048600
  1.2 0.1 edge.1
  1.3 0.0 copy-start.3
  1.3 2.2 %collective-permute-start.2 = (f32[6,32,256]{2,1,0:T(8,128)S(1)}, f32[6,32,256]{2,1,0:T(8,128)S(1)}, u32[]{:S(2)}, u32[]{:S(2)}) collective-permute-start(f32[6,32,256]{2,1,0:T(8,128)S(1)} %get-tuple-element.36), channel_id=1, source_target_pairs={{0,8},{8,16},{16,24},{24,32},{32,40},{40,48},{48,56},{56,64},{64,7... | collective-permute-start | bytes 589832 | tf_op jit(solution)/shard_map/ppermute | solution.py:337
  3.5 4.9 %local_right_products.1 = (f32[32,1664]{1,0:T(8,128)S(1)}, f32[32,1664]{1,0:T(8,128)S(1)}, f32[32,1664]{1,0:T(8,128)S(1)}, f32[32,1664]{1,0:T(8,128)S(1)}, f32[3...) custom-call(s32[3]{0:T(128)S(1)} %copy-done.3, ...), custom_call_target="tpu_custom_call" | custom-call | flops 2151677952 | bytes 4194304 | tf_op jit(solution)/shard_map/local_right_products/pallas_call | solution.py:338
  8.4 3.7 %collective-permute-start = (f32[32,1664]{1,0:T(8,128)S(1)}, f32[32,1664]{1,0:T(8,128)S(1)}, u32[]{:S(2)}, u32[]{:S(2)}) collective-permute-start(f32[32,1664]{1,0:T(8,128)S(1)} %get-tuple-element.33), channel_id=1, source_target_pairs={{0,4},{1,5},{2,6},{3,7},{4,0},{5,1},{6,2},{7,3},{8,12},{9,13},{10,... | collective-permute-start | bytes 638984 | tf_op jit(solution)/shard_map/ppermute | solution.py:307
  12.1 0.9 %collective-permute-start.1 = (f32[32,1664]{1,0:T(8,128)S(1)}, f32[32,1664]{1,0:T(8,128)S(1)}, u32[]{:S(2)}, u32[]{:S(2)}) collective-permute-start(f32[32,1664]{1,0:T(8,128)S(1)} %get-tuple-element.34), channel_id=1, source_target_pairs={{0,5},{1,4},{2,7},{3,6},{4,1},{5,0},{6,3},{7,2},{8,13},{9,12},{10,... | collective-permute-start | bytes 638984 | tf_op jit(solution)/shard_map/ppermute | solution.py:307
  13.1 0.0 collective-permute-done.2.halo_ref
  13.1 2.3 %halo_right_products.1 = (f32[32,2048]{1,0:T(8,128)S(1)}, f32[32,2048]{1,0:T(8,128)S(1)}, f32[32,384]{1,0:T(8,128)S(1)}, f32[32,384]{1,0:T(8,128)S(1)}, f32[32,2...) custom-call(f32[6,32,256]{2,1,0:T(8,128)S(1)} %collective-permute-done.2.halo_ref, ...), custom_call_target="tpu_custom_call" | custom-call | flops 377487360 | bytes 2097152 | tf_op jit(solution)/shard_map/halo_right_products/pallas_call | solution.py:350
  15.3 3.2 %collective-permute-start.5 = (f32[32,384]{1,0:T(8,128)S(1)}, f32[32,384]{1,0:T(8,128)S(1)}, u32[]{:S(2)}, u32[]{:S(2)}) collective-permute-start(f32[32,384]{1,0:T(8,128)S(1)} %get-tuple-element.45), channel_id=1, source_target_pairs={{0,4},{1,5},{2,6},{3,7},{4,0},{5,1},{6,2},{7,3},{8,12},{9,13},{10,... | collective-permute-start | bytes 147464 | tf_op jit(solution)/shard_map/ppermute | solution.py:307
  18.6 0.3 collective-permute-start.6
  18.9 1.2 %collective-permute-start.3 = (f32[32,2048]{1,0:T(8,128)S(1)}, f32[32,2048]{1,0:T(8,128)S(1)}, u32[]{:S(2)}, u32[]{:S(2)}) collective-permute-start(f32[32,2048]{1,0:T(8,128)S(1)} %get-tuple-element.43), channel_id=1, source_target_pairs={{0,2},{1,3},{2,4},{3,5},{4,6},{5,7},{6,0},{7,1},{8,10},{9,11},{10,... | collective-permute-start | bytes 786440 | tf_op jit(solution)/shard_map/ppermute | solution.py:307
  20.1 2.1 %collective-permute-start.4 = (f32[32,2048]{1,0:T(8,128)S(1)}, f32[32,2048]{1,0:T(8,128)S(1)}, u32[]{:S(2)}, u32[]{:S(2)}) collective-permute-start(f32[32,2048]{1,0:T(8,128)S(1)} %get-tuple-element.44), channel_id=1, source_target_pairs={{0,6},{1,7},{2,0},{3,1},{4,2},{5,3},{6,4},{7,5},{8,14},{9,15},{10,... | collective-permute-start | bytes 786440 | tf_op jit(solution)/shard_map/ppermute | solution.py:307
  22.2 0.4 collective-permute-done.1.rest_1_
  22.6 1.6 %collective-permute-start.7 = (f32[32,2048]{1,0:T(8,128)S(1)}, f32[32,2048]{1,0:T(8,128)S(1)}, u32[]{:S(2)}, u32[]{:S(2)}) collective-permute-start(f32[32,2048]{1,0:T(8,128)S(1)} %get-tuple-element.47), channel_id=1, source_target_pairs={{0,3},{1,2},{2,5},{3,4},{4,7},{5,6},{6,1},{7,0},{8,11},{9,10},{10,... | collective-permute-start | bytes 786440 | tf_op jit(solution)/shard_map/ppermute | solution.py:307
  24.2 4.2 %collective-permute-start.8 = (f32[32,2048]{1,0:T(8,128)S(1)}, f32[32,2048]{1,0:T(8,128)S(1)}, u32[]{:S(2)}, u32[]{:S(2)}) collective-permute-start(f32[32,2048]{1,0:T(8,128)S(1)} %get-tuple-element.48), channel_id=1, source_target_pairs={{0,7},{1,6},{2,1},{3,0},{4,3},{5,2},{6,5},{7,4},{8,15},{9,14},{10,... | collective-permute-start | bytes 786440 | tf_op jit(solution)/shard_map/ppermute | solution.py:307
  28.4 1.8 %collective-permute-done.3.rest_3_ = f32[32,2048]{1,0:T(8,128)S(1)} collective-permute-done((f32[32,2048]{1,0:T(8,128)S(1)}, f32[32,2048]{1,0:T(8,128)S(1)}, u32[]{:S(2)}, u32[]{:S(2)}) %collective-permute-start.3) | collective-permute-done | bytes 262176 | tf_op jit(solution)/shard_map/ppermute | solution.py:307
  30.2 5.6 %collective-permute-done.7.rest_7_ = f32[32,2048]{1,0:T(8,128)S(1)} collective-permute-done((f32[32,2048]{1,0:T(8,128)S(1)}, f32[32,2048]{1,0:T(8,128)S(1)}, u32[]{:S(2)}, u32[]{:S(2)}) %collective-permute-start.7) | collective-permute-done | bytes 262176 | tf_op jit(solution)/shard_map/ppermute | solution.py:307
  35.8 0.4 collective-permute-done.8.rest_8_
  36.3 4.7 %left_products.1 = (f32[256,768]{1,0:T(8,128)S(1)}, f32[15,32,256]{2,1,0:T(8,128)S(1)}) custom-call(f32[3,256,256]{2,1,0:T(8,128)S(1)} %get-tuple-element.32.c_ref, f32[32,1664]{1,0:T(8,128)S(1)} %collective-permute-done.rest_0_, f32[32,1664]{1,0:T(8,128)S(1)} %collective-permute-done.1.rest_1_, f32[32,1664]{1,0:T(8,128)S(1)} %get-tuple-element.35.rest_2_, ...), custom_call_target="tpu_custom_call" | custom-call | flops 2717908992 | bytes 8388608 | tf_op jit(solution)/shard_map/left_products/pallas_call | solution.py:363
  40.9 4.7 %collective-permute-start.10 = (f32[15,32,256]{2,1,0:T(8,128)S(1)}, f32[15,32,256]{2,1,0:T(8,128)S(1)}, u32[]{:S(2)}, u32[]{:S(2)}) collective-permute-start(f32[15,32,256]{2,1,0:T(8,128)S(1)} %get-tuple-element.51), channel_id=1, source_target_pairs={{0,120},{8,112},{16,104},{24,96},{32,88},{40,80},{48,72},{56,64},{... | collective-permute-start | bytes 1474568 | tf_op jit(solution)/shard_map/ppermute | solution.py:387
  45.6 0.2 pack.1
  45.9 0.0 copy-start.1
  45.9 0.9 %collective-permute-start.11 = (f32[2,136,128]{2,1,0:T(8,128)S(1)}, f32[2,136,128]{2,1,0:T(8,128)S(1)}, u32[]{:S(2)}, u32[]{:S(2)}) collective-permute-start(f32[2,136,128]{2,1,0:T(8,128)S(1)} %get-tuple-element.54), channel_id=1, source_target_pairs={{0,2},{1,3},{2,4},{3,5},{4,6},{5,7},{6,0},{7,1},{8,10},{9,11},{10,... | collective-permute-start | bytes 417800 | tf_op jit(solution)/shard_map/ppermute | solution.py:307
  46.8 1.9 %collective-permute-start.12 = (f32[2,136,128]{2,1,0:T(8,128)S(1)}, f32[2,136,128]{2,1,0:T(8,128)S(1)}, u32[]{:S(2)}, u32[]{:S(2)}) collective-permute-start(f32[2,136,128]{2,1,0:T(8,128)S(1)} %get-tuple-element.55), channel_id=1, source_target_pairs={{0,6},{1,7},{2,0},{3,1},{4,2},{5,3},{6,4},{7,5},{8,14},{9,15},{10,... | collective-permute-start | bytes 417800 | tf_op jit(solution)/shard_map/ppermute | solution.py:307
  48.6 1.2 %collective-permute-start.13 = (f32[2,136,128]{2,1,0:T(8,128)S(1)}, f32[2,136,128]{2,1,0:T(8,128)S(1)}, u32[]{:S(2)}, u32[]{:S(2)}) collective-permute-start(f32[2,136,128]{2,1,0:T(8,128)S(1)} %get-tuple-element.56), channel_id=1, source_target_pairs={{0,4},{1,5},{2,6},{3,7},{4,0},{5,1},{6,2},{7,3},{8,12},{9,13},{10,... | collective-permute-start | bytes 417800 | tf_op jit(solution)/shard_map/ppermute | solution.py:307
  49.9 2.4 %collective-permute-done.11.rest_1_ = f32[2,136,128]{2,1,0:T(8,128)S(1)} collective-permute-done((f32[2,136,128]{2,1,0:T(8,128)S(1)}, f32[2,136,128]{2,1,0:T(8,128)S(1)}, u32[]{:S(2)}, u32[]{:S(2)}) %collective-permute-start.11) | collective-permute-done | bytes 139296 | tf_op jit(solution)/shard_map/ppermute | solution.py:307
  52.3 3.5 %collective-permute-done.13.rest_3_ = f32[2,136,128]{2,1,0:T(8,128)S(1)} collective-permute-done((f32[2,136,128]{2,1,0:T(8,128)S(1)}, f32[2,136,128]{2,1,0:T(8,128)S(1)}, u32[]{:S(2)}, u32[]{:S(2)}) %collective-permute-start.13) | collective-permute-done | bytes 139296 | tf_op jit(solution)/shard_map/ppermute | solution.py:307
  55.8 1.5 %collective-permute-start.14 = (f32[4,136,128]{2,1,0:T(8,128)S(1)}, f32[4,136,128]{2,1,0:T(8,128)S(1)}, u32[]{:S(2)}, u32[]{:S(2)}) collective-permute-start(f32[4,136,128]{2,1,0:T(8,128)S(1)} %pad_maximum_fusion), channel_id=1, source_target_pairs={{0,1},{1,0},{2,3},{3,2},{4,5},{5,4},{6,7},{7,6},{8,9},{9,8},{10,11... | collective-permute-start | bytes 835592 | tf_op jit(solution)/shard_map/ppermute | solution.py:307
  57.4 0.1 join_mirror.1.mirror_ref
  57.4 1.1 %collective-permute-done.14.rest_4_ = f32[4,136,128]{2,1,0:T(8,128)S(1)} collective-permute-done((f32[4,136,128]{2,1,0:T(8,128)S(1)}, f32[4,136,128]{2,1,0:T(8,128)S(1)}, u32[]{:S(2)}, u32[]{:S(2)}) %collective-permute-start.14) | collective-permute-done | bytes 278560 | tf_op jit(solution)/shard_map/ppermute | solution.py:307
  58.5 1.5 %join.1 = f32[32,32,256]{2,1,0:T(8,128)} custom-call(f32[32,32,256]{2,1,0:T(8,128)S(1)} %copy-done.1, f32[15,32,256]{2,1,0:T(8,128)S(1)} %join_mirror.1.mirror_ref, f32[2,136,128]{2,1,0:T(8,128)S(1)} %get-tuple-element.53.rest_0_, f32[2,136,128]{2,1,0:T(8,128)S(1)} %collective-permute-done.11.rest_1_, f32[2,136,128]{2,1,0:T(8,128)S(1)} %collective-permute-done.12.rest_2_, ...), custom_call_target="tpu_custom_call" | custom-call | tf_op jit(solution)/shard_map/join/pallas_call | solution.py:398
  (18 shorter events, 0.1 us)
Async XLA Ops:
  0.0 1.2 %copy-start = (f32[32,32,256]{2,1,0:T(8,128)S(1)}, f32[32,32,256]{2,1,0:T(8,128)}, u32[]{:S(2)}) copy-start(f32[32,32,256]{2,1,0:T(8,128)} %n_ref.5) | copy-start | bytes 3145732
  1.2 2.3 %copy-start.2 = (f32[3,256,256]{2,1,0:T(8,128)S(1)}, f32[3,256,256]{2,1,0:T(8,128)}, u32[]{:S(2)}) copy-start(f32[3,256,256]{2,1,0:T(8,128)} %c_ref.1) | copy-start | bytes 2359300
  1.3 2.2 %copy-start.3 = (s32[3]{0:T(128)S(1)}, s32[3]{0:T(128)}, u32[]{:S(2)}) copy-start(s32[3]{0:T(128)} %shift_ref.1) | copy-start | bytes 40
  1.3 11.7 %collective-permute-start.2 = (f32[6,32,256]{2,1,0:T(8,128)S(1)}, f32[6,32,256]{2,1,0:T(8,128)S(1)}, u32[]{:S(2)}, u32[]{:S(2)}) collective-permute-start(f32[6,32,256]{2,1,0:T(8,128)S(1)} %get-tuple-element.36), channel_id=1, source_target_pairs={{0,8},{8,16},{16,24},{24,32},{32,40},{40,48},{48,56},{56,64},{64,7... | collective-permute-start | bytes 589832 | tf_op jit(solution)/shard_map/ppermute | solution.py:337
  8.4 11.7 %collective-permute-start = (f32[32,1664]{1,0:T(8,128)S(1)}, f32[32,1664]{1,0:T(8,128)S(1)}, u32[]{:S(2)}, u32[]{:S(2)}) collective-permute-start(f32[32,1664]{1,0:T(8,128)S(1)} %get-tuple-element.33), channel_id=1, source_target_pairs={{0,4},{1,5},{2,6},{3,7},{4,0},{5,1},{6,2},{7,3},{8,12},{9,13},{10,... | collective-permute-start | bytes 638984 | tf_op jit(solution)/shard_map/ppermute | solution.py:307
  12.1 10.5 %collective-permute-start.1 = (f32[32,1664]{1,0:T(8,128)S(1)}, f32[32,1664]{1,0:T(8,128)S(1)}, u32[]{:S(2)}, u32[]{:S(2)}) collective-permute-start(f32[32,1664]{1,0:T(8,128)S(1)} %get-tuple-element.34), channel_id=1, source_target_pairs={{0,5},{1,4},{2,7},{3,6},{4,1},{5,0},{6,3},{7,2},{8,13},{9,12},{10,... | collective-permute-start | bytes 638984 | tf_op jit(solution)/shard_map/ppermute | solution.py:307
  15.3 8.9 %collective-permute-start.5 = (f32[32,384]{1,0:T(8,128)S(1)}, f32[32,384]{1,0:T(8,128)S(1)}, u32[]{:S(2)}, u32[]{:S(2)}) collective-permute-start(f32[32,384]{1,0:T(8,128)S(1)} %get-tuple-element.45), channel_id=1, source_target_pairs={{0,4},{1,5},{2,6},{3,7},{4,0},{5,1},{6,2},{7,3},{8,12},{9,13},{10,... | collective-permute-start | bytes 147464 | tf_op jit(solution)/shard_map/ppermute | solution.py:307
  18.6 9.9 %collective-permute-start.6 = (f32[32,384]{1,0:T(8,128)S(1)}, f32[32,384]{1,0:T(8,128)S(1)}, u32[]{:S(2)}, u32[]{:S(2)}) collective-permute-start(f32[32,384]{1,0:T(8,128)S(1)} %get-tuple-element.46), channel_id=1, source_target_pairs={{0,5},{1,4},{2,7},{3,6},{4,1},{5,0},{6,3},{7,2},{8,13},{9,12},{10,... | collective-permute-start | bytes 147464 | tf_op jit(solution)/shard_map/ppermute | solution.py:307
  18.9 11.3 %collective-permute-start.3 = (f32[32,2048]{1,0:T(8,128)S(1)}, f32[32,2048]{1,0:T(8,128)S(1)}, u32[]{:S(2)}, u32[]{:S(2)}) collective-permute-start(f32[32,2048]{1,0:T(8,128)S(1)} %get-tuple-element.43), channel_id=1, source_target_pairs={{0,2},{1,3},{2,4},{3,5},{4,6},{5,7},{6,0},{7,1},{8,10},{9,11},{10,... | collective-permute-start | bytes 786440 | tf_op jit(solution)/shard_map/ppermute | solution.py:307
  20.1 10.1 %collective-permute-start.4 = (f32[32,2048]{1,0:T(8,128)S(1)}, f32[32,2048]{1,0:T(8,128)S(1)}, u32[]{:S(2)}, u32[]{:S(2)}) collective-permute-start(f32[32,2048]{1,0:T(8,128)S(1)} %get-tuple-element.44), channel_id=1, source_target_pairs={{0,6},{1,7},{2,0},{3,1},{4,2},{5,3},{6,4},{7,5},{8,14},{9,15},{10,... | collective-permute-start | bytes 786440 | tf_op jit(solution)/shard_map/ppermute | solution.py:307
  22.6 13.2 %collective-permute-start.7 = (f32[32,2048]{1,0:T(8,128)S(1)}, f32[32,2048]{1,0:T(8,128)S(1)}, u32[]{:S(2)}, u32[]{:S(2)}) collective-permute-start(f32[32,2048]{1,0:T(8,128)S(1)} %get-tuple-element.47), channel_id=1, source_target_pairs={{0,3},{1,2},{2,5},{3,4},{4,7},{5,6},{6,1},{7,0},{8,11},{9,10},{10,... | collective-permute-start | bytes 786440 | tf_op jit(solution)/shard_map/ppermute | solution.py:307
  24.2 12.0 %collective-permute-start.8 = (f32[32,2048]{1,0:T(8,128)S(1)}, f32[32,2048]{1,0:T(8,128)S(1)}, u32[]{:S(2)}, u32[]{:S(2)}) collective-permute-start(f32[32,2048]{1,0:T(8,128)S(1)} %get-tuple-element.48), channel_id=1, source_target_pairs={{0,7},{1,6},{2,1},{3,0},{4,3},{5,2},{6,5},{7,4},{8,15},{9,14},{10,... | collective-permute-start | bytes 786440 | tf_op jit(solution)/shard_map/ppermute | solution.py:307
  28.4 7.9 %collective-permute-start.9 = (f32[32,2048]{1,0:T(8,128)S(1)}, f32[32,2048]{1,0:T(8,128)S(1)}, u32[]{:S(2)}, u32[]{:S(2)}) collective-permute-start(f32[32,2048]{1,0:T(8,128)S(1)} %get-tuple-element.49), channel_id=1, source_target_pairs={{0,1},{1,0},{2,3},{3,2},{4,5},{5,4},{6,7},{7,6},{8,9},{9,8},{10,11... | collective-permute-start | bytes 786440 | tf_op jit(solution)/shard_map/ppermute | solution.py:307
  40.9 16.4 %collective-permute-start.10 = (f32[15,32,256]{2,1,0:T(8,128)S(1)}, f32[15,32,256]{2,1,0:T(8,128)S(1)}, u32[]{:S(2)}, u32[]{:S(2)}) collective-permute-start(f32[15,32,256]{2,1,0:T(8,128)S(1)} %get-tuple-element.51), channel_id=1, source_target_pairs={{0,120},{8,112},{16,104},{24,96},{32,88},{40,80},{48,72},{56,64},{... | collective-permute-start | bytes 1474568 | tf_op jit(solution)/shard_map/ppermute | solution.py:387
  45.9 11.5 %copy-start.1 = (f32[32,32,256]{2,1,0:T(8,128)S(1)}, f32[32,32,256]{2,1,0:T(8,128)}, u32[]{:S(2)}) copy-start(f32[32,32,256]{2,1,0:T(8,128)} %n_ref.5) | copy-start | bytes 3145732
  45.9 6.4 %collective-permute-start.11 = (f32[2,136,128]{2,1,0:T(8,128)S(1)}, f32[2,136,128]{2,1,0:T(8,128)S(1)}, u32[]{:S(2)}, u32[]{:S(2)}) collective-permute-start(f32[2,136,128]{2,1,0:T(8,128)S(1)} %get-tuple-element.54), channel_id=1, source_target_pairs={{0,2},{1,3},{2,4},{3,5},{4,6},{5,7},{6,0},{7,1},{8,10},{9,11},{10,... | collective-permute-start | bytes 417800 | tf_op jit(solution)/shard_map/ppermute | solution.py:307
  46.8 5.5 %collective-permute-start.12 = (f32[2,136,128]{2,1,0:T(8,128)S(1)}, f32[2,136,128]{2,1,0:T(8,128)S(1)}, u32[]{:S(2)}, u32[]{:S(2)}) collective-permute-start(f32[2,136,128]{2,1,0:T(8,128)S(1)} %get-tuple-element.55), channel_id=1, source_target_pairs={{0,6},{1,7},{2,0},{3,1},{4,2},{5,3},{6,4},{7,5},{8,14},{9,15},{10,... | collective-permute-start | bytes 417800 | tf_op jit(solution)/shard_map/ppermute | solution.py:307
  48.6 7.2 %collective-permute-start.13 = (f32[2,136,128]{2,1,0:T(8,128)S(1)}, f32[2,136,128]{2,1,0:T(8,128)S(1)}, u32[]{:S(2)}, u32[]{:S(2)}) collective-permute-start(f32[2,136,128]{2,1,0:T(8,128)S(1)} %get-tuple-element.56), channel_id=1, source_target_pairs={{0,4},{1,5},{2,6},{3,7},{4,0},{5,1},{6,2},{7,3},{8,12},{9,13},{10,... | collective-permute-start | bytes 417800 | tf_op jit(solution)/shard_map/ppermute | solution.py:307
  55.8 2.7 %collective-permute-start.14 = (f32[4,136,128]{2,1,0:T(8,128)S(1)}, f32[4,136,128]{2,1,0:T(8,128)S(1)}, u32[]{:S(2)}, u32[]{:S(2)}) collective-permute-start(f32[4,136,128]{2,1,0:T(8,128)S(1)} %pad_maximum_fusion), channel_id=1, source_target_pairs={{0,1},{1,0},{2,3},{3,2},{4,5},{5,4},{6,7},{7,6},{8,9},{9,8},{10,11... | collective-permute-start | bytes 835592 | tf_op jit(solution)/shard_map/ppermute | solution.py:307
